TPU v7x, 32 devices: a whole 2x2x4 slice. The times are simulated.
32 devices in a mesh: view: 16 (over z, y, core), chord: 2 (over x).
Axes of the slice: x: 2, y: 2, z: 4, core: 2. Of those that a mesh axis runs over, the one named last changes fastest.
Arguments:
- proj: bfloat16 [192, 256, 128], P('view', 'chord'), may hold values from -6 to 6
- tiles: bfloat16 [96, 256, 1024], P('view'), may hold values from -0.0390625 to 0.0390625
- owner: int32 [2, 128], replicated, may hold values from 0 to 127, as said below
- lengths: int32 [2, 128], replicated, may hold values from 1 to 1024, as said below
Outputs:
- recon: float32 [2, 128, 1024], P('chord', 'view')
Inputs may be any that keep to these rules, and one draw needn't show every extreme that they name: `owner`: each row is an ordering of the 128 chords of one group. In each group, the lengths of the chords at owner positions k * 8 to k * 8 + 7 sum to at most 4608, exactly 4608 for some k; the largest entry of each row is 1024.
All inputs are finite; a program needn't handle non-finite values.
Results may differ from a plain program's by a relative error of at most 0.0003.
Values sent between devices are 32-bit elements; how exact they have to be, the bound alone decides.
No kernel may reach another device: no remote copies, remote signals or barrier semaphores. Data moves between devices by JAX's collectives and lax.ppermute only.
A program may use at most 64 MiB of HBM per device.

v0:
```python
from functools import partial
import math

import jax
import jax.numpy as jnp
from jax import lax
from jax.sharding import PartitionSpec as P

NB = 4


def kernel_table(rows, start, cols):
    row_pos = start + jnp.arange(rows, dtype=jnp.float32)[:, None]
    col_pos = jnp.arange(cols, dtype=jnp.float32)[None, :]
    return 1.0 / (row_pos - col_pos + 0.5)


def weigh(length, count, start):
    position = start + jnp.arange(count, dtype=jnp.float32)[None, :] + 0.5
    inside = position < length
    return (inside, jnp.sqrt(jnp.where(inside, position * (length - position), 1.0)))


def invert_block(sums, length, table, start):
    length = length.astype(jnp.float32)[:, None]
    col_in, col_w = weigh(length, sums.shape[1], 0.0)
    row_in, row_w = weigh(length, table.shape[0], start)
    scaled = jnp.where(col_in, col_w * sums, 0.0)
    image = jnp.dot(
        scaled, table.T, precision=lax.Precision.HIGHEST, preferred_element_type=jnp.float32
    )
    return jnp.where(row_in, image / (math.pi * row_w), 0.0)


def bucket_invert(capacity, table, chord_row, chord_length):
    result = invert_block(
        chord_row[None, :capacity], chord_length[None], table[:capacity, :capacity], 0.0
    )[0]
    return jnp.pad(result, (0, chord_row.shape[0] - capacity))


def per_device(proj, tiles, owner, lengths):
    view_count, group_rows, footprint = proj.shape
    block_count = tiles.shape[0]
    samples = tiles.shape[2]
    block_views = view_count // block_count
    group = lax.axis_index("chord")
    view_place = lax.axis_index("view")
    view_devices = lax.axis_size("view")
    owned = group_rows // view_devices
    my_order = lax.dynamic_index_in_dim(owner, group, 0, keepdims=False)
    data_blocks = proj.reshape(block_count, block_views, group_rows, footprint)
    tile_stack = tiles.reshape(block_count, block_views, footprint, samples)
    ordered_len = jnp.take_along_axis(lengths, owner, axis=1)
    owned_len = lax.dynamic_slice_in_dim(ordered_len, view_place * owned, owned, axis=1)
    my_len = lax.dynamic_index_in_dim(owned_len, group, 0, keepdims=False)
    picked = jnp.take(data_blocks, my_order, axis=2)

    def step(total, inputs):
        views_now, tile = inputs
        return (
            total + jnp.einsum("vkd,vds->ks", views_now, tile, preferred_element_type=jnp.float32),
            None,
        )

    start_total = jnp.zeros((my_order.shape[0], samples), jnp.float32)
    total, _ = lax.scan(step, start_total, (picked, tile_stack))
    chord_totals = lax.psum_scatter(total, "view", scatter_dimension=0, tiled=True)
    table = kernel_table(samples, 0.0, samples)
    branches = [partial(bucket_invert, samples * (level + 1) // NB, table) for level in range(NB)]

    def one_chord(inputs):
        chord_row, chord_length = inputs
        level = jnp.minimum((chord_length - 1) * NB // samples, NB - 1)
        return lax.switch(level, branches, chord_row, chord_length)

    recon = lax.map(one_chord, (chord_totals, my_len))
    return recon[None]


def solution(mesh):
    placed = (P("view", "chord", None), P("view", None, None), P(), P())
    return jax.shard_map(
        per_device, mesh=mesh, in_specs=placed, out_specs=P("chord", "view", None), check_vma=False
    )
```

profile of v0, /device:TPU:4, one launch (start us, length us, event | category | flops | bytes accessed | tf_op | source)
XLA Modules:
  0.0 159.2 jit_solution(9059013054166725831)
XLA Ops:
  6.5 0.7 fusion.31
  7.2 0.7 compare_and_fusion
  7.9 1.4 copy.6
  9.3 1.7 %gather_fusion = bf16[128,6,2,128]{3,2,1,0:T(2,128)(2,1)S(1)} fusion(bf16[6,2,128,128]{3,1,2,0:T(2,128)(2,1)S(1)} %copy.6, s32[1024]{0:T(1024)S(1)} %pad_clamp_fusion), kind=kCustom, calls=%fused_computation | custom fusion | bytes 786944 | tf_op jit(solution)/shard_map/jit(_take)/gather | solution.py:57
  11.0 0.4 fusion.29
  11.5 8.5 %while.27 = (s32[]{:T(128)}, f32[128,1024]{1,0:T(8,128)S(1)}, bf16[6,2,128,128]{3,1,0,2:T(2,128)(2,1)S(1)}, bf16[6,2,128,1024]{3,2,1,0:T(8,128)(2,1)}, s32[]{:T(128)}, /*index=5*/s32[]{:T(128)}) while((s32[]{:T(128)}, f32[128,1024]{1,0:T(8,128)S(1)}, bf16[6,2,128,128]{3,1,0,2:T(2,128)(2,1)S(1)}, ...), condition=%wide.region_1.2_spmd.clone, body=%wide.region_0.1_spmd.clone.sunk | while | flops 67371008 | bytes 1770067 | solution.py:67
  11.6 1.3 fusion.41
  13.0 1.3 fusion.41
  14.4 1.3 fusion.41
  15.8 1.3 fusion.41
  17.3 1.3 fusion.41
  18.7 1.3 fusion.41
  20.1 0.8 copy-done.1
  20.9 2.4 %gather_fusion.1 = s32[256]{0:T(256)S(1)} fusion(s32[2,128]{1,0:T(2,128)S(1)} %copy-done, s32[256]{0:T(256)S(1)} %fusion.30), kind=kCustom, calls=%fused_computation.1 | custom fusion | bytes 4096 | tf_op jit(solution)/shard_map/jit(take_along_axis)/gather | solution.py:54
  23.4 54.5 %reduce-scatter.2.cloned.1.call-done = f32[8,1024]{1,0:T(8,128)} async-done(((f32[128,1024]{1,0:T(8,128)}), f32[8,1024]{1,0:T(8,128)}) %reduce-scatter.2.cloned.1.call-update) | async-done | bytes 32784 | tf_op jit(solution)/shard_map/reduce_scatter | solution.py:68
  77.9 74.5 %while.26 = (s32[]{:T(128)}, f32[8,1024]{1,0:T(8,128)}, s32[8]{0:T(128)S(1)}, f32[8,1024]{1,0:T(8,128)}, s32[]{:T(128)}, /*index=5*/s32[]{:T(128)}, s32[]{:T(128...) while((s32[]{:T(128)}, f32[8,1024]{1,0:T(8,128)}, s32[8]{0:T(128)S(1)}, ...), condition=%wide.region_8.9_spmd.clone.clone, body=%wide.region_3.8_spmd.clone.clone.sunk | while | flops 15744022 | bytes 8429955 | solution.py:77
  77.9 0.6 dynamic_slice.69
  79.1 2.6 %add_divide_fusion.2 = f32[1024,1024]{1,0:T(8,128)} fusion(), kind=kLoop, calls=%fused_computation.51.clone.1 | loop fusion | flops 3145728 | bytes 4194304 | tf_op jit(solution)/shard_map/div | solution.py:15
  81.7 3.5 %conditional.4 = (f32[1,1024]{1,0:T(1,128)S(1)}) conditional(s32[]{:T(128)} %clamp.21, (s32[]{:T(128)}, f32[8,1024]{1,0:T(8,128)}, s32[]{:T(128)}, f32[1024,1024]{1,0:T(8,128)}) %tuple.84, (s32[]{:T(128)}, f32[8,1024]{1,0:T(8,128)}, s32[]{:T(128)}, f32[1024,1024]{1,0:T(8,128)}) %tuple.84, (s32[]{:T(128)}, ...), branch_computations={%region_4.4_spmd, %region_5.5_spmd, %region_6.6_spmd, %region_7.7_... | conditional | flops 12598273 | bytes 4227100 | solution.py:75
  82.2 0.7 constant_dynamic-slice_fusion.1
  83.0 2.2 %fusion.8 = f32[1,512]{1,0:T(1,128)S(1)} fusion(f32[512,1]{0,1:T(1,128)S(1)} %bitcast.68, f32[1024,1024]{1,0:T(8,128)} %get-tuple-element.202), kind=kOutput, calls=%fused_computation.14 | convolution fusion | flops 3145728 | bytes 1052672 | tf_op jit(solution)/shard_map/while/body/eval_jaxpr/cond/branch_1_fun/dot_general | solution.py:29
  85.2 1.4 dynamic_update_slice.11
  86.6 0.6 dynamic_slice.69
  87.8 2.6 %add_divide_fusion.2 = f32[1024,1024]{1,0:T(8,128)} fusion(), kind=kLoop, calls=%fused_computation.51.clone.1 | loop fusion | flops 3145728 | bytes 4194304 | tf_op jit(solution)/shard_map/div | solution.py:15
  90.4 3.5 %conditional.4 = (f32[1,1024]{1,0:T(1,128)S(1)}) conditional(s32[]{:T(128)} %clamp.21, (s32[]{:T(128)}, f32[8,1024]{1,0:T(8,128)}, s32[]{:T(128)}, f32[1024,1024]{1,0:T(8,128)}) %tuple.84, (s32[]{:T(128)}, f32[8,1024]{1,0:T(8,128)}, s32[]{:T(128)}, f32[1024,1024]{1,0:T(8,128)}) %tuple.84, (s32[]{:T(128)}, ...), branch_computations={%region_4.4_spmd, %region_5.5_spmd, %region_6.6_spmd, %region_7.7_... | conditional | flops 12598273 | bytes 4227100 | solution.py:75
  91.0 0.7 constant_dynamic-slice_fusion.1
  91.7 2.2 %fusion.8 = f32[1,512]{1,0:T(1,128)S(1)} fusion(f32[512,1]{0,1:T(1,128)S(1)} %bitcast.68, f32[1024,1024]{1,0:T(8,128)} %get-tuple-element.202), kind=kOutput, calls=%fused_computation.14 | convolution fusion | flops 3145728 | bytes 1052672 | tf_op jit(solution)/shard_map/while/body/eval_jaxpr/cond/branch_1_fun/dot_general | solution.py:29
  93.9 1.4 dynamic_update_slice.11
  95.3 0.6 dynamic_slice.69
  96.5 2.6 %add_divide_fusion.2 = f32[1024,1024]{1,0:T(8,128)} fusion(), kind=kLoop, calls=%fused_computation.51.clone.1 | loop fusion | flops 3145728 | bytes 4194304 | tf_op jit(solution)/shard_map/div | solution.py:15
  99.1 3.5 %conditional.4 = (f32[1,1024]{1,0:T(1,128)S(1)}) conditional(s32[]{:T(128)} %clamp.21, (s32[]{:T(128)}, f32[8,1024]{1,0:T(8,128)}, s32[]{:T(128)}, f32[1024,1024]{1,0:T(8,128)}) %tuple.84, (s32[]{:T(128)}, f32[8,1024]{1,0:T(8,128)}, s32[]{:T(128)}, f32[1024,1024]{1,0:T(8,128)}) %tuple.84, (s32[]{:T(128)}, ...), branch_computations={%region_4.4_spmd, %region_5.5_spmd, %region_6.6_spmd, %region_7.7_... | conditional | flops 12598273 | bytes 4227100 | solution.py:75
  99.7 0.7 constant_dynamic-slice_fusion.1
  100.4 2.2 %fusion.8 = f32[1,512]{1,0:T(1,128)S(1)} fusion(f32[512,1]{0,1:T(1,128)S(1)} %bitcast.68, f32[1024,1024]{1,0:T(8,128)} %get-tuple-element.202), kind=kOutput, calls=%fused_computation.14 | convolution fusion | flops 3145728 | bytes 1052672 | tf_op jit(solution)/shard_map/while/body/eval_jaxpr/cond/branch_1_fun/dot_general | solution.py:29
  102.7 1.4 dynamic_update_slice.11
  104.1 0.6 dynamic_slice.69
  105.2 2.6 %add_divide_fusion.2 = f32[1024,1024]{1,0:T(8,128)} fusion(), kind=kLoop, calls=%fused_computation.51.clone.1 | loop fusion | flops 3145728 | bytes 4194304 | tf_op jit(solution)/shard_map/div | solution.py:15
  107.8 2.6 %conditional.4 = (f32[1,1024]{1,0:T(1,128)S(1)}) conditional(s32[]{:T(128)} %clamp.21, (s32[]{:T(128)}, f32[8,1024]{1,0:T(8,128)}, s32[]{:T(128)}, f32[1024,1024]{1,0:T(8,128)}) %tuple.84, (s32[]{:T(128)}, f32[8,1024]{1,0:T(8,128)}, s32[]{:T(128)}, f32[1024,1024]{1,0:T(8,128)}) %tuple.84, (s32[]{:T(128)}, ...), branch_computations={%region_4.4_spmd, %region_5.5_spmd, %region_6.6_spmd, %region_7.7_... | conditional | flops 12598273 | bytes 4227100 | solution.py:75
  108.4 0.7 constant_dynamic-slice_fusion
  109.1 1.2 fusion.2
  110.4 1.4 dynamic_update_slice.11
  111.8 0.6 dynamic_slice.69
  113.0 2.6 %add_divide_fusion.2 = f32[1024,1024]{1,0:T(8,128)} fusion(), kind=kLoop, calls=%fused_computation.51.clone.1 | loop fusion | flops 3145728 | bytes 4194304 | tf_op jit(solution)/shard_map/div | solution.py:15
  115.6 2.6 %conditional.4 = (f32[1,1024]{1,0:T(1,128)S(1)}) conditional(s32[]{:T(128)} %clamp.21, (s32[]{:T(128)}, f32[8,1024]{1,0:T(8,128)}, s32[]{:T(128)}, f32[1024,1024]{1,0:T(8,128)}) %tuple.84, (s32[]{:T(128)}, f32[8,1024]{1,0:T(8,128)}, s32[]{:T(128)}, f32[1024,1024]{1,0:T(8,128)}) %tuple.84, (s32[]{:T(128)}, ...), branch_computations={%region_4.4_spmd, %region_5.5_spmd, %region_6.6_spmd, %region_7.7_... | conditional | flops 12598273 | bytes 4227100 | solution.py:75
  116.2 0.7 constant_dynamic-slice_fusion
  116.9 1.2 fusion.2
  118.2 1.4 dynamic_update_slice.11
  119.6 0.6 dynamic_slice.69
  120.8 2.6 %add_divide_fusion.2 = f32[1024,1024]{1,0:T(8,128)} fusion(), kind=kLoop, calls=%fused_computation.51.clone.1 | loop fusion | flops 3145728 | bytes 4194304 | tf_op jit(solution)/shard_map/div | solution.py:15
  123.4 7.0 %conditional.4 = (f32[1,1024]{1,0:T(1,128)S(1)}) conditional(s32[]{:T(128)} %clamp.21, (s32[]{:T(128)}, f32[8,1024]{1,0:T(8,128)}, s32[]{:T(128)}, f32[1024,1024]{1,0:T(8,128)}) %tuple.84, (s32[]{:T(128)}, f32[8,1024]{1,0:T(8,128)}, s32[]{:T(128)}, f32[1024,1024]{1,0:T(8,128)}) %tuple.84, (s32[]{:T(128)}, ...), branch_computations={%region_4.4_spmd, %region_5.5_spmd, %region_6.6_spmd, %region_7.7_... | conditional | flops 12598273 | bytes 4227100 | solution.py:75
  124.0 0.8 constant_dynamic-slice_fusion.2
  124.8 5.6 %fusion.32 = f32[1,1024]{1,0:T(1,128)S(1)} fusion(f32[1024,1]{0,1:T(1,128)S(1)} %bitcast.65, f32[1024,1024]{1,0:T(8,128)} %get-tuple-element.210), kind=kOutput, calls=%fused_computation.65 | convolution fusion | flops 12582912 | bytes 4202496 | tf_op jit(solution)/shard_map/while/body/eval_jaxpr/cond/branch_3_fun/dot_general | solution.py:29
  130.4 1.4 dynamic_update_slice.11
  131.8 0.6 dynamic_slice.69
  133.0 2.6 %add_divide_fusion.2 = f32[1024,1024]{1,0:T(8,128)} fusion(), kind=kLoop, calls=%fused_computation.51.clone.1 | loop fusion | flops 3145728 | bytes 4194304 | tf_op jit(solution)/shard_map/div | solution.py:15
  135.6 5.1 %conditional.4 = (f32[1,1024]{1,0:T(1,128)S(1)}) conditional(s32[]{:T(128)} %clamp.21, (s32[]{:T(128)}, f32[8,1024]{1,0:T(8,128)}, s32[]{:T(128)}, f32[1024,1024]{1,0:T(8,128)}) %tuple.84, (s32[]{:T(128)}, f32[8,1024]{1,0:T(8,128)}, s32[]{:T(128)}, f32[1024,1024]{1,0:T(8,128)}) %tuple.84, (s32[]{:T(128)}, ...), branch_computations={%region_4.4_spmd, %region_5.5_spmd, %region_6.6_spmd, %region_7.7_... | conditional | flops 12598273 | bytes 4227100 | solution.py:75
  136.2 0.8 dynamic-slice_reduce_fusion
  137.0 3.7 %fusion.23 = f32[768]{0:T(1024)S(1)} fusion(f32[768,1]{0,1:T(1,128)S(1)} %reshape.169, f32[1024,1024]{1,0:T(8,128)} %get-tuple-element.206), kind=kOutput, calls=%fused_computation.42 | convolution fusion | flops 7077888 | bytes 2365440 | tf_op jit(solution)/shard_map/while/body/eval_jaxpr/cond/branch_2_fun/dot_general | solution.py:29
  140.7 1.4 dynamic_update_slice.11
  142.1 0.6 dynamic_slice.69
  143.3 2.6 %add_divide_fusion.2 = f32[1024,1024]{1,0:T(8,128)} fusion(), kind=kLoop, calls=%fused_computation.51.clone.1 | loop fusion | flops 3145728 | bytes 4194304 | tf_op jit(solution)/shard_map/div | solution.py:15
  145.9 5.1 %conditional.4 = (f32[1,1024]{1,0:T(1,128)S(1)}) conditional(s32[]{:T(128)} %clamp.21, (s32[]{:T(128)}, f32[8,1024]{1,0:T(8,128)}, s32[]{:T(128)}, f32[1024,1024]{1,0:T(8,128)}) %tuple.84, (s32[]{:T(128)}, f32[8,1024]{1,0:T(8,128)}, s32[]{:T(128)}, f32[1024,1024]{1,0:T(8,128)}) %tuple.84, (s32[]{:T(128)}, ...), branch_computations={%region_4.4_spmd, %region_5.5_spmd, %region_6.6_spmd, %region_7.7_... | conditional | flops 12598273 | bytes 4227100 | solution.py:75
  146.4 0.8 dynamic-slice_reduce_fusion
  147.2 3.7 %fusion.23 = f32[768]{0:T(1024)S(1)} fusion(f32[768,1]{0,1:T(1,128)S(1)} %reshape.169, f32[1024,1024]{1,0:T(8,128)} %get-tuple-element.206), kind=kOutput, calls=%fused_computation.42 | convolution fusion | flops 7077888 | bytes 2365440 | tf_op jit(solution)/shard_map/while/body/eval_jaxpr/cond/branch_2_fun/dot_general | solution.py:29
  151.0 1.4 dynamic_update_slice.11
  (44 shorter events, 0.9 us)
Async XLA Ops:
  6.5 14.4 %copy-start = (s32[2,128]{1,0:T(2,128)S(1)}, s32[2,128]{1,0:T(2,128)}, u32[]{:S(2)}) copy-start(s32[2,128]{1,0:T(2,128)} %param.15) | copy-start | bytes 3076
  6.5 71.4 %reduce-scatter.2.cloned.1.call-start = ((), (), s32[]{:S(2)}) async-start(), calls=%async_computation.1 | async-start | bytes 557056 | tf_op jit(solution)/shard_map/reduce_scatter | solution.py:68
  11.5 9.4 %copy-start.2 = (s32[2,128]{1,0:T(2,128)S(1)}, s32[2,128]{1,0:T(2,128)}, u32[]{:S(2)}) copy-start(s32[2,128]{1,0:T(2,128)} %param.14) | copy-start | bytes 3076
  20.0 0.8 copy-start.1
Sparse Core Ops, SparseCore 0:
  21.0 56.8 reduce-scatter.1
where the time goes:
time: 160 us; the launch traced here: 159 us
  waiting for transfers between devices  54.5 us (34%)
  matrix products  29.9 us (19%)
  local copies, waits for them, and re-layouts  28.4 us (18%)
  other arithmetic  23.2 us (14%)
  between operations  13.5 us (8%)
  loops' own time  9.69 us (6%)
    reduce_scatter x1, waiting for transfers between devices, per_device(): lax.psum_scatter(total, 'view', scatter_dimension=0, tiled=True)  54.5 us
    dot_general x8, matrix products, invert_block(): jnp.dot(scaled, table.T, precision=lax.Precision.HIGHEST, preferred_eleme...  21.9 us
    div x8, other arithmetic, kernel_table(): return 1.0 / (row_pos - col_pos + 0.5)  20.9 us
    dynamic_update_slice x8, local copies, waits for them, and re-layouts, per_device(): recon = lax.map(one_chord, (chord_totals, my_len))  11.2 us
    dot_general x6, matrix products, step(): jnp.einsum('vkd,vds->ks', views_now, tile, preferred_element_type=jnp.flo...  8.01 us
    dynamic_slice x9, local copies, waits for them, and re-layouts, per_device(): recon = lax.map(one_chord, (chord_totals, my_len))  5.37 us
    slice x7, local copies, waits for them, and re-layouts, bucket_invert(): chord_row[None, :capacity]  5.12 us
    another operation x1, loops' own time, per_device(): recon = lax.map(one_chord, (chord_totals, my_len))  4.8 us
  transfers between devices with their start and end apart: 1, of which 1 were waited for; matrix products, arithmetic and copies ran while one was open for 2% of the time, Pallas kernels for 0%

commit v1 on v0

v1 whole, which is shorter than its diff:
```python
import math

import jax
import jax.numpy as jnp
from jax import lax
from jax.experimental import pallas as pl
from jax.experimental.pallas import tpu as pltpu
from jax.sharding import PartitionSpec as P

LANE = 128
OWNED_SAMPLES = 4608
COLS = 256


def exchange_masks(devices):
    steps = devices.bit_length() - 1
    return [1] + [(1 << step) | 1 for step in range(1, steps)]


def slot_mask(slot, devices):
    masks = exchange_masks(devices)
    steps = len(masks)
    distance = 0
    for step, mask in enumerate(masks):
        bit = (slot >> (steps - 1 - step)) & 1
        distance = distance ^ (bit * mask)
    return distance


def slot_of(distance, devices):
    steps = devices.bit_length() - 1
    slot = jnp.zeros_like(distance)
    parity = jnp.zeros_like(distance)
    for step in range(1, steps):
        bit = (distance >> step) & 1
        slot = slot | (bit << (steps - 1 - step))
        parity = parity ^ bit
    first = (distance & 1) ^ parity
    return slot | (first << (steps - 1))


def rows_per_owner(owned):
    rows = (OWNED_SAMPLES + owned * (LANE - 1)) // LANE
    return -(-rows // 4) * 4


def block_counts(owner_ref, lengths_ref, group, place, owned):
    total = jnp.int32(0)
    lengths = []
    for index in range(owned):
        length = lengths_ref[group, owner_ref[group, place * owned + index]]
        lengths.append(length)
        blocks = (length + (LANE - 1)) >> 7
        total = total + lax.shift_right_logical(jnp.int32(0x11111111), 32 - 4 * blocks)
    return total, lengths


def block_offsets(counts, blocks):
    offset = jnp.int32(0)
    offsets = []
    for block in range(blocks):
        offsets.append(offset)
        offset = offset + (lax.shift_right_logical(counts, 4 * block) & 15)
    return offsets


def project_kernel(
    devices, owner_hbm, lengths_hbm, proj_hbm, tiles_hbm, keep_ref, send_ref,
    owner_s, lengths_s, owner_v, lengths_v, proj_buf, tile_buf, left_buf, sums_buf,
    small_sem, proj_sem, tile_sem,
):
    views, rows, footprint = proj_buf.shape
    chunks = tile_buf.shape[0]
    samples = chunks * COLS
    owned = rows // devices
    group = lax.axis_index("chord")
    me = lax.axis_index("view")
    small = [
        pltpu.make_async_copy(source, kept, small_sem.at[index])
        for index, (source, kept) in enumerate(
            [(owner_hbm, owner_v), (lengths_hbm, lengths_v), (owner_hbm, owner_s), (lengths_hbm, lengths_s)]
        )
    ]
    for copy in small:
        copy.start()
    proj_copy = pltpu.make_async_copy(proj_hbm, proj_buf, proj_sem)
    proj_copy.start()
    tile_copies = []
    for chunk in range(chunks):
        copy = pltpu.make_async_copy(
            tiles_hbm.at[:, :, pl.ds(chunk * COLS, COLS)], tile_buf.at[chunk], tile_sem.at[chunk]
        )
        copy.start()
        tile_copies.append(copy)

    keep_ref[...] = jnp.zeros_like(keep_ref)
    send_ref[...] = jnp.zeros_like(send_ref)
    for copy in small:
        copy.wait()
    down = lax.broadcasted_iota(jnp.int32, (rows, rows), 0)
    across = lax.broadcasted_iota(jnp.int32, (rows, rows), 1)
    diagonal = down == across

    def turned(row):
        spread = jnp.broadcast_to(row.astype(jnp.float32), (rows, rows))
        return jnp.sum(jnp.where(diagonal, spread, 0.0), axis=1, keepdims=True)

    order = turned(owner_v[pl.ds(group, 1), :])
    hit = order == across.astype(jnp.float32)
    position = jnp.sum(jnp.where(hit, down.astype(jnp.float32), 0.0), axis=0, keepdims=True)
    position = position.astype(jnp.int32)
    place = position // owned
    slot = slot_of(place ^ me, devices)
    key = (slot * (samples + 1) + (samples - lengths_v[pl.ds(group, 1), :])) * owned + (
        position - place * owned
    )
    key = key.astype(jnp.float32)
    target = jnp.sum(jnp.where(turned(key) < key, 1.0, 0.0), axis=0, keepdims=True)
    pick = jnp.where(down.astype(jnp.float32) == target, 1.0, 0.0).astype(jnp.bfloat16)

    proj_copy.wait()
    for view in range(views):
        moved = jnp.dot(pick, proj_buf[view], preferred_element_type=jnp.float32)
        left_buf[:, view * footprint : (view + 1) * footprint] = moved.astype(jnp.bfloat16)
    for chunk in range(chunks):
        tile_copies[chunk].wait()
        right = tile_buf[chunk].reshape(views * footprint, COLS)
        sums_buf[:, chunk * COLS : (chunk + 1) * COLS] = jnp.dot(
            left_buf[...], right, preferred_element_type=jnp.float32
        )

    packed = rows_per_owner(owned)
    half = devices // 2
    blocks = samples // LANE

    def pack(slot_index, base, out_ref):
        at = me ^ slot_mask(slot_index, devices)
        counts, _ = block_counts(owner_s, lengths_s, group, at, owned)
        for block, offset in enumerate(block_offsets(counts, blocks)):
            out_ref[pl.ds(base + offset, owned), :] = sums_buf[
                pl.ds(slot_index * owned, owned), block * LANE : (block + 1) * LANE
            ]

    if devices <= 16:
        for index in range(half):
            pack(half + index, index * packed, send_ref)
        for index in range(half):
            pack(index, index * packed, keep_ref)
    else:

        @pl.loop(0, half)
        def _(index):
            pack(half + index, index * packed, send_ref)

        @pl.loop(0, half)
        def _(index):
            pack(index, index * packed, keep_ref)


def project(proj, tiles, owner, lengths, devices):
    views, rows, footprint = proj.shape
    blocks, depth, samples = tiles.shape
    owned = rows // devices
    chunks = samples // COLS
    half_rows = devices // 2 * rows_per_owner(owned) + owned
    shape = pltpu.VMEM((half_rows, LANE), jnp.float32)
    inputs = [pltpu.with_memory_space_constraint(x, pltpu.HBM) for x in (owner, lengths, proj, tiles)]

    def kernel(*refs):
        project_kernel(devices, *refs)

    vmem = pl.BlockSpec(memory_space=pltpu.VMEM)
    hbm = pl.BlockSpec(memory_space=pltpu.HBM)
    return pl.pallas_call(
        kernel,
        out_shape=(shape, shape),
        in_specs=[hbm] * 4,
        out_specs=(vmem, vmem),
        scratch_shapes=[
            pltpu.SMEM(owner.shape, jnp.int32),
            pltpu.SMEM(lengths.shape, jnp.int32),
            pltpu.VMEM(owner.shape, jnp.int32),
            pltpu.VMEM(lengths.shape, jnp.int32),
            pltpu.VMEM(proj.shape, jnp.bfloat16),
            pltpu.VMEM((chunks, blocks, depth, COLS), jnp.bfloat16),
            pltpu.VMEM((rows, views * footprint), jnp.bfloat16),
            pltpu.VMEM((rows, samples), jnp.float32),
            pltpu.SemaphoreType.DMA((4,)),
            pltpu.SemaphoreType.DMA,
            pltpu.SemaphoreType.DMA((chunks,)),
        ],
        compiler_params=pltpu.CompilerParams(vmem_limit_bytes=40 << 20),
        cost_estimate=pl.CostEstimate(
            flops=2 * rows * views * footprint * samples,
            bytes_accessed=2 * (proj.size + tiles.size),
            transcendentals=0,
        ),
        name="project",
    )(*inputs)


def invert_kernel(devices, owner_s, lengths_s, mine_ref, other_ref, coarse_ref, fine_ref, out_ref, sum_buf, row_buf):
    owned, samples = row_buf.shape
    group = lax.axis_index("chord")
    me = lax.axis_index("view")
    packed = mine_ref.shape[0]
    sum_buf[0:packed, :] = mine_ref[...] + other_ref[...]
    counts, lengths = block_counts(owner_s, lengths_s, group, me, owned)
    offsets = block_offsets(counts, samples // LANE)
    for index in range(owned):
        rank = jnp.int32(0)
        for other in range(owned):
            if other < index:
                rank = rank + (lengths[other] >= lengths[index]).astype(jnp.int32)
            elif other > index:
                rank = rank + (lengths[other] > lengths[index]).astype(jnp.int32)
        for block, offset in enumerate(offsets):
            row_buf[index : index + 1, block * LANE : (block + 1) * LANE] = sum_buf[
                pl.ds(offset + rank, 1), :
            ]
    sub = lax.broadcasted_iota(jnp.int32, (owned, COLS), 0)
    length = jnp.zeros((owned, COLS), jnp.float32)
    for index in range(owned):
        length = jnp.where(sub == index, lengths[index].astype(jnp.float32), length)
    bins = samples // COLS
    lane = lax.broadcasted_iota(jnp.int32, (owned, COLS), 1).astype(jnp.float32) + 0.5
    weights, left = [], []
    for part in range(bins):
        spot = lane + float(part * COLS)
        inside = spot < length
        weight = jnp.sqrt(jnp.where(inside, spot * (length - spot), 1.0))
        weights.append((inside, weight))
        scaled = jnp.where(inside, weight * row_buf[:, part * COLS : (part + 1) * COLS], 0.0)
        coarse = scaled.astype(jnp.bfloat16)
        fine = (scaled - coarse.astype(jnp.float32)).astype(jnp.bfloat16)
        left.append(jnp.concatenate([coarse, fine], axis=0))
    image = [None] * bins
    for shift in range(1 - bins, bins):
        first, last = max(0, -shift), min(bins, bins - shift)
        stack = jnp.concatenate(left[first:last], axis=0)
        product = jnp.dot(
            stack, coarse_ref[shift + bins - 1], preferred_element_type=jnp.float32
        ) + jnp.dot(stack, fine_ref[shift + bins - 1], preferred_element_type=jnp.float32)
        for place, part in enumerate(range(first, last)):
            base = place * 2 * owned
            term = product[base : base + owned] + product[base + owned : base + 2 * owned]
            to = part + shift
            image[to] = term if image[to] is None else image[to] + term
    for part in range(bins):
        inside, weight = weights[part]
        out_ref[0, :, part * COLS : (part + 1) * COLS] = jnp.where(
            inside, image[part] / (math.pi * weight), 0.0
        )


def invert(mine, other, table, owner, lengths, devices, owned, samples):
    def kernel(*refs):
        invert_kernel(devices, *refs)

    smem = pl.BlockSpec(memory_space=pltpu.SMEM)
    vmem = pl.BlockSpec(memory_space=pltpu.VMEM)
    return pl.pallas_call(
        kernel,
        out_shape=jax.ShapeDtypeStruct((1, owned, samples), jnp.float32),
        in_specs=[smem, smem, vmem, vmem, vmem, vmem],
        out_specs=vmem,
        scratch_shapes=[
            pltpu.VMEM((mine.shape[0] + 3 * owned, LANE), jnp.float32),
            pltpu.VMEM((owned, samples), jnp.float32),
        ],
        compiler_params=pltpu.CompilerParams(vmem_limit_bytes=32 << 20),
        name="invert",
    )(owner, lengths, mine, other, *table)


def hilbert_table(bins):
    shape = (2 * bins - 1, COLS, COLS)
    shift = (lax.broadcasted_iota(jnp.int32, shape, 0) - (bins - 1)) * COLS
    gap = shift + lax.broadcasted_iota(jnp.int32, shape, 2) - lax.broadcasted_iota(jnp.int32, shape, 1)
    exact = 1.0 / (gap.astype(jnp.float32) + 0.5)
    coarse = lax.reduce_precision(exact, 8, 7)
    return coarse.astype(jnp.bfloat16), (exact - coarse).astype(jnp.bfloat16)


def per_device(proj, tiles, owner, lengths):
    devices = lax.axis_size("view")
    rows = proj.shape[1]
    samples = tiles.shape[2]
    owned = rows // devices
    packed = rows_per_owner(owned)
    keep, send = project(proj, tiles, owner, lengths, devices)
    table = hilbert_table(samples // COLS)
    held = devices // 2
    for mask in exchange_masks(devices)[:-1]:
        pairs = [(device, device ^ mask) for device in range(devices)]
        total = keep + lax.ppermute(send, "view", pairs)
        held //= 2
        keep, send = total[: held * packed], total[held * packed : 2 * held * packed]
    mask = exchange_masks(devices)[-1]
    pairs = [(device, device ^ mask) for device in range(devices)]
    other = lax.ppermute(send, "view", pairs)
    return invert(keep, other, table, owner, lengths, devices, owned, samples)


def solution(mesh):
    placed = (P("view", "chord", None), P("view", None, None), P(), P())
    return jax.shard_map(
        per_device, mesh=mesh, in_specs=placed, out_specs=P("chord", "view", None), check_vma=False
    )
```

time: 160 us -> 20.4 us (0.13)
  the two profiles are of different devices: /device:TPU:4 before, /device:TPU:0 now
where the time goes in v1:
time: 20.4 us; the launch traced here: 20.3 us
  starting transfers between devices  8.22 us (40%)
  waiting for transfers between devices  6.42 us (31%)
  Pallas kernels  4.95 us (24%)
  other arithmetic  0.61 us (3%)
    ppermute x3, waiting for transfers between devices, per_device(): total = keep + lax.ppermute(send, 'view', pairs)  5.47 us
    ppermute x3, starting transfers between devices, per_device(): total = keep + lax.ppermute(send, 'view', pairs)  5.24 us
    pallas_call x1, Pallas kernels, project(): pl.pallas_call(kernel, out_shape=(shape, shape), in_specs=[hbm] * 4, out_...  3.26 us
    ppermute x1, starting transfers between devices, per_device(): other = lax.ppermute(send, 'view', pairs)  2.98 us
    pallas_call x1, Pallas kernels, invert(): pl.pallas_call(kernel, out_shape=jax.ShapeDtypeStruct((1, owned, samples)...  1.69 us
    ppermute x1, waiting for transfers between devices, per_device(): other = lax.ppermute(send, 'view', pairs)  0.95 us
    convert_element_type x1, other arithmetic, hilbert_table(): return (coarse.astype(jnp.bfloat16), (exact - coarse).astype(jnp.bfloat16))  0.56 us
  transfers between devices with their start and end apart: 4, of which 4 were waited for; matrix products, arithmetic and copies ran while one was open for 3% of the time, Pallas kernels for 0%

profile of v1, /device:TPU:0, one launch (start us, length us, event | category | flops | bytes accessed | tf_op | source)
XLA Modules:
  0.0 20.3 jit_solution(7179310672546811325)
XLA Ops:
  0.0 3.3 %project.1 = (f32[360,128]{1,0:T(8,128)S(1)}, f32[360,128]{1,0:T(8,128)S(1)}) custom-call(s32[2,128]{1,0:T(2,128)} %refs_0_.3, s32[2,128]{1,0:T(2,128)} %refs_1_.3, bf16[12,128,128]{2,1,0:T(8,128)(2,1)} %refs_2_.1, bf16[6,256,1024]{2,1,0:T(8,128)(2,1)} %refs_3_.1), custom_call_target="tpu_custom_call" | custom-call | flops 402653184 | bytes 3538944 | tf_op jit(solution)/shard_map/project/pallas_call | solution.py:174
  3.3 0.0 copy-start
  3.3 0.0 copy-start.1
  3.3 0.5 %collective-permute-start = (f32[360,128]{1,0:T(8,128)S(1)}, f32[360,128]{1,0:T(8,128)S(1)}, u32[]{:S(2)}, u32[]{:S(2)}) collective-permute-start(f32[360,128]{1,0:T(8,128)S(1)} %get-tuple-element.8), channel_id=1, source_target_pairs={{0,2},{2,0},{4,6},{6,4},{8,10},{10,8},{12,14},{14,12},{16,18},{18,... | collective-permute-start | bytes 552968 | tf_op jit(solution)/shard_map/ppermute | solution.py:296
  3.8 1.1 %collective-permute-done = f32[360,128]{1,0:T(8,128)S(1)} collective-permute-done((f32[360,128]{1,0:T(8,128)S(1)}, f32[360,128]{1,0:T(8,128)S(1)}, u32[]{:S(2)}, u32[]{:S(2)}) %collective-permute-start) | collective-permute-done | bytes 184352 | tf_op jit(solution)/shard_map/ppermute | solution.py:296
  4.9 2.7 %collective-permute-start.1 = (f32[176,128]{1,0:T(8,128)S(1)}, f32[176,128]{1,0:T(8,128)S(1)}, u32[]{:S(2)}, u32[]{:S(2)}) collective-permute-start(f32[176,128]{1,0:T(8,128)S(1)} %slice.25), channel_id=1, source_target_pairs={{0,6},{2,4},{4,2},{6,0},{8,14},{10,12},{12,10},{14,8},{16,22},{18,... | collective-permute-start | bytes 270344 | tf_op jit(solution)/shard_map/ppermute | solution.py:296
  7.6 2.7 %collective-permute-done.1 = f32[176,128]{1,0:T(8,128)S(1)} collective-permute-done((f32[176,128]{1,0:T(8,128)S(1)}, f32[176,128]{1,0:T(8,128)S(1)}, u32[]{:S(2)}, u32[]{:S(2)}) %collective-permute-start.1) | collective-permute-done | bytes 90144 | tf_op jit(solution)/shard_map/ppermute | solution.py:296
  10.3 2.0 %collective-permute-start.2 = (f32[88,128]{1,0:T(8,128)S(1)}, f32[88,128]{1,0:T(8,128)S(1)}, u32[]{:S(2)}, u32[]{:S(2)}) collective-permute-start(f32[88,128]{1,0:T(8,128)S(1)} %slice.27), channel_id=1, source_target_pairs={{0,10},{2,8},{4,14},{6,12},{8,2},{10,0},{12,6},{14,4},{16,26},{18,... | collective-permute-start | bytes 135176 | tf_op jit(solution)/shard_map/ppermute | solution.py:296
  12.4 1.7 %collective-permute-done.2 = f32[88,128]{1,0:T(8,128)S(1)} collective-permute-done((f32[88,128]{1,0:T(8,128)S(1)}, f32[88,128]{1,0:T(8,128)S(1)}, u32[]{:S(2)}, u32[]{:S(2)}) %collective-permute-start.2) | collective-permute-done | bytes 45088 | tf_op jit(solution)/shard_map/ppermute | solution.py:296
  14.1 3.0 %collective-permute-start.3 = (f32[44,128]{1,0:T(8,128)S(1)}, f32[44,128]{1,0:T(8,128)S(1)}, u32[]{:S(2)}, u32[]{:S(2)}) collective-permute-start(f32[44,128]{1,0:T(8,128)S(1)} %get-tuple-element.9), channel_id=1, source_target_pairs={{0,18},{2,16},{4,22},{6,20},{8,26},{10,24},{12,30},{14,28},{16,2},... | collective-permute-start | bytes 67592 | tf_op jit(solution)/shard_map/ppermute | solution.py:301
  17.1 0.6 %fusion = (bf16[7,256,256]{2,1,0:T(8,128)(2,1)S(1)}, bf16[7,256,256]{2,1,0:T(8,128)(2,1)S(1)}) fusion(s32[7]{0:T(128)S(1)} %add_multiply_fusion), kind=kLoop, calls=%fused_computation.2 | loop fusion | flops 4128768 | bytes 1835036 | tf_op jit(solution)/shard_map/convert_element_type | solution.py:282
  17.7 0.9 %collective-permute-done.3.refs_3_ = f32[44,128]{1,0:T(8,128)S(1)} collective-permute-done((f32[44,128]{1,0:T(8,128)S(1)}, f32[44,128]{1,0:T(8,128)S(1)}, u32[]{:S(2)}, u32[]{:S(2)}) %collective-permute-start.3) | collective-permute-done | bytes 22560 | tf_op jit(solution)/shard_map/ppermute | solution.py:301
  18.6 0.0 copy-done
  18.6 0.0 copy-done.1
  18.6 1.7 %invert.1 = f32[1,8,1024]{2,1,0:T(8,128)} custom-call(s32[2,128]{1,0:T(2,128)S(1)} %copy-done, s32[2,128]{1,0:T(2,128)S(1)} %copy-done.1, f32[44,128]{1,0:T(8,128)S(1)} %get-tuple-element.10.refs_2_, f32[44,128]{1,0:T(8,128)S(1)} %collective-permute-done.3.refs_3_, bf16[7,256,256]{2,1,0:T(8,128)(2,1)S(1)} %get-tuple-element.12.refs_4_, ...), custom_call_target="tpu_custom_call" | custom-call | tf_op jit(solution)/shard_map/invert/pallas_call | solution.py:262
  (7 shorter events, 0.1 us)
Async XLA Ops:
  3.3 15.3 %copy-start = (s32[2,128]{1,0:T(2,128)S(1)}, s32[2,128]{1,0:T(2,128)}, u32[]{:S(2)}) copy-start(s32[2,128]{1,0:T(2,128)} %refs_0_.3) | copy-start | bytes 3076
  3.3 15.3 %copy-start.1 = (s32[2,128]{1,0:T(2,128)S(1)}, s32[2,128]{1,0:T(2,128)}, u32[]{:S(2)}) copy-start(s32[2,128]{1,0:T(2,128)} %refs_1_.3) | copy-start | bytes 3076
  3.3 1.6 %collective-permute-start = (f32[360,128]{1,0:T(8,128)S(1)}, f32[360,128]{1,0:T(8,128)S(1)}, u32[]{:S(2)}, u32[]{:S(2)}) collective-permute-start(f32[360,128]{1,0:T(8,128)S(1)} %get-tuple-element.8), channel_id=1, source_target_pairs={{0,2},{2,0},{4,6},{6,4},{8,10},{10,8},{12,14},{14,12},{16,18},{18,... | collective-permute-start | bytes 552968 | tf_op jit(solution)/shard_map/ppermute | solution.py:296
  4.9 5.4 %collective-permute-start.1 = (f32[176,128]{1,0:T(8,128)S(1)}, f32[176,128]{1,0:T(8,128)S(1)}, u32[]{:S(2)}, u32[]{:S(2)}) collective-permute-start(f32[176,128]{1,0:T(8,128)S(1)} %slice.25), channel_id=1, source_target_pairs={{0,6},{2,4},{4,2},{6,0},{8,14},{10,12},{12,10},{14,8},{16,22},{18,... | collective-permute-start | bytes 270344 | tf_op jit(solution)/shard_map/ppermute | solution.py:296
  10.3 3.8 %collective-permute-start.2 = (f32[88,128]{1,0:T(8,128)S(1)}, f32[88,128]{1,0:T(8,128)S(1)}, u32[]{:S(2)}, u32[]{:S(2)}) collective-permute-start(f32[88,128]{1,0:T(8,128)S(1)} %slice.27), channel_id=1, source_target_pairs={{0,10},{2,8},{4,14},{6,12},{8,2},{10,0},{12,6},{14,4},{16,26},{18,... | collective-permute-start | bytes 135176 | tf_op jit(solution)/shard_map/ppermute | solution.py:296
  14.1 4.5 %collective-permute-start.3 = (f32[44,128]{1,0:T(8,128)S(1)}, f32[44,128]{1,0:T(8,128)S(1)}, u32[]{:S(2)}, u32[]{:S(2)}) collective-permute-start(f32[44,128]{1,0:T(8,128)S(1)} %get-tuple-element.9), channel_id=1, source_target_pairs={{0,18},{2,16},{4,22},{6,20},{8,26},{10,24},{12,30},{14,28},{16,2},... | collective-permute-start | bytes 67592 | tf_op jit(solution)/shard_map/ppermute | solution.py:301

commit v2 on v1

--- a/solution.py
+++ b/solution.py
@@ -44,41 +44,48 @@
     return -(-rows // 4) * 4
 
 
-def block_counts(owner_ref, lengths_ref, group, place, owned):
+def block_counts(lengths):
     total = jnp.int32(0)
-    lengths = []
-    for index in range(owned):
-        length = lengths_ref[group, owner_ref[group, place * owned + index]]
-        lengths.append(length)
+    for length in lengths:
         blocks = (length + (LANE - 1)) >> 7
         total = total + lax.shift_right_logical(jnp.int32(0x11111111), 32 - 4 * blocks)
-    return total, lengths
-
-
-def block_offsets(counts, blocks):
-    offset = jnp.int32(0)
-    offsets = []
-    for block in range(blocks):
-        offsets.append(offset)
-        offset = offset + (lax.shift_right_logical(counts, 4 * block) & 15)
-    return offsets
+    return total
+
+
+def offset_words(counts):
+    even = counts & 0x0F0F0F0F
+    odd = lax.shift_right_logical(counts, 4) & 0x0F0F0F0F
+    before = ((even + odd) * 0x01010101) << 8
+    return before, before + even
+
+
+def row_of(words, block):
+    return lax.shift_right_logical(words[block % 2], 8 * (block // 2)) & 255
+
+
+def owned_lengths(owner_ref, lengths_ref, group, place, owned):
+    return [lengths_ref[group, owner_ref[group, place * owned + index]] for index in range(owned)]
+
+
+def column_chunks(samples):
+    return [(0, samples // 2), (samples // 2, samples // 2)]
 
 
 def project_kernel(
     devices, owner_hbm, lengths_hbm, proj_hbm, tiles_hbm, keep_ref, send_ref,
-    owner_s, lengths_s, owner_v, lengths_v, proj_buf, tile_buf, left_buf, sums_buf,
-    small_sem, proj_sem, tile_sem,
+    owner_v, lengths_v, offset_v, offset_s, proj_buf, tile_buf, left_buf, sums_buf,
+    small_sem, offset_sem, proj_sem, tile_sem,
 ):
     views, rows, footprint = proj_buf.shape
-    chunks = tile_buf.shape[0]
-    samples = chunks * COLS
+    samples = tile_buf.shape[2]
+    chunks = column_chunks(samples)
     owned = rows // devices
     group = lax.axis_index("chord")
     me = lax.axis_index("view")
     small = [
         pltpu.make_async_copy(source, kept, small_sem.at[index])
         for index, (source, kept) in enumerate(
-            [(owner_hbm, owner_v), (lengths_hbm, lengths_v), (owner_hbm, owner_s), (lengths_hbm, lengths_s)]
+            [(owner_hbm, owner_v), (lengths_hbm, lengths_v)]
         )
     ]
     for copy in small:
@@ -86,9 +93,10 @@
     proj_copy = pltpu.make_async_copy(proj_hbm, proj_buf, proj_sem)
     proj_copy.start()
     tile_copies = []
-    for chunk in range(chunks):
+    for index, (start, width) in enumerate(chunks):
+        columns = pl.ds(start, width)
         copy = pltpu.make_async_copy(
-            tiles_hbm.at[:, :, pl.ds(chunk * COLS, COLS)], tile_buf.at[chunk], tile_sem.at[chunk]
+            tiles_hbm.at[:, :, columns], tile_buf.at[:, :, columns], tile_sem.at[index]
         )
         copy.start()
         tile_copies.append(copy)
@@ -105,63 +113,90 @@
         spread = jnp.broadcast_to(row.astype(jnp.float32), (rows, rows))
         return jnp.sum(jnp.where(diagonal, spread, 0.0), axis=1, keepdims=True)
 
+    lengths = lengths_v[pl.ds(group, 1), :]
     order = turned(owner_v[pl.ds(group, 1), :])
     hit = order == across.astype(jnp.float32)
     position = jnp.sum(jnp.where(hit, down.astype(jnp.float32), 0.0), axis=0, keepdims=True)
     position = position.astype(jnp.int32)
     place = position // owned
     slot = slot_of(place ^ me, devices)
-    key = (slot * (samples + 1) + (samples - lengths_v[pl.ds(group, 1), :])) * owned + (
+
+    reach = turned((lengths + (LANE - 1)) // LANE)
+    block_index = lax.broadcasted_iota(jnp.int32, (rows, LANE), 1).astype(jnp.float32)
+    before = jnp.where(block_index < samples // LANE, jnp.minimum(block_index, reach), 0.0)
+    member = lax.broadcasted_iota(jnp.int32, (devices, rows), 0) == slot
+    offset_v[...] = jnp.dot(
+        jnp.where(member, 1.0, 0.0).astype(jnp.bfloat16),
+        before.astype(jnp.bfloat16),
+        preferred_element_type=jnp.float32,
+    ).astype(jnp.int32)
+    offset_copy = pltpu.make_async_copy(offset_v, offset_s, offset_sem)
+    offset_copy.start()
+
+    key = (slot * (samples + 1) + (samples - lengths)) * owned + (
         position - place * owned
     )
     key = key.astype(jnp.float32)
     target = jnp.sum(jnp.where(turned(key) < key, 1.0, 0.0), axis=0, keepdims=True)
     pick = jnp.where(down.astype(jnp.float32) == target, 1.0, 0.0).astype(jnp.bfloat16)
 
+    def each_slot(body):
+        if devices <= 16:
+            for index in range(devices):
+                body(index)
+        else:
+            pl.loop(0, devices)(body)
+
     proj_copy.wait()
     for view in range(views):
         moved = jnp.dot(pick, proj_buf[view], preferred_element_type=jnp.float32)
         left_buf[:, view * footprint : (view + 1) * footprint] = moved.astype(jnp.bfloat16)
-    for chunk in range(chunks):
-        tile_copies[chunk].wait()
-        right = tile_buf[chunk].reshape(views * footprint, COLS)
-        sums_buf[:, chunk * COLS : (chunk + 1) * COLS] = jnp.dot(
+
+    packed = rows_per_owner(owned)
+    half = devices // 2
+
+    def put(slot_index, offset, value):
+        def to(out_ref, base):
+            out_ref[pl.ds(base + offset, owned), :] = value
+
+        if isinstance(slot_index, int):
+            if slot_index < half:
+                to(keep_ref, slot_index * packed)
+            else:
+                to(send_ref, (slot_index - half) * packed)
+        else:
+            pl.when(slot_index < half)(lambda: to(keep_ref, slot_index * packed))
+            pl.when(slot_index >= half)(lambda: to(send_ref, (slot_index - half) * packed))
+
+    def pack(first, last):
+        def one(slot_index):
+            for block in range(first, last):
+                value = sums_buf[pl.ds(slot_index * owned, owned), block * LANE : (block + 1) * LANE]
+                put(slot_index, offset_s[slot_index, block] if block else 0, value)
+
+        each_slot(one)
+
+    ready = 1
+    for index, (start, width) in enumerate(chunks):
+        tile_copies[index].wait()
+        right = tile_buf[:, :, start : start + width].reshape(views * footprint, width)
+        sums_buf[:, start : start + width] = jnp.dot(
             left_buf[...], right, preferred_element_type=jnp.float32
         )
-
-    packed = rows_per_owner(owned)
-    half = devices // 2
-    blocks = samples // LANE
-
-    def pack(slot_index, base, out_ref):
-        at = me ^ slot_mask(slot_index, devices)
-        counts, _ = block_counts(owner_s, lengths_s, group, at, owned)
-        for block, offset in enumerate(block_offsets(counts, blocks)):
-            out_ref[pl.ds(base + offset, owned), :] = sums_buf[
-                pl.ds(slot_index * owned, owned), block * LANE : (block + 1) * LANE
-            ]
-
-    if devices <= 16:
-        for index in range(half):
-            pack(half + index, index * packed, send_ref)
-        for index in range(half):
-            pack(index, index * packed, keep_ref)
-    else:
-
-        @pl.loop(0, half)
-        def _(index):
-            pack(half + index, index * packed, send_ref)
-
-        @pl.loop(0, half)
-        def _(index):
-            pack(index, index * packed, keep_ref)
+        if index == 1:
+            offset_copy.wait()
+        if index:
+            pack(ready, start // LANE)
+            ready = max(ready, start // LANE)
+    pack(ready, samples // LANE)
+    pack(0, 1)
 
 
 def project(proj, tiles, owner, lengths, devices):
     views, rows, footprint = proj.shape
     blocks, depth, samples = tiles.shape
     owned = rows // devices
-    chunks = samples // COLS
+    chunks = column_chunks(samples)
     half_rows = devices // 2 * rows_per_owner(owned) + owned
     shape = pltpu.VMEM((half_rows, LANE), jnp.float32)
     inputs = [pltpu.with_memory_space_constraint(x, pltpu.HBM) for x in (owner, lengths, proj, tiles)]
@@ -177,17 +212,18 @@
         in_specs=[hbm] * 4,
         out_specs=(vmem, vmem),
         scratch_shapes=[
-            pltpu.SMEM(owner.shape, jnp.int32),
-            pltpu.SMEM(lengths.shape, jnp.int32),
             pltpu.VMEM(owner.shape, jnp.int32),
             pltpu.VMEM(lengths.shape, jnp.int32),
+            pltpu.VMEM((devices, LANE), jnp.int32),
+            pltpu.SMEM((devices, LANE), jnp.int32),
             pltpu.VMEM(proj.shape, jnp.bfloat16),
-            pltpu.VMEM((chunks, blocks, depth, COLS), jnp.bfloat16),
+            pltpu.VMEM(tiles.shape, jnp.bfloat16),
             pltpu.VMEM((rows, views * footprint), jnp.bfloat16),
             pltpu.VMEM((rows, samples), jnp.float32),
-            pltpu.SemaphoreType.DMA((4,)),
+            pltpu.SemaphoreType.DMA((2,)),
             pltpu.SemaphoreType.DMA,
-            pltpu.SemaphoreType.DMA((chunks,)),
+            pltpu.SemaphoreType.DMA,
+            pltpu.SemaphoreType.DMA((len(chunks),)),
         ],
         compiler_params=pltpu.CompilerParams(vmem_limit_bytes=40 << 20),
         cost_estimate=pl.CostEstimate(
@@ -205,8 +241,9 @@
     me = lax.axis_index("view")
     packed = mine_ref.shape[0]
     sum_buf[0:packed, :] = mine_ref[...] + other_ref[...]
-    counts, lengths = block_counts(owner_s, lengths_s, group, me, owned)
-    offsets = block_offsets(counts, samples // LANE)
+    lengths = owned_lengths(owner_s, lengths_s, group, me, owned)
+    words = offset_words(block_counts(lengths))
+    offsets = [row_of(words, block) for block in range(samples // LANE)]
     for index in range(owned):
         rank = jnp.int32(0)
         for other in range(owned):

time: 20.4 us -> 19.7 us (0.966)
  Pallas kernels: 4.95 us -> 4.24 us
    pallas_call x1, Pallas kernels: 3.26 us -> 2.56 us  [project(): pl.pallas_call(kernel, out_shape=(shape, shape), in_specs=[hbm] * 4, out_...]
where the time goes in v2:
time: 19.7 us; the launch traced here: 19.6 us
  starting transfers between devices  8.23 us (42%)
  waiting for transfers between devices  6.42 us (33%)
  Pallas kernels  4.24 us (22%)
  other arithmetic  0.61 us (3%)
    ppermute x3, waiting for transfers between devices, per_device(): total = keep + lax.ppermute(send, 'view', pairs)  5.47 us
    ppermute x3, starting transfers between devices, per_device(): total = keep + lax.ppermute(send, 'view', pairs)  5.25 us
    ppermute x1, starting transfers between devices, per_device(): other = lax.ppermute(send, 'view', pairs)  2.98 us
    pallas_call x1, Pallas kernels, project(): pl.pallas_call(kernel, out_shape=(shape, shape), in_specs=[hbm] * 4, out_...  2.56 us
    pallas_call x1, Pallas kernels, invert(): pl.pallas_call(kernel, out_shape=jax.ShapeDtypeStruct((1, owned, samples)...  1.68 us
    ppermute x1, waiting for transfers between devices, per_device(): other = lax.ppermute(send, 'view', pairs)  0.95 us
    convert_element_type x1, other arithmetic, hilbert_table(): return (coarse.astype(jnp.bfloat16), (exact - coarse).astype(jnp.bfloat16))  0.56 us
  transfers between devices with their start and end apart: 4, of which 4 were waited for; matrix products, arithmetic and copies ran while one was open for 3% of the time, Pallas kernels for 0%

profile of v2, /device:TPU:0, one launch (start us, length us, event | category | flops | bytes accessed | tf_op | source)
XLA Modules:
  0.0 19.6 jit_solution(8067027604192691444)
XLA Ops:
  0.0 2.6 %project.1 = (f32[360,128]{1,0:T(8,128)S(1)}, f32[360,128]{1,0:T(8,128)S(1)}) custom-call(s32[2,128]{1,0:T(2,128)} %refs_0_.3, s32[2,128]{1,0:T(2,128)} %refs_1_.3, bf16[12,128,128]{2,1,0:T(8,128)(2,1)} %refs_2_.1, bf16[6,256,1024]{2,1,0:T(8,128)(2,1)} %refs_3_.1), custom_call_target="tpu_custom_call" | custom-call | flops 402653184 | bytes 3538944 | tf_op jit(solution)/shard_map/project/pallas_call | solution.py:209
  2.6 0.0 copy-start
  2.6 0.0 copy-start.1
  2.6 0.5 %collective-permute-start = (f32[360,128]{1,0:T(8,128)S(1)}, f32[360,128]{1,0:T(8,128)S(1)}, u32[]{:S(2)}, u32[]{:S(2)}) collective-permute-start(f32[360,128]{1,0:T(8,128)S(1)} %get-tuple-element.8), channel_id=1, source_target_pairs={{0,2},{2,0},{4,6},{6,4},{8,10},{10,8},{12,14},{14,12},{16,18},{18,... | collective-permute-start | bytes 552968 | tf_op jit(solution)/shard_map/ppermute | solution.py:333
  3.1 1.1 %collective-permute-done = f32[360,128]{1,0:T(8,128)S(1)} collective-permute-done((f32[360,128]{1,0:T(8,128)S(1)}, f32[360,128]{1,0:T(8,128)S(1)}, u32[]{:S(2)}, u32[]{:S(2)}) %collective-permute-start) | collective-permute-done | bytes 184352 | tf_op jit(solution)/shard_map/ppermute | solution.py:333
  4.2 2.7 %collective-permute-start.1 = (f32[176,128]{1,0:T(8,128)S(1)}, f32[176,128]{1,0:T(8,128)S(1)}, u32[]{:S(2)}, u32[]{:S(2)}) collective-permute-start(f32[176,128]{1,0:T(8,128)S(1)} %slice.25), channel_id=1, source_target_pairs={{0,6},{2,4},{4,2},{6,0},{8,14},{10,12},{12,10},{14,8},{16,22},{18,... | collective-permute-start | bytes 270344 | tf_op jit(solution)/shard_map/ppermute | solution.py:333
  6.9 2.7 %collective-permute-done.1 = f32[176,128]{1,0:T(8,128)S(1)} collective-permute-done((f32[176,128]{1,0:T(8,128)S(1)}, f32[176,128]{1,0:T(8,128)S(1)}, u32[]{:S(2)}, u32[]{:S(2)}) %collective-permute-start.1) | collective-permute-done | bytes 90144 | tf_op jit(solution)/shard_map/ppermute | solution.py:333
  9.6 2.0 %collective-permute-start.2 = (f32[88,128]{1,0:T(8,128)S(1)}, f32[88,128]{1,0:T(8,128)S(1)}, u32[]{:S(2)}, u32[]{:S(2)}) collective-permute-start(f32[88,128]{1,0:T(8,128)S(1)} %slice.27), channel_id=1, source_target_pairs={{0,10},{2,8},{4,14},{6,12},{8,2},{10,0},{12,6},{14,4},{16,26},{18,... | collective-permute-start | bytes 135176 | tf_op jit(solution)/shard_map/ppermute | solution.py:333
  11.7 1.7 %collective-permute-done.2 = f32[88,128]{1,0:T(8,128)S(1)} collective-permute-done((f32[88,128]{1,0:T(8,128)S(1)}, f32[88,128]{1,0:T(8,128)S(1)}, u32[]{:S(2)}, u32[]{:S(2)}) %collective-permute-start.2) | collective-permute-done | bytes 45088 | tf_op jit(solution)/shard_map/ppermute | solution.py:333
  13.4 3.0 %collective-permute-start.3 = (f32[44,128]{1,0:T(8,128)S(1)}, f32[44,128]{1,0:T(8,128)S(1)}, u32[]{:S(2)}, u32[]{:S(2)}) collective-permute-start(f32[44,128]{1,0:T(8,128)S(1)} %get-tuple-element.9), channel_id=1, source_target_pairs={{0,18},{2,16},{4,22},{6,20},{8,26},{10,24},{12,30},{14,28},{16,2},... | collective-permute-start | bytes 67592 | tf_op jit(solution)/shard_map/ppermute | solution.py:338
  16.4 0.6 %fusion = (bf16[7,256,256]{2,1,0:T(8,128)(2,1)S(1)}, bf16[7,256,256]{2,1,0:T(8,128)(2,1)S(1)}) fusion(s32[7]{0:T(128)S(1)} %add_multiply_fusion), kind=kLoop, calls=%fused_computation.2 | loop fusion | flops 4128768 | bytes 1835036 | tf_op jit(solution)/shard_map/convert_element_type | solution.py:319
  17.0 0.9 %collective-permute-done.3.refs_3_ = f32[44,128]{1,0:T(8,128)S(1)} collective-permute-done((f32[44,128]{1,0:T(8,128)S(1)}, f32[44,128]{1,0:T(8,128)S(1)}, u32[]{:S(2)}, u32[]{:S(2)}) %collective-permute-start.3) | collective-permute-done | bytes 22560 | tf_op jit(solution)/shard_map/ppermute | solution.py:338
  17.9 0.0 copy-done
  17.9 0.0 copy-done.1
  17.9 1.7 %invert.1 = f32[1,8,1024]{2,1,0:T(8,128)} custom-call(s32[2,128]{1,0:T(2,128)S(1)} %copy-done, s32[2,128]{1,0:T(2,128)S(1)} %copy-done.1, f32[44,128]{1,0:T(8,128)S(1)} %get-tuple-element.10.refs_2_, f32[44,128]{1,0:T(8,128)S(1)} %collective-permute-done.3.refs_3_, bf16[7,256,256]{2,1,0:T(8,128)(2,1)S(1)} %get-tuple-element.12.refs_4_, ...), custom_call_target="tpu_custom_call" | custom-call | tf_op jit(solution)/shard_map/invert/pallas_call | solution.py:299
  (7 shorter events, 0.1 us)
Async XLA Ops:
  2.6 15.3 %copy-start = (s32[2,128]{1,0:T(2,128)S(1)}, s32[2,128]{1,0:T(2,128)}, u32[]{:S(2)}) copy-start(s32[2,128]{1,0:T(2,128)} %refs_0_.3) | copy-start | bytes 3076
  2.6 15.3 %copy-start.1 = (s32[2,128]{1,0:T(2,128)S(1)}, s32[2,128]{1,0:T(2,128)}, u32[]{:S(2)}) copy-start(s32[2,128]{1,0:T(2,128)} %refs_1_.3) | copy-start | bytes 3076
  2.6 1.6 %collective-permute-start = (f32[360,128]{1,0:T(8,128)S(1)}, f32[360,128]{1,0:T(8,128)S(1)}, u32[]{:S(2)}, u32[]{:S(2)}) collective-permute-start(f32[360,128]{1,0:T(8,128)S(1)} %get-tuple-element.8), channel_id=1, source_target_pairs={{0,2},{2,0},{4,6},{6,4},{8,10},{10,8},{12,14},{14,12},{16,18},{18,... | collective-permute-start | bytes 552968 | tf_op jit(solution)/shard_map/ppermute | solution.py:333
  4.2 5.4 %collective-permute-start.1 = (f32[176,128]{1,0:T(8,128)S(1)}, f32[176,128]{1,0:T(8,128)S(1)}, u32[]{:S(2)}, u32[]{:S(2)}) collective-permute-start(f32[176,128]{1,0:T(8,128)S(1)} %slice.25), channel_id=1, source_target_pairs={{0,6},{2,4},{4,2},{6,0},{8,14},{10,12},{12,10},{14,8},{16,22},{18,... | collective-permute-start | bytes 270344 | tf_op jit(solution)/shard_map/ppermute | solution.py:333
  9.6 3.8 %collective-permute-start.2 = (f32[88,128]{1,0:T(8,128)S(1)}, f32[88,128]{1,0:T(8,128)S(1)}, u32[]{:S(2)}, u32[]{:S(2)}) collective-permute-start(f32[88,128]{1,0:T(8,128)S(1)} %slice.27), channel_id=1, source_target_pairs={{0,10},{2,8},{4,14},{6,12},{8,2},{10,0},{12,6},{14,4},{16,26},{18,... | collective-permute-start | bytes 135176 | tf_op jit(solution)/shard_map/ppermute | solution.py:333
  13.4 4.5 %collective-permute-start.3 = (f32[44,128]{1,0:T(8,128)S(1)}, f32[44,128]{1,0:T(8,128)S(1)}, u32[]{:S(2)}, u32[]{:S(2)}) collective-permute-start(f32[44,128]{1,0:T(8,128)S(1)} %get-tuple-element.9), channel_id=1, source_target_pairs={{0,18},{2,16},{4,22},{6,20},{8,26},{10,24},{12,30},{14,28},{16,2},... | collective-permute-start | bytes 67592 | tf_op jit(solution)/shard_map/ppermute | solution.py:338

commit v3 on v2

--- a/solution.py
+++ b/solution.py
@@ -42,29 +42,6 @@
 def rows_per_owner(owned):
     rows = (OWNED_SAMPLES + owned * (LANE - 1)) // LANE
     return -(-rows // 4) * 4
-
-
-def block_counts(lengths):
-    total = jnp.int32(0)
-    for length in lengths:
-        blocks = (length + (LANE - 1)) >> 7
-        total = total + lax.shift_right_logical(jnp.int32(0x11111111), 32 - 4 * blocks)
-    return total
-
-
-def offset_words(counts):
-    even = counts & 0x0F0F0F0F
-    odd = lax.shift_right_logical(counts, 4) & 0x0F0F0F0F
-    before = ((even + odd) * 0x01010101) << 8
-    return before, before + even
-
-
-def row_of(words, block):
-    return lax.shift_right_logical(words[block % 2], 8 * (block // 2)) & 255
-
-
-def owned_lengths(owner_ref, lengths_ref, group, place, owned):
-    return [lengths_ref[group, owner_ref[group, place * owned + index]] for index in range(owned)]
 
 
 def column_chunks(samples):
@@ -235,42 +212,112 @@
     )(*inputs)
 
 
-def invert_kernel(devices, owner_s, lengths_s, mine_ref, other_ref, coarse_ref, fine_ref, out_ref, sum_buf, row_buf):
-    owned, samples = row_buf.shape
+def prepare_kernel(
+    devices, owner_hbm, lengths_hbm, unpick_ref, inner_ref, outer_ref, coarse_ref, fine_ref,
+    owner_s, lengths_s, sem,
+):
+    owned, samples = inner_ref.shape
+    blocks = samples // LANE
+    packed = unpick_ref.shape[1]
+    distances = coarse_ref.shape[0]
     group = lax.axis_index("chord")
     me = lax.axis_index("view")
-    packed = mine_ref.shape[0]
-    sum_buf[0:packed, :] = mine_ref[...] + other_ref[...]
-    lengths = owned_lengths(owner_s, lengths_s, group, me, owned)
-    words = offset_words(block_counts(lengths))
-    offsets = [row_of(words, block) for block in range(samples // LANE)]
+    copies = [
+        pltpu.make_async_copy(owner_hbm, owner_s, sem.at[0]),
+        pltpu.make_async_copy(lengths_hbm, lengths_s, sem.at[1]),
+    ]
+    for copy in copies:
+        copy.start()
+    across = lax.broadcasted_iota(jnp.int32, (COLS, COLS), 1)
+    gap = (across - lax.broadcasted_iota(jnp.int32, (COLS, COLS), 0)).astype(jnp.float32) + 0.5
+    for index in range(distances):
+        exact = 1.0 / (gap + float((index - distances // 2) * COLS))
+        coarse = exact.astype(jnp.bfloat16)
+        coarse_ref[index] = coarse
+        fine_ref[index] = (exact - coarse.astype(jnp.float32)).astype(jnp.bfloat16)
+    for copy in copies:
+        copy.wait()
+    lengths = [lengths_s[group, owner_s[group, me * owned + index]] for index in range(owned)]
+
+    sub = lax.broadcasted_iota(jnp.int32, (owned, LANE), 0)
+    lane = lax.broadcasted_iota(jnp.int32, (owned, LANE), 1)
+    length = jnp.zeros((owned, LANE), jnp.int32)
     for index in range(owned):
-        rank = jnp.int32(0)
-        for other in range(owned):
-            if other < index:
-                rank = rank + (lengths[other] >= lengths[index]).astype(jnp.int32)
-            elif other > index:
-                rank = rank + (lengths[other] > lengths[index]).astype(jnp.int32)
-        for block, offset in enumerate(offsets):
-            row_buf[index : index + 1, block * LANE : (block + 1) * LANE] = sum_buf[
-                pl.ds(offset + rank, 1), :
-            ]
-    sub = lax.broadcasted_iota(jnp.int32, (owned, COLS), 0)
-    length = jnp.zeros((owned, COLS), jnp.float32)
+        length = jnp.where(sub == index, lengths[index], length)
+    rank = jnp.zeros((owned, LANE), jnp.int32)
     for index in range(owned):
-        length = jnp.where(sub == index, lengths[index].astype(jnp.float32), length)
+        ahead = (lengths[index] > length) | ((lengths[index] == length) & (index < sub))
+        rank = rank + jnp.where(ahead, 1, 0)
+    reach = (length + (LANE - 1)) >> 7
+    rows = []
+    for block in range(blocks):
+        offset = jnp.int32(0)
+        for index in range(owned):
+            offset = offset + jnp.minimum((lengths[index] + (LANE - 1)) >> 7, block)
+        hit = (lane == rank + offset) & (reach > block)
+        rows.append(jnp.where(hit, 1.0, 0.0))
+    unpick_ref[...] = jnp.concatenate(rows, axis=0)[:, :packed].astype(jnp.bfloat16)
+
+    long = length.astype(jnp.float32)
+    for block in range(blocks):
+        spot = (lane + block * LANE).astype(jnp.float32) + 0.5
+        inside = spot < long
+        weight = jnp.sqrt(jnp.where(inside, spot * (long - spot), 1.0))
+        columns = slice(block * LANE, (block + 1) * LANE)
+        inner_ref[:, columns] = jnp.where(inside, weight, 0.0)
+        outer_ref[:, columns] = jnp.where(inside, 1.0 / (math.pi * weight), 0.0)
+
+
+def prepare(owner, lengths, devices, owned, samples, packed):
+    distances = 2 * (samples // COLS) - 1
+    inputs = [pltpu.with_memory_space_constraint(x, pltpu.HBM) for x in (owner, lengths)]
+    vmem = pl.BlockSpec(memory_space=pltpu.VMEM)
+
+    def kernel(*refs):
+        prepare_kernel(devices, *refs)
+
+    return pl.pallas_call(
+        kernel,
+        out_shape=(
+            pltpu.VMEM((owned * samples // LANE, packed), jnp.bfloat16),
+            pltpu.VMEM((owned, samples), jnp.float32),
+            pltpu.VMEM((owned, samples), jnp.float32),
+            pltpu.VMEM((distances, COLS, COLS), jnp.bfloat16),
+            pltpu.VMEM((distances, COLS, COLS), jnp.bfloat16),
+        ),
+        in_specs=[pl.BlockSpec(memory_space=pltpu.HBM)] * 2,
+        out_specs=(vmem,) * 5,
+        scratch_shapes=[
+            pltpu.SMEM(owner.shape, jnp.int32),
+            pltpu.SMEM(lengths.shape, jnp.int32),
+            pltpu.SemaphoreType.DMA((2,)),
+        ],
+        compiler_params=pltpu.CompilerParams(vmem_limit_bytes=32 << 20),
+        cost_estimate=pl.CostEstimate(flops=1 << 22, bytes_accessed=1 << 21, transcendentals=1 << 19),
+        name="prepare",
+    )(*inputs)
+
+
+def invert_kernel(mine_ref, other_ref, unpick_ref, inner_ref, outer_ref, coarse_ref, fine_ref, out_ref):
+    owned, samples = inner_ref.shape
     bins = samples // COLS
-    lane = lax.broadcasted_iota(jnp.int32, (owned, COLS), 1).astype(jnp.float32) + 0.5
-    weights, left = [], []
+    per_bin = COLS // LANE
+
+    def halves(value):
+        coarse = value.astype(jnp.bfloat16)
+        return coarse, (value - coarse.astype(jnp.float32)).astype(jnp.bfloat16)
+
+    both = jnp.concatenate(halves(mine_ref[...] + other_ref[...]), axis=1)
+    spread = jnp.dot(unpick_ref[...], both, preferred_element_type=jnp.float32)
+    spread = spread[:, :LANE] + spread[:, LANE:]
+    left = []
     for part in range(bins):
-        spot = lane + float(part * COLS)
-        inside = spot < length
-        weight = jnp.sqrt(jnp.where(inside, spot * (length - spot), 1.0))
-        weights.append((inside, weight))
-        scaled = jnp.where(inside, weight * row_buf[:, part * COLS : (part + 1) * COLS], 0.0)
-        coarse = scaled.astype(jnp.bfloat16)
-        fine = (scaled - coarse.astype(jnp.float32)).astype(jnp.bfloat16)
-        left.append(jnp.concatenate([coarse, fine], axis=0))
+        sums = jnp.concatenate(
+            [spread[block * owned : (block + 1) * owned] for block in range(part * per_bin, (part + 1) * per_bin)],
+            axis=1,
+        )
+        scaled = inner_ref[:, part * COLS : (part + 1) * COLS] * sums
+        left.append(jnp.concatenate(halves(scaled), axis=0))
     image = [None] * bins
     for shift in range(1 - bins, bins):
         first, last = max(0, -shift), min(bins, bins - shift)
@@ -284,39 +331,20 @@
             to = part + shift
             image[to] = term if image[to] is None else image[to] + term
     for part in range(bins):
-        inside, weight = weights[part]
-        out_ref[0, :, part * COLS : (part + 1) * COLS] = jnp.where(
-            inside, image[part] / (math.pi * weight), 0.0
-        )
-
-
-def invert(mine, other, table, owner, lengths, devices, owned, samples):
-    def kernel(*refs):
-        invert_kernel(devices, *refs)
-
-    smem = pl.BlockSpec(memory_space=pltpu.SMEM)
+        columns = slice(part * COLS, (part + 1) * COLS)
+        out_ref[0, :, columns] = image[part] * outer_ref[:, columns]
+
+
+def invert(mine, other, prepared, owned, samples):
     vmem = pl.BlockSpec(memory_space=pltpu.VMEM)
     return pl.pallas_call(
-        kernel,
+        invert_kernel,
         out_shape=jax.ShapeDtypeStruct((1, owned, samples), jnp.float32),
-        in_specs=[smem, smem, vmem, vmem, vmem, vmem],
+        in_specs=[vmem] * 7,
         out_specs=vmem,
-        scratch_shapes=[
-            pltpu.VMEM((mine.shape[0] + 3 * owned, LANE), jnp.float32),
-            pltpu.VMEM((owned, samples), jnp.float32),
-        ],
         compiler_params=pltpu.CompilerParams(vmem_limit_bytes=32 << 20),
         name="invert",
-    )(owner, lengths, mine, other, *table)
-
-
-def hilbert_table(bins):
-    shape = (2 * bins - 1, COLS, COLS)
-    shift = (lax.broadcasted_iota(jnp.int32, shape, 0) - (bins - 1)) * COLS
-    gap = shift + lax.broadcasted_iota(jnp.int32, shape, 2) - lax.broadcasted_iota(jnp.int32, shape, 1)
-    exact = 1.0 / (gap.astype(jnp.float32) + 0.5)
-    coarse = lax.reduce_precision(exact, 8, 7)
-    return coarse.astype(jnp.bfloat16), (exact - coarse).astype(jnp.bfloat16)
+    )(mine, other, *prepared)
 
 
 def per_device(proj, tiles, owner, lengths):
@@ -326,7 +354,7 @@
     owned = rows // devices
     packed = rows_per_owner(owned)
     keep, send = project(proj, tiles, owner, lengths, devices)
-    table = hilbert_table(samples // COLS)
+    prepared = prepare(owner, lengths, devices, owned, samples, packed)
     held = devices // 2
     for mask in exchange_masks(devices)[:-1]:
         pairs = [(device, device ^ mask) for device in range(devices)]
@@ -336,7 +364,7 @@
     mask = exchange_masks(devices)[-1]
     pairs = [(device, device ^ mask) for device in range(devices)]
     other = lax.ppermute(send, "view", pairs)
-    return invert(keep, other, table, owner, lengths, devices, owned, samples)
+    return invert(keep, other, prepared, owned, samples)
 
 
 def solution(mesh):

time: 19.7 us -> 19.2 us (0.975)
  other arithmetic: 0.61 us -> 0.04 us
  Pallas kernels: 4.24 us -> 4.5 us
  waiting for transfers between devices: 6.42 us -> 6.17 us
    convert_element_type x1 -> x0, other arithmetic: 0.56 us -> none  [hilbert_table(): return (coarse.astype(jnp.bfloat16), (exact - coarse).astype(jnp.bfloat16))]
    pallas_call x1 -> x2, Pallas kernels: 1.68 us -> 1.94 us  [the longest x1 1.12 us: invert(): pl.pallas_call(invert_kernel, out_shape=jax.ShapeDtypeStruct((1, owned, s...]
    ppermute x1, waiting for transfers between devices: 0.95 us -> 0.69 us  [per_device(): other = lax.ppermute(send, 'view', pairs)]
  transfers between devices with their start and end apart: 4 -> 4, of which waited for: 4 -> 4; matrix products, arithmetic and copies ran while one was open for 3% -> 0% of each run, Pallas kernels for 0% -> 4%
where the time goes in v3:
time: 19.2 us; the launch traced here: 19 us
  starting transfers between devices  8.23 us (43%)
  waiting for transfers between devices  6.17 us (32%)
  Pallas kernels  4.5 us (23%)
    ppermute x3, waiting for transfers between devices, per_device(): total = keep + lax.ppermute(send, 'view', pairs)  5.48 us
    ppermute x3, starting transfers between devices, per_device(): total = keep + lax.ppermute(send, 'view', pairs)  5.25 us
    ppermute x1, starting transfers between devices, per_device(): other = lax.ppermute(send, 'view', pairs)  2.98 us
    pallas_call x1, Pallas kernels, project(): pl.pallas_call(kernel, out_shape=(shape, shape), in_specs=[hbm] * 4, out_...  2.56 us
    pallas_call x1, Pallas kernels, invert(): pl.pallas_call(invert_kernel, out_shape=jax.ShapeDtypeStruct((1, owned, s...  1.12 us
    pallas_call x1, Pallas kernels, prepare(): pl.pallas_call(kernel, out_shape=(pltpu.VMEM((owned * samples // LANE, pa...  0.82 us
    ppermute x1, waiting for transfers between devices, per_device(): other = lax.ppermute(send, 'view', pairs)  0.69 us
  transfers between devices with their start and end apart: 4, of which 4 were waited for; matrix products, arithmetic and copies ran while one was open for 0% of the time, Pallas kernels for 4%

profile of v3, /device:TPU:0, one launch (start us, length us, event | category | flops | bytes accessed | tf_op | source)
XLA Modules:
  0.0 19.0 jit_solution(5235056450146483907)
XLA Ops:
  0.0 2.6 %project.1 = (f32[360,128]{1,0:T(8,128)S(1)}, f32[360,128]{1,0:T(8,128)S(1)}) custom-call(s32[2,128]{1,0:T(2,128)} %refs_0_.3, s32[2,128]{1,0:T(2,128)} %refs_1_.3, bf16[12,128,128]{2,1,0:T(8,128)(2,1)} %refs_2_.1, bf16[6,256,1024]{2,1,0:T(8,128)(2,1)} %refs_3_.1), custom_call_target="tpu_custom_call" | custom-call | flops 402653184 | bytes 3538944 | tf_op jit(solution)/shard_map/project/pallas_call | solution.py:186
  2.6 0.5 %collective-permute-start = (f32[360,128]{1,0:T(8,128)S(1)}, f32[360,128]{1,0:T(8,128)S(1)}, u32[]{:S(2)}, u32[]{:S(2)}) collective-permute-start(f32[360,128]{1,0:T(8,128)S(1)} %get-tuple-element.13), channel_id=1, source_target_pairs={{0,2},{2,0},{4,6},{6,4},{8,10},{10,8},{12,14},{14,12},{16,18},{18,... | collective-permute-start | bytes 552968 | tf_op jit(solution)/shard_map/ppermute | solution.py:361
  3.1 1.1 %collective-permute-done = f32[360,128]{1,0:T(8,128)S(1)} collective-permute-done((f32[360,128]{1,0:T(8,128)S(1)}, f32[360,128]{1,0:T(8,128)S(1)}, u32[]{:S(2)}, u32[]{:S(2)}) %collective-permute-start) | collective-permute-done | bytes 184352 | tf_op jit(solution)/shard_map/ppermute | solution.py:361
  4.2 2.7 %collective-permute-start.1 = (f32[176,128]{1,0:T(8,128)S(1)}, f32[176,128]{1,0:T(8,128)S(1)}, u32[]{:S(2)}, u32[]{:S(2)}) collective-permute-start(f32[176,128]{1,0:T(8,128)S(1)} %slice.25), channel_id=1, source_target_pairs={{0,6},{2,4},{4,2},{6,0},{8,14},{10,12},{12,10},{14,8},{16,22},{18,... | collective-permute-start | bytes 270344 | tf_op jit(solution)/shard_map/ppermute | solution.py:361
  6.9 2.7 %collective-permute-done.1 = f32[176,128]{1,0:T(8,128)S(1)} collective-permute-done((f32[176,128]{1,0:T(8,128)S(1)}, f32[176,128]{1,0:T(8,128)S(1)}, u32[]{:S(2)}, u32[]{:S(2)}) %collective-permute-start.1) | collective-permute-done | bytes 90144 | tf_op jit(solution)/shard_map/ppermute | solution.py:361
  9.6 2.0 %collective-permute-start.2 = (f32[88,128]{1,0:T(8,128)S(1)}, f32[88,128]{1,0:T(8,128)S(1)}, u32[]{:S(2)}, u32[]{:S(2)}) collective-permute-start(f32[88,128]{1,0:T(8,128)S(1)} %slice.27), channel_id=1, source_target_pairs={{0,10},{2,8},{4,14},{6,12},{8,2},{10,0},{12,6},{14,4},{16,26},{18,... | collective-permute-start | bytes 135176 | tf_op jit(solution)/shard_map/ppermute | solution.py:361
  11.6 1.7 %collective-permute-done.2 = f32[88,128]{1,0:T(8,128)S(1)} collective-permute-done((f32[88,128]{1,0:T(8,128)S(1)}, f32[88,128]{1,0:T(8,128)S(1)}, u32[]{:S(2)}, u32[]{:S(2)}) %collective-permute-start.2) | collective-permute-done | bytes 45088 | tf_op jit(solution)/shard_map/ppermute | solution.py:361
  13.4 3.0 %collective-permute-start.3 = (f32[44,128]{1,0:T(8,128)S(1)}, f32[44,128]{1,0:T(8,128)S(1)}, u32[]{:S(2)}, u32[]{:S(2)}) collective-permute-start(f32[44,128]{1,0:T(8,128)S(1)} %get-tuple-element.19), channel_id=1, source_target_pairs={{0,18},{2,16},{4,22},{6,20},{8,26},{10,24},{12,30},{14,28},{16,2},... | collective-permute-start | bytes 67592 | tf_op jit(solution)/shard_map/ppermute | solution.py:366
  16.4 0.8 %prepare.1 = (bf16[64,44]{1,0:T(8,128)(2,1)S(1)}, f32[8,1024]{1,0:T(8,128)S(1)}, f32[8,1024]{1,0:T(8,128)S(1)}, bf16[7,256,256]{2,1,0:T(8,128)(2,1)S(1)}, bf16[7,256,256]{2,1,0:T(8,128)(2,1)S(1)}) custom-call(s32[2,128]{1,0:T(2,128)} %refs_0_.3, s32[2,128]{1,0:T(2,128)} %refs_1_.3), custom_call_target="tpu_custom_call" | custom-call | flops 4194304 | bytes 2097152 | tf_op jit(solution)/shard_map/prepare/pallas_call | solution.py:279
  17.2 0.7 %collective-permute-done.3.other_ref = f32[44,128]{1,0:T(8,128)S(1)} collective-permute-done((f32[44,128]{1,0:T(8,128)S(1)}, f32[44,128]{1,0:T(8,128)S(1)}, u32[]{:S(2)}, u32[]{:S(2)}) %collective-permute-start.3) | collective-permute-done | bytes 22560 | tf_op jit(solution)/shard_map/ppermute | solution.py:366
  17.9 1.1 %invert.1 = f32[1,8,1024]{2,1,0:T(8,128)} custom-call(f32[44,128]{1,0:T(8,128)S(1)} %get-tuple-element.20.mine_ref, f32[44,128]{1,0:T(8,128)S(1)} %collective-permute-done.3.other_ref, bf16[64,44]{1,0:T(8,128)(2,1)S(1)} %get-tuple-element.14.unpick_ref, f32[8,1024]{1,0:T(8,128)S(1)} %get-tuple-element.15.inner_ref, ...), custom_call_target="tpu_custom_call" | custom-call | tf_op jit(solution)/shard_map/invert/pallas_call | solution.py:340
  (6 shorter events, 0.1 us)
Async XLA Ops:
  2.6 1.6 %collective-permute-start = (f32[360,128]{1,0:T(8,128)S(1)}, f32[360,128]{1,0:T(8,128)S(1)}, u32[]{:S(2)}, u32[]{:S(2)}) collective-permute-start(f32[360,128]{1,0:T(8,128)S(1)} %get-tuple-element.13), channel_id=1, source_target_pairs={{0,2},{2,0},{4,6},{6,4},{8,10},{10,8},{12,14},{14,12},{16,18},{18,... | collective-permute-start | bytes 552968 | tf_op jit(solution)/shard_map/ppermute | solution.py:361
  4.2 5.4 %collective-permute-start.1 = (f32[176,128]{1,0:T(8,128)S(1)}, f32[176,128]{1,0:T(8,128)S(1)}, u32[]{:S(2)}, u32[]{:S(2)}) collective-permute-start(f32[176,128]{1,0:T(8,128)S(1)} %slice.25), channel_id=1, source_target_pairs={{0,6},{2,4},{4,2},{6,0},{8,14},{10,12},{12,10},{14,8},{16,22},{18,... | collective-permute-start | bytes 270344 | tf_op jit(solution)/shard_map/ppermute | solution.py:361
  9.6 3.8 %collective-permute-start.2 = (f32[88,128]{1,0:T(8,128)S(1)}, f32[88,128]{1,0:T(8,128)S(1)}, u32[]{:S(2)}, u32[]{:S(2)}) collective-permute-start(f32[88,128]{1,0:T(8,128)S(1)} %slice.27), channel_id=1, source_target_pairs={{0,10},{2,8},{4,14},{6,12},{8,2},{10,0},{12,6},{14,4},{16,26},{18,... | collective-permute-start | bytes 135176 | tf_op jit(solution)/shard_map/ppermute | solution.py:361
  13.4 4.5 %collective-permute-start.3 = (f32[44,128]{1,0:T(8,128)S(1)}, f32[44,128]{1,0:T(8,128)S(1)}, u32[]{:S(2)}, u32[]{:S(2)}) collective-permute-start(f32[44,128]{1,0:T(8,128)S(1)} %get-tuple-element.19), channel_id=1, source_target_pairs={{0,18},{2,16},{4,22},{6,20},{8,26},{10,24},{12,30},{14,28},{16,2},... | collective-permute-start | bytes 67592 | tf_op jit(solution)/shard_map/ppermute | solution.py:366

commit v4 on v3

--- a/solution.py
+++ b/solution.py
@@ -12,31 +12,36 @@
 COLS = 256
 
 
-def exchange_masks(devices):
+def side(place):
+    return (place ^ (place >> 1) ^ (place >> 2)) & 1
+
+
+def exchange_pairs(devices):
+    steps = [[place ^ 1 for place in range(devices)]]
+    for first, second in ((3, 5), (5, 3)):
+        steps.append([place ^ (second if side(place) else first) for place in range(devices)])
+    step = 8
+    while step < devices:
+        steps.append([place ^ (step | 1) for place in range(devices)])
+        step *= 2
+    return [list(enumerate(partners)) for partners in steps]
+
+
+def slot_of(place, me, devices):
+    distance = place ^ me
     steps = devices.bit_length() - 1
-    return [1] + [(1 << step) | 1 for step in range(1, steps)]
-
-
-def slot_mask(slot, devices):
-    masks = exchange_masks(devices)
-    steps = len(masks)
-    distance = 0
-    for step, mask in enumerate(masks):
-        bit = (slot >> (steps - 1 - step)) & 1
-        distance = distance ^ (bit * mask)
-    return distance
-
-
-def slot_of(distance, devices):
-    steps = devices.bit_length() - 1
+    first = distance & 1
     slot = jnp.zeros_like(distance)
-    parity = jnp.zeros_like(distance)
     for step in range(1, steps):
         bit = (distance >> step) & 1
-        slot = slot | (bit << (steps - 1 - step))
-        parity = parity ^ bit
-    first = (distance & 1) ^ parity
-    return slot | (first << (steps - 1))
+        first = first ^ bit
+        if step > 2:
+            slot = slot | (bit << (steps - 1 - step))
+    near, far = (distance >> 1) & 1, (distance >> 2) & 1
+    swap = side(me) ^ first
+    early = jnp.where(swap == 1, far, near)
+    late = jnp.where(swap == 1, near, far)
+    return slot | (first << (steps - 1)) | (early << (steps - 2)) | (late << (steps - 3))
 
 
 def rows_per_owner(owned):
@@ -96,7 +101,7 @@
     position = jnp.sum(jnp.where(hit, down.astype(jnp.float32), 0.0), axis=0, keepdims=True)
     position = position.astype(jnp.int32)
     place = position // owned
-    slot = slot_of(place ^ me, devices)
+    slot = slot_of(place, me, devices)
 
     reach = turned((lengths + (LANE - 1)) // LANE)
     block_index = lax.broadcasted_iota(jnp.int32, (rows, LANE), 1).astype(jnp.float32)
@@ -356,14 +361,12 @@
     keep, send = project(proj, tiles, owner, lengths, devices)
     prepared = prepare(owner, lengths, devices, owned, samples, packed)
     held = devices // 2
-    for mask in exchange_masks(devices)[:-1]:
-        pairs = [(device, device ^ mask) for device in range(devices)]
+    steps = exchange_pairs(devices)
+    for pairs in steps[:-1]:
         total = keep + lax.ppermute(send, "view", pairs)
         held //= 2
         keep, send = total[: held * packed], total[held * packed : 2 * held * packed]
-    mask = exchange_masks(devices)[-1]
-    pairs = [(device, device ^ mask) for device in range(devices)]
-    other = lax.ppermute(send, "view", pairs)
+    other = lax.ppermute(send, "view", steps[-1])
     return invert(keep, other, prepared, owned, samples)
 
 

time: 19.2 us -> 18.4 us (0.958)
  waiting for transfers between devices: 6.17 us -> 5.69 us
  starting transfers between devices: 8.23 us -> 7.9 us
    ppermute x3, waiting for transfers between devices: 5.48 us -> 5 us  [per_device(): total = keep + lax.ppermute(send, 'view', pairs)]
  transfers between devices with their start and end apart: 4 -> 4, of which waited for: 4 -> 4; matrix products, arithmetic and copies ran while one was open for 0% -> 0% of each run, Pallas kernels for 4% -> 5%
where the time goes in v4:
time: 18.4 us; the launch traced here: 18.2 us
  starting transfers between devices  7.9 us (43%)
  waiting for transfers between devices  5.69 us (31%)
  Pallas kernels  4.5 us (24%)
    ppermute x3, starting transfers between devices, per_device(): total = keep + lax.ppermute(send, 'view', pairs)  5.08 us
    ppermute x3, waiting for transfers between devices, per_device(): total = keep + lax.ppermute(send, 'view', pairs)  5 us
    ppermute x1, starting transfers between devices, per_device(): other = lax.ppermute(send, 'view', steps[-1])  2.82 us
    pallas_call x1, Pallas kernels, project(): pl.pallas_call(kernel, out_shape=(shape, shape), in_specs=[hbm] * 4, out_...  2.56 us
    pallas_call x1, Pallas kernels, invert(): pl.pallas_call(invert_kernel, out_shape=jax.ShapeDtypeStruct((1, owned, s...  1.12 us
    pallas_call x1, Pallas kernels, prepare(): pl.pallas_call(kernel, out_shape=(pltpu.VMEM((owned * samples // LANE, pa...  0.82 us
    ppermute x1, waiting for transfers between devices, per_device(): other = lax.ppermute(send, 'view', steps[-1])  0.69 us
  transfers between devices with their start and end apart: 4, of which 4 were waited for; matrix products, arithmetic and copies ran while one was open for 0% of the time, Pallas kernels for 5%

profile of v4, /device:TPU:0, one launch (start us, length us, event | category | flops | bytes accessed | tf_op | source)
XLA Modules:
  0.0 18.2 jit_solution(5153039990403075522)
XLA Ops:
  0.0 2.6 %project.1 = (f32[360,128]{1,0:T(8,128)S(1)}, f32[360,128]{1,0:T(8,128)S(1)}) custom-call(s32[2,128]{1,0:T(2,128)} %refs_0_.3, s32[2,128]{1,0:T(2,128)} %refs_1_.3, bf16[12,128,128]{2,1,0:T(8,128)(2,1)} %refs_2_.1, bf16[6,256,1024]{2,1,0:T(8,128)(2,1)} %refs_3_.1), custom_call_target="tpu_custom_call" | custom-call | flops 402653184 | bytes 3538944 | tf_op jit(solution)/shard_map/project/pallas_call | solution.py:191
  2.6 0.5 %collective-permute-start = (f32[360,128]{1,0:T(8,128)S(1)}, f32[360,128]{1,0:T(8,128)S(1)}, u32[]{:S(2)}, u32[]{:S(2)}) collective-permute-start(f32[360,128]{1,0:T(8,128)S(1)} %get-tuple-element.13), channel_id=1, source_target_pairs={{0,2},{2,0},{4,6},{6,4},{8,10},{10,8},{12,14},{14,12},{16,18},{18,... | collective-permute-start | bytes 552968 | tf_op jit(solution)/shard_map/ppermute | solution.py:366
  3.1 1.1 %collective-permute-done = f32[360,128]{1,0:T(8,128)S(1)} collective-permute-done((f32[360,128]{1,0:T(8,128)S(1)}, f32[360,128]{1,0:T(8,128)S(1)}, u32[]{:S(2)}, u32[]{:S(2)}) %collective-permute-start) | collective-permute-done | bytes 184352 | tf_op jit(solution)/shard_map/ppermute | solution.py:366
  4.2 2.7 %collective-permute-start.1 = (f32[176,128]{1,0:T(8,128)S(1)}, f32[176,128]{1,0:T(8,128)S(1)}, u32[]{:S(2)}, u32[]{:S(2)}) collective-permute-start(f32[176,128]{1,0:T(8,128)S(1)} %slice.25), channel_id=1, source_target_pairs={{0,6},{2,8},{4,14},{6,0},{8,2},{10,12},{12,10},{14,4},{16,22},{18,... | collective-permute-start | bytes 270344 | tf_op jit(solution)/shard_map/ppermute | solution.py:366
  6.9 2.2 %collective-permute-done.1 = f32[176,128]{1,0:T(8,128)S(1)} collective-permute-done((f32[176,128]{1,0:T(8,128)S(1)}, f32[176,128]{1,0:T(8,128)S(1)}, u32[]{:S(2)}, u32[]{:S(2)}) %collective-permute-start.1) | collective-permute-done | bytes 90144 | tf_op jit(solution)/shard_map/ppermute | solution.py:366
  9.1 1.9 %collective-permute-start.2 = (f32[88,128]{1,0:T(8,128)S(1)}, f32[88,128]{1,0:T(8,128)S(1)}, u32[]{:S(2)}, u32[]{:S(2)}) collective-permute-start(f32[88,128]{1,0:T(8,128)S(1)} %slice.27), channel_id=1, source_target_pairs={{0,10},{2,4},{4,2},{6,12},{8,14},{10,0},{12,6},{14,8},{16,26},{18,... | collective-permute-start | bytes 135176 | tf_op jit(solution)/shard_map/ppermute | solution.py:366
  11.0 1.7 %collective-permute-done.2 = f32[88,128]{1,0:T(8,128)S(1)} collective-permute-done((f32[88,128]{1,0:T(8,128)S(1)}, f32[88,128]{1,0:T(8,128)S(1)}, u32[]{:S(2)}, u32[]{:S(2)}) %collective-permute-start.2) | collective-permute-done | bytes 45088 | tf_op jit(solution)/shard_map/ppermute | solution.py:366
  12.7 2.8 %collective-permute-start.3 = (f32[44,128]{1,0:T(8,128)S(1)}, f32[44,128]{1,0:T(8,128)S(1)}, u32[]{:S(2)}, u32[]{:S(2)}) collective-permute-start(f32[44,128]{1,0:T(8,128)S(1)} %get-tuple-element.19), channel_id=1, source_target_pairs={{0,18},{2,16},{4,22},{6,20},{8,26},{10,24},{12,30},{14,28},{16,2},... | collective-permute-start | bytes 67592 | tf_op jit(solution)/shard_map/ppermute | solution.py:369
  15.6 0.8 %prepare.1 = (bf16[64,44]{1,0:T(8,128)(2,1)S(1)}, f32[8,1024]{1,0:T(8,128)S(1)}, f32[8,1024]{1,0:T(8,128)S(1)}, bf16[7,256,256]{2,1,0:T(8,128)(2,1)S(1)}, bf16[7,256,256]{2,1,0:T(8,128)(2,1)S(1)}) custom-call(s32[2,128]{1,0:T(2,128)} %refs_0_.3, s32[2,128]{1,0:T(2,128)} %refs_1_.3), custom_call_target="tpu_custom_call" | custom-call | flops 4194304 | bytes 2097152 | tf_op jit(solution)/shard_map/prepare/pallas_call | solution.py:284
  16.4 0.7 %collective-permute-done.3.other_ref = f32[44,128]{1,0:T(8,128)S(1)} collective-permute-done((f32[44,128]{1,0:T(8,128)S(1)}, f32[44,128]{1,0:T(8,128)S(1)}, u32[]{:S(2)}, u32[]{:S(2)}) %collective-permute-start.3) | collective-permute-done | bytes 22560 | tf_op jit(solution)/shard_map/ppermute | solution.py:369
  17.1 1.1 %invert.1 = f32[1,8,1024]{2,1,0:T(8,128)} custom-call(f32[44,128]{1,0:T(8,128)S(1)} %get-tuple-element.20.mine_ref, f32[44,128]{1,0:T(8,128)S(1)} %collective-permute-done.3.other_ref, bf16[64,44]{1,0:T(8,128)(2,1)S(1)} %get-tuple-element.14.unpick_ref, f32[8,1024]{1,0:T(8,128)S(1)} %get-tuple-element.15.inner_ref, ...), custom_call_target="tpu_custom_call" | custom-call | tf_op jit(solution)/shard_map/invert/pallas_call | solution.py:345
  (6 shorter events, 0.1 us)
Async XLA Ops:
  2.6 1.6 %collective-permute-start = (f32[360,128]{1,0:T(8,128)S(1)}, f32[360,128]{1,0:T(8,128)S(1)}, u32[]{:S(2)}, u32[]{:S(2)}) collective-permute-start(f32[360,128]{1,0:T(8,128)S(1)} %get-tuple-element.13), channel_id=1, source_target_pairs={{0,2},{2,0},{4,6},{6,4},{8,10},{10,8},{12,14},{14,12},{16,18},{18,... | collective-permute-start | bytes 552968 | tf_op jit(solution)/shard_map/ppermute | solution.py:366
  4.2 4.9 %collective-permute-start.1 = (f32[176,128]{1,0:T(8,128)S(1)}, f32[176,128]{1,0:T(8,128)S(1)}, u32[]{:S(2)}, u32[]{:S(2)}) collective-permute-start(f32[176,128]{1,0:T(8,128)S(1)} %slice.25), channel_id=1, source_target_pairs={{0,6},{2,8},{4,14},{6,0},{8,2},{10,12},{12,10},{14,4},{16,22},{18,... | collective-permute-start | bytes 270344 | tf_op jit(solution)/shard_map/ppermute | solution.py:366
  9.1 3.6 %collective-permute-start.2 = (f32[88,128]{1,0:T(8,128)S(1)}, f32[88,128]{1,0:T(8,128)S(1)}, u32[]{:S(2)}, u32[]{:S(2)}) collective-permute-start(f32[88,128]{1,0:T(8,128)S(1)} %slice.27), channel_id=1, source_target_pairs={{0,10},{2,4},{4,2},{6,12},{8,14},{10,0},{12,6},{14,8},{16,26},{18,... | collective-permute-start | bytes 135176 | tf_op jit(solution)/shard_map/ppermute | solution.py:366
  12.7 4.3 %collective-permute-start.3 = (f32[44,128]{1,0:T(8,128)S(1)}, f32[44,128]{1,0:T(8,128)S(1)}, u32[]{:S(2)}, u32[]{:S(2)}) collective-permute-start(f32[44,128]{1,0:T(8,128)S(1)} %get-tuple-element.19), channel_id=1, source_target_pairs={{0,18},{2,16},{4,22},{6,20},{8,26},{10,24},{12,30},{14,28},{16,2},... | collective-permute-start | bytes 67592 | tf_op jit(solution)/shard_map/ppermute | solution.py:369

commit v5 on v4

--- a/solution.py
+++ b/solution.py
@@ -218,12 +218,11 @@
 
 
 def prepare_kernel(
-    devices, owner_hbm, lengths_hbm, unpick_ref, inner_ref, outer_ref, coarse_ref, fine_ref,
+    devices, owner_hbm, lengths_hbm, offset_ref, rank_ref, inner_ref, outer_ref, coarse_ref, fine_ref,
     owner_s, lengths_s, sem,
 ):
     owned, samples = inner_ref.shape
     blocks = samples // LANE
-    packed = unpick_ref.shape[1]
     distances = coarse_ref.shape[0]
     group = lax.axis_index("chord")
     me = lax.axis_index("view")
@@ -253,15 +252,12 @@
     for index in range(owned):
         ahead = (lengths[index] > length) | ((lengths[index] == length) & (index < sub))
         rank = rank + jnp.where(ahead, 1, 0)
-    reach = (length + (LANE - 1)) >> 7
-    rows = []
+    rank_ref[...] = rank
     for block in range(blocks):
         offset = jnp.int32(0)
         for index in range(owned):
             offset = offset + jnp.minimum((lengths[index] + (LANE - 1)) >> 7, block)
-        hit = (lane == rank + offset) & (reach > block)
-        rows.append(jnp.where(hit, 1.0, 0.0))
-    unpick_ref[...] = jnp.concatenate(rows, axis=0)[:, :packed].astype(jnp.bfloat16)
+        offset_ref[0, block] = offset
 
     long = length.astype(jnp.float32)
     for block in range(blocks):
@@ -273,7 +269,7 @@
         outer_ref[:, columns] = jnp.where(inside, 1.0 / (math.pi * weight), 0.0)
 
 
-def prepare(owner, lengths, devices, owned, samples, packed):
+def prepare(owner, lengths, devices, owned, samples):
     distances = 2 * (samples // COLS) - 1
     inputs = [pltpu.with_memory_space_constraint(x, pltpu.HBM) for x in (owner, lengths)]
     vmem = pl.BlockSpec(memory_space=pltpu.VMEM)
@@ -284,14 +280,15 @@
     return pl.pallas_call(
         kernel,
         out_shape=(
-            pltpu.VMEM((owned * samples // LANE, packed), jnp.bfloat16),
+            pltpu.SMEM((1, samples // LANE), jnp.int32),
+            pltpu.VMEM((owned, LANE), jnp.int32),
             pltpu.VMEM((owned, samples), jnp.float32),
             pltpu.VMEM((owned, samples), jnp.float32),
             pltpu.VMEM((distances, COLS, COLS), jnp.bfloat16),
             pltpu.VMEM((distances, COLS, COLS), jnp.bfloat16),
         ),
         in_specs=[pl.BlockSpec(memory_space=pltpu.HBM)] * 2,
-        out_specs=(vmem,) * 5,
+        out_specs=(pl.BlockSpec(memory_space=pltpu.SMEM),) + (vmem,) * 5,
         scratch_shapes=[
             pltpu.SMEM(owner.shape, jnp.int32),
             pltpu.SMEM(lengths.shape, jnp.int32),
@@ -303,7 +300,9 @@
     )(*inputs)
 
 
-def invert_kernel(mine_ref, other_ref, unpick_ref, inner_ref, outer_ref, coarse_ref, fine_ref, out_ref):
+def invert_kernel(
+    mine_ref, other_ref, offset_ref, rank_ref, inner_ref, outer_ref, coarse_ref, fine_ref, out_ref, sum_buf
+):
     owned, samples = inner_ref.shape
     bins = samples // COLS
     per_bin = COLS // LANE
@@ -312,16 +311,21 @@
         coarse = value.astype(jnp.bfloat16)
         return coarse, (value - coarse.astype(jnp.float32)).astype(jnp.bfloat16)
 
-    both = jnp.concatenate(halves(mine_ref[...] + other_ref[...]), axis=1)
-    spread = jnp.dot(unpick_ref[...], both, preferred_element_type=jnp.float32)
-    spread = spread[:, :LANE] + spread[:, LANE:]
+    packed = mine_ref.shape[0]
+    sum_buf[0:packed, :] = mine_ref[...] + other_ref[...]
+    rank = rank_ref[...]
+
+    def chord_rows(block):
+        ordered = sum_buf[pl.ds(offset_ref[0, block], owned), :]
+        return jnp.take_along_axis(ordered, rank, axis=0)
+
     left = []
     for part in range(bins):
         sums = jnp.concatenate(
-            [spread[block * owned : (block + 1) * owned] for block in range(part * per_bin, (part + 1) * per_bin)],
-            axis=1,
+            [chord_rows(block) for block in range(part * per_bin, (part + 1) * per_bin)], axis=1
         )
-        scaled = inner_ref[:, part * COLS : (part + 1) * COLS] * sums
+        weight = inner_ref[:, part * COLS : (part + 1) * COLS]
+        scaled = jnp.where(weight > 0.0, weight * sums, 0.0)
         left.append(jnp.concatenate(halves(scaled), axis=0))
     image = [None] * bins
     for shift in range(1 - bins, bins):
@@ -345,8 +349,9 @@
     return pl.pallas_call(
         invert_kernel,
         out_shape=jax.ShapeDtypeStruct((1, owned, samples), jnp.float32),
-        in_specs=[vmem] * 7,
+        in_specs=[vmem, vmem, pl.BlockSpec(memory_space=pltpu.SMEM)] + [vmem] * 5,
         out_specs=vmem,
+        scratch_shapes=[pltpu.VMEM((mine.shape[0] + owned, LANE), jnp.float32)],
         compiler_params=pltpu.CompilerParams(vmem_limit_bytes=32 << 20),
         name="invert",
     )(mine, other, *prepared)
@@ -359,13 +364,14 @@
     owned = rows // devices
     packed = rows_per_owner(owned)
     keep, send = project(proj, tiles, owner, lengths, devices)
-    prepared = prepare(owner, lengths, devices, owned, samples, packed)
+    prepared = prepare(owner, lengths, devices, owned, samples)
     held = devices // 2
     steps = exchange_pairs(devices)
     for pairs in steps[:-1]:
-        total = keep + lax.ppermute(send, "view", pairs)
+        other = lax.ppermute(send, "view", pairs)
         held //= 2
-        keep, send = total[: held * packed], total[held * packed : 2 * held * packed]
+        middle = held * packed
+        keep, send = keep[:middle] + other[:middle], keep[middle : 2 * middle] + other[middle : 2 * middle]
     other = lax.ppermute(send, "view", steps[-1])
     return invert(keep, other, prepared, owned, samples)
 

time: 18.4 us -> 18.2 us (0.989)
  no operation moved by 1% of the time
where the time goes in v5:
time: 18.2 us; the launch traced here: 18.1 us
  starting transfers between devices  7.9 us (43%)
  waiting for transfers between devices  5.69 us (31%)
  Pallas kernels  4.39 us (24%)
    ppermute x3, starting transfers between devices, per_device(): other = lax.ppermute(send, 'view', pairs)  5.08 us
    ppermute x3, waiting for transfers between devices, per_device(): other = lax.ppermute(send, 'view', pairs)  5 us
    ppermute x1, starting transfers between devices, per_device(): other = lax.ppermute(send, 'view', steps[-1])  2.82 us
    pallas_call x1, Pallas kernels, project(): pl.pallas_call(kernel, out_shape=(shape, shape), in_specs=[hbm] * 4, out_...  2.56 us
    pallas_call x1, Pallas kernels, invert(): pl.pallas_call(invert_kernel, out_shape=jax.ShapeDtypeStruct((1, owned, s...  1.01 us
    pallas_call x1, Pallas kernels, prepare(): pl.pallas_call(kernel, out_shape=(pltpu.SMEM((1, samples // LANE), jnp.in...  0.82 us
    ppermute x1, waiting for transfers between devices, per_device(): other = lax.ppermute(send, 'view', steps[-1])  0.69 us
  transfers between devices with their start and end apart: 4, of which 4 were waited for; matrix products, arithmetic and copies ran while one was open for 0% of the time, Pallas kernels for 5%

profile of v5, /device:TPU:0, one launch (start us, length us, event | category | flops | bytes accessed | tf_op | source)
XLA Modules:
  0.0 18.1 jit_solution(928123493049745176)
XLA Ops:
  0.0 2.6 %project.1 = (f32[360,128]{1,0:T(8,128)S(1)}, f32[360,128]{1,0:T(8,128)S(1)}) custom-call(s32[2,128]{1,0:T(2,128)} %refs_0_.3, s32[2,128]{1,0:T(2,128)} %refs_1_.3, bf16[12,128,128]{2,1,0:T(8,128)(2,1)} %refs_2_.1, bf16[6,256,1024]{2,1,0:T(8,128)(2,1)} %refs_3_.1), custom_call_target="tpu_custom_call" | custom-call | flops 402653184 | bytes 3538944 | tf_op jit(solution)/shard_map/project/pallas_call | solution.py:191
  2.6 0.5 %collective-permute-start = (f32[360,128]{1,0:T(8,128)S(1)}, f32[360,128]{1,0:T(8,128)S(1)}, u32[]{:S(2)}, u32[]{:S(2)}) collective-permute-start(f32[360,128]{1,0:T(8,128)S(1)} %get-tuple-element.14), channel_id=1, source_target_pairs={{0,2},{2,0},{4,6},{6,4},{8,10},{10,8},{12,14},{14,12},{16,18},{18,... | collective-permute-start | bytes 552968 | tf_op jit(solution)/shard_map/ppermute | solution.py:371
  3.1 1.1 %collective-permute-done = f32[360,128]{1,0:T(8,128)S(1)} collective-permute-done((f32[360,128]{1,0:T(8,128)S(1)}, f32[360,128]{1,0:T(8,128)S(1)}, u32[]{:S(2)}, u32[]{:S(2)}) %collective-permute-start) | collective-permute-done | bytes 184352 | tf_op jit(solution)/shard_map/ppermute | solution.py:371
  4.2 2.7 %collective-permute-start.1 = (f32[176,128]{1,0:T(8,128)S(1)}, f32[176,128]{1,0:T(8,128)S(1)}, u32[]{:S(2)}, u32[]{:S(2)}) collective-permute-start(f32[176,128]{1,0:T(8,128)S(1)} %get-tuple-element.22), channel_id=1, source_target_pairs={{0,6},{2,8},{4,14},{6,0},{8,2},{10,12},{12,10},{14,4},{16,22},{18,... | collective-permute-start | bytes 270344 | tf_op jit(solution)/shard_map/ppermute | solution.py:371
  6.9 2.2 %collective-permute-done.1 = f32[176,128]{1,0:T(8,128)S(1)} collective-permute-done((f32[176,128]{1,0:T(8,128)S(1)}, f32[176,128]{1,0:T(8,128)S(1)}, u32[]{:S(2)}, u32[]{:S(2)}) %collective-permute-start.1) | collective-permute-done | bytes 90144 | tf_op jit(solution)/shard_map/ppermute | solution.py:371
  9.1 1.9 %collective-permute-start.2 = (f32[88,128]{1,0:T(8,128)S(1)}, f32[88,128]{1,0:T(8,128)S(1)}, u32[]{:S(2)}, u32[]{:S(2)}) collective-permute-start(f32[88,128]{1,0:T(8,128)S(1)} %get-tuple-element.24), channel_id=1, source_target_pairs={{0,10},{2,4},{4,2},{6,12},{8,14},{10,0},{12,6},{14,8},{16,26},{18,... | collective-permute-start | bytes 135176 | tf_op jit(solution)/shard_map/ppermute | solution.py:371
  11.0 1.7 %collective-permute-done.2 = f32[88,128]{1,0:T(8,128)S(1)} collective-permute-done((f32[88,128]{1,0:T(8,128)S(1)}, f32[88,128]{1,0:T(8,128)S(1)}, u32[]{:S(2)}, u32[]{:S(2)}) %collective-permute-start.2) | collective-permute-done | bytes 45088 | tf_op jit(solution)/shard_map/ppermute | solution.py:371
  12.7 2.8 %collective-permute-start.3 = (f32[44,128]{1,0:T(8,128)S(1)}, f32[44,128]{1,0:T(8,128)S(1)}, u32[]{:S(2)}, u32[]{:S(2)}) collective-permute-start(f32[44,128]{1,0:T(8,128)S(1)} %get-tuple-element.25), channel_id=1, source_target_pairs={{0,18},{2,16},{4,22},{6,20},{8,26},{10,24},{12,30},{14,28},{16,2},... | collective-permute-start | bytes 67592 | tf_op jit(solution)/shard_map/ppermute | solution.py:375
  15.5 0.8 %prepare.1 = (s32[1,8]{1,0:T(1,128)S(4)}, s32[8,128]{1,0:T(8,128)S(1)}, f32[8,1024]{1,0:T(8,128)S(1)}, f32[8,1024]{1,0:T(8,128)S(1)}, bf16[7,256,256]{2,1,0:T(8,...) custom-call(s32[2,128]{1,0:T(2,128)} %refs_0_.3, s32[2,128]{1,0:T(2,128)} %refs_1_.3), custom_call_target="tpu_custom_call" | custom-call | flops 4194304 | bytes 2097152 | tf_op jit(solution)/shard_map/prepare/pallas_call | solution.py:280
  16.3 0.7 %collective-permute-done.3.other_ref = f32[44,128]{1,0:T(8,128)S(1)} collective-permute-done((f32[44,128]{1,0:T(8,128)S(1)}, f32[44,128]{1,0:T(8,128)S(1)}, u32[]{:S(2)}, u32[]{:S(2)}) %collective-permute-start.3) | collective-permute-done | bytes 22560 | tf_op jit(solution)/shard_map/ppermute | solution.py:375
  17.0 1.0 %invert.1 = f32[1,8,1024]{2,1,0:T(8,128)} custom-call(f32[44,128]{1,0:T(8,128)S(1)} %get-tuple-element.26.mine_ref, f32[44,128]{1,0:T(8,128)S(1)} %collective-permute-done.3.other_ref, s32[1,8]{1,0:T(1,128)S(4)} %get-tuple-element.15.offset_ref, s32[8,128]{1,0:T(8,128)S(1)} %get-tuple-element.16.rank_ref, f32[8,1024]{1,0:T(8,128)S(1)} %get-tuple-element.17.inner_ref, ...), custom_call_target="tpu_custom_call" | custom-call | tf_op jit(solution)/shard_map/invert/pallas_call | solution.py:349
  (3 shorter events, 0.0 us)
Async XLA Ops:
  2.6 1.6 %collective-permute-start = (f32[360,128]{1,0:T(8,128)S(1)}, f32[360,128]{1,0:T(8,128)S(1)}, u32[]{:S(2)}, u32[]{:S(2)}) collective-permute-start(f32[360,128]{1,0:T(8,128)S(1)} %get-tuple-element.14), channel_id=1, source_target_pairs={{0,2},{2,0},{4,6},{6,4},{8,10},{10,8},{12,14},{14,12},{16,18},{18,... | collective-permute-start | bytes 552968 | tf_op jit(solution)/shard_map/ppermute | solution.py:371
  4.2 4.9 %collective-permute-start.1 = (f32[176,128]{1,0:T(8,128)S(1)}, f32[176,128]{1,0:T(8,128)S(1)}, u32[]{:S(2)}, u32[]{:S(2)}) collective-permute-start(f32[176,128]{1,0:T(8,128)S(1)} %get-tuple-element.22), channel_id=1, source_target_pairs={{0,6},{2,8},{4,14},{6,0},{8,2},{10,12},{12,10},{14,4},{16,22},{18,... | collective-permute-start | bytes 270344 | tf_op jit(solution)/shard_map/ppermute | solution.py:371
  9.1 3.6 %collective-permute-start.2 = (f32[88,128]{1,0:T(8,128)S(1)}, f32[88,128]{1,0:T(8,128)S(1)}, u32[]{:S(2)}, u32[]{:S(2)}) collective-permute-start(f32[88,128]{1,0:T(8,128)S(1)} %get-tuple-element.24), channel_id=1, source_target_pairs={{0,10},{2,4},{4,2},{6,12},{8,14},{10,0},{12,6},{14,8},{16,26},{18,... | collective-permute-start | bytes 135176 | tf_op jit(solution)/shard_map/ppermute | solution.py:371
  12.7 4.3 %collective-permute-start.3 = (f32[44,128]{1,0:T(8,128)S(1)}, f32[44,128]{1,0:T(8,128)S(1)}, u32[]{:S(2)}, u32[]{:S(2)}) collective-permute-start(f32[44,128]{1,0:T(8,128)S(1)} %get-tuple-element.25), channel_id=1, source_target_pairs={{0,18},{2,16},{4,22},{6,20},{8,26},{10,24},{12,30},{14,28},{16,2},... | collective-permute-start | bytes 67592 | tf_op jit(solution)/shard_map/ppermute | solution.py:375

commit v6 on v5

--- a/solution.py
+++ b/solution.py
@@ -54,7 +54,7 @@
 
 
 def project_kernel(
-    devices, owner_hbm, lengths_hbm, proj_hbm, tiles_hbm, keep_ref, send_ref,
+    devices, owner_hbm, lengths_hbm, proj_hbm, tiles_hbm, keep_late_ref, keep_ref, send_late_ref, send_ref,
     owner_v, lengths_v, offset_v, offset_s, proj_buf, tile_buf, left_buf, sums_buf,
     small_sem, offset_sem, proj_sem, tile_sem,
 ):
@@ -83,8 +83,9 @@
         copy.start()
         tile_copies.append(copy)
 
-    keep_ref[...] = jnp.zeros_like(keep_ref)
-    send_ref[...] = jnp.zeros_like(send_ref)
+    quarters = [keep_late_ref, keep_ref, send_late_ref, send_ref]
+    for ref in quarters:
+        ref[...] = jnp.zeros_like(ref)
     for copy in small:
         copy.wait()
     down = lax.broadcasted_iota(jnp.int32, (rows, rows), 0)
@@ -135,20 +136,18 @@
         left_buf[:, view * footprint : (view + 1) * footprint] = moved.astype(jnp.bfloat16)
 
     packed = rows_per_owner(owned)
-    half = devices // 2
+    quarter = devices // 4
 
     def put(slot_index, offset, value):
-        def to(out_ref, base):
-            out_ref[pl.ds(base + offset, owned), :] = value
+        def to(out_ref, index):
+            out_ref[pl.ds(index * packed + offset, owned), :] = value
 
         if isinstance(slot_index, int):
-            if slot_index < half:
-                to(keep_ref, slot_index * packed)
-            else:
-                to(send_ref, (slot_index - half) * packed)
+            to(quarters[slot_index // quarter], slot_index % quarter)
         else:
-            pl.when(slot_index < half)(lambda: to(keep_ref, slot_index * packed))
-            pl.when(slot_index >= half)(lambda: to(send_ref, (slot_index - half) * packed))
+            for number, ref in enumerate(quarters):
+                here = slot_index // quarter == number
+                pl.when(here)(lambda ref=ref, number=number: to(ref, slot_index - number * quarter))
 
     def pack(first, last):
         def one(slot_index):
@@ -179,8 +178,8 @@
     blocks, depth, samples = tiles.shape
     owned = rows // devices
     chunks = column_chunks(samples)
-    half_rows = devices // 2 * rows_per_owner(owned) + owned
-    shape = pltpu.VMEM((half_rows, LANE), jnp.float32)
+    quarter_rows = devices // 4 * rows_per_owner(owned) + owned
+    shape = pltpu.VMEM((quarter_rows, LANE), jnp.float32)
     inputs = [pltpu.with_memory_space_constraint(x, pltpu.HBM) for x in (owner, lengths, proj, tiles)]
 
     def kernel(*refs):
@@ -190,9 +189,9 @@
     hbm = pl.BlockSpec(memory_space=pltpu.HBM)
     return pl.pallas_call(
         kernel,
-        out_shape=(shape, shape),
+        out_shape=(shape,) * 4,
         in_specs=[hbm] * 4,
-        out_specs=(vmem, vmem),
+        out_specs=(vmem,) * 4,
         scratch_shapes=[
             pltpu.VMEM(owner.shape, jnp.int32),
             pltpu.VMEM(lengths.shape, jnp.int32),
@@ -363,16 +362,32 @@
     samples = tiles.shape[2]
     owned = rows // devices
     packed = rows_per_owner(owned)
-    keep, send = project(proj, tiles, owner, lengths, devices)
+    keep_late, keep, send_late, send = project(proj, tiles, owner, lengths, devices)
     prepared = prepare(owner, lengths, devices, owned, samples)
-    held = devices // 2
-    steps = exchange_pairs(devices)
-    for pairs in steps[:-1]:
-        other = lax.ppermute(send, "view", pairs)
+    *steps, last_step = exchange_pairs(devices)
+
+    def total(terms, place, count):
+        first, *rest = [array[base + place * packed : base + (place + count) * packed] for array, base in terms]
+        for value in rest:
+            first = first + value
+        return first
+
+    held = devices // 4
+    kept, kept_late = [(keep, 0)], [(keep_late, 0)]
+    for pairs in steps:
+        other, other_late = lax.ppermute(send, "view", pairs), lax.ppermute(send_late, "view", pairs)
+        kept.append((other, 0))
+        if held == 1:
+            break
         held //= 2
-        middle = held * packed
-        keep, send = keep[:middle] + other[:middle], keep[middle : 2 * middle] + other[middle : 2 * middle]
-    other = lax.ppermute(send, "view", steps[-1])
+        send = total(kept, held, held)
+        send, *arrays = lax.optimization_barrier((send, *[array for array, _ in kept]))
+        send_late = total([(array, base) for array, (_, base) in zip(arrays, kept)], 0, held)
+        kept_late.append((other_late, 0))
+        kept = [(array, base + held * packed) for array, base in kept_late]
+    other = lax.ppermute(total(kept, 0, 1), "view", last_step)
+    other_late, other = lax.optimization_barrier((other_late, other))
+    keep = total(kept_late + [(other_late, 0)], 0, 1)
     return invert(keep, other, prepared, owned, samples)
 
 

time: 18.2 us -> 17.5 us (0.962)
  waiting for transfers between devices: 5.69 us -> 4.77 us
  starting transfers between devices: 7.9 us -> 8.1 us
    ppermute x4 -> x7, waiting for transfers between devices: 5.69 us -> 4.77 us  [the longest x3 3.92 us: per_device(): lax.ppermute(send, 'view', pairs)]
    ppermute x4 -> x7, starting transfers between devices: 7.9 us -> 8.1 us  [the longest x3 5.32 us: per_device(): lax.ppermute(send, 'view', pairs)]
  transfers between devices with their start and end apart: 4 -> 7, of which waited for: 4 -> 4; matrix products, arithmetic and copies ran while one was open for 0% -> 0% of each run, Pallas kernels for 5% -> 5%
where the time goes in v6:
time: 17.5 us; the launch traced here: 17.3 us
  starting transfers between devices  8.1 us (46%)
  waiting for transfers between devices  4.77 us (27%)
  Pallas kernels  4.39 us (25%)
    ppermute x3, starting transfers between devices, per_device(): lax.ppermute(send, 'view', pairs)  5.32 us
    ppermute x3, waiting for transfers between devices, per_device(): lax.ppermute(send, 'view', pairs)  3.92 us
    pallas_call x1, Pallas kernels, project(): pl.pallas_call(kernel, out_shape=(shape,) * 4, in_specs=[hbm] * 4, out_sp...  2.55 us
    ppermute x1, starting transfers between devices, per_device(): other = lax.ppermute(total(kept, 0, 1), 'view', last_step)  2.54 us
    pallas_call x1, Pallas kernels, invert(): pl.pallas_call(invert_kernel, out_shape=jax.ShapeDtypeStruct((1, owned, s...  1.02 us
    ppermute x1, waiting for transfers between devices, per_device(): other = lax.ppermute(total(kept, 0, 1), 'view', last_step)  0.84 us
    pallas_call x1, Pallas kernels, prepare(): pl.pallas_call(kernel, out_shape=(pltpu.SMEM((1, samples // LANE), jnp.in...  0.82 us
  transfers between devices with their start and end apart: 7, of which 4 were waited for; matrix products, arithmetic and copies ran while one was open for 0% of the time, Pallas kernels for 5%

profile of v6, /device:TPU:0, one launch (start us, length us, event | category | flops | bytes accessed | tf_op | source)
XLA Modules:
  0.0 17.3 jit_solution(10192944689134319377)
XLA Ops:
  0.0 2.6 %project.1 = (f32[184,128]{1,0:T(8,128)S(1)}, f32[184,128]{1,0:T(8,128)S(1)}, f32[184,128]{1,0:T(8,128)S(1)}, f32[184,128]{1,0:T(8,128)S(1)}) custom-call(s32[2,128]{1,0:T(2,128)} %refs_0_.3, s32[2,128]{1,0:T(2,128)} %refs_1_.3, bf16[12,128,128]{2,1,0:T(8,128)(2,1)} %refs_2_.1, bf16[6,256,1024]{2,1,0:T(8,128)(2,1)} %refs_3_.1), custom_call_target="tpu_custom_call" | custom-call | flops 402653184 | bytes 3538944 | tf_op jit(solution)/shard_map/project/pallas_call | solution.py:190
  2.6 0.5 %collective-permute-start.1 = (f32[184,128]{1,0:T(8,128)S(1)}, f32[184,128]{1,0:T(8,128)S(1)}, u32[]{:S(2)}, u32[]{:S(2)}) collective-permute-start(f32[184,128]{1,0:T(8,128)S(1)} %get-tuple-element.27), channel_id=1, source_target_pairs={{0,2},{2,0},{4,6},{6,4},{8,10},{10,8},{12,14},{14,12},{16,18},{18,... | collective-permute-start | bytes 282632 | tf_op jit(solution)/shard_map/ppermute | solution.py:378
  3.1 0.1 collective-permute-start
  3.2 0.9 %collective-permute-done.1 = f32[184,128]{1,0:T(8,128)S(1)} collective-permute-done((f32[184,128]{1,0:T(8,128)S(1)}, f32[184,128]{1,0:T(8,128)S(1)}, u32[]{:S(2)}, u32[]{:S(2)}) %collective-permute-start.1) | collective-permute-done | bytes 94240 | tf_op jit(solution)/shard_map/ppermute | solution.py:378
  4.0 2.6 %collective-permute-start.3 = (f32[88,128]{1,0:T(8,128)S(1)}, f32[88,128]{1,0:T(8,128)S(1)}, u32[]{:S(2)}, u32[]{:S(2)}) collective-permute-start(f32[88,128]{1,0:T(8,128)S(1)} %slice_add_fusion), channel_id=1, source_target_pairs={{0,6},{2,8},{4,14},{6,0},{8,2},{10,12},{12,10},{14,4},{16,22},{18,... | collective-permute-start | bytes 135176 | tf_op jit(solution)/shard_map/ppermute | solution.py:378
  6.7 0.1 collective-permute-start.2
  6.7 0.0 collective-permute-done
  6.8 1.6 %collective-permute-done.3 = f32[88,128]{1,0:T(8,128)S(1)} collective-permute-done((f32[88,128]{1,0:T(8,128)S(1)}, f32[88,128]{1,0:T(8,128)S(1)}, u32[]{:S(2)}, u32[]{:S(2)}) %collective-permute-start.3) | collective-permute-done | bytes 45088 | tf_op jit(solution)/shard_map/ppermute | solution.py:378
  8.4 2.2 %collective-permute-start.5 = (f32[44,128]{1,0:T(8,128)S(1)}, f32[44,128]{1,0:T(8,128)S(1)}, u32[]{:S(2)}, u32[]{:S(2)}) collective-permute-start(f32[44,128]{1,0:T(8,128)S(1)} %slice_add_fusion.4), channel_id=1, source_target_pairs={{0,10},{2,4},{4,2},{6,12},{8,14},{10,0},{12,6},{14,8},{16,26},{18,... | collective-permute-start | bytes 67592 | tf_op jit(solution)/shard_map/ppermute | solution.py:378
  10.6 0.1 collective-permute-start.4
  10.7 0.0 collective-permute-done.2
  10.7 1.4 %collective-permute-done.5 = f32[44,128]{1,0:T(8,128)S(1)} collective-permute-done((f32[44,128]{1,0:T(8,128)S(1)}, f32[44,128]{1,0:T(8,128)S(1)}, u32[]{:S(2)}, u32[]{:S(2)}) %collective-permute-start.5) | collective-permute-done | bytes 22560 | tf_op jit(solution)/shard_map/ppermute | solution.py:378
  12.1 2.5 %collective-permute-start.6 = (f32[44,128]{1,0:T(8,128)S(1)}, f32[44,128]{1,0:T(8,128)S(1)}, u32[]{:S(2)}, u32[]{:S(2)}) collective-permute-start(f32[44,128]{1,0:T(8,128)S(1)} %fusion), channel_id=1, source_target_pairs={{0,18},{2,16},{4,22},{6,20},{8,26},{10,24},{12,30},{14,28},{16,2},... | collective-permute-start | bytes 67592 | tf_op jit(solution)/shard_map/ppermute | solution.py:388
  14.6 0.8 %prepare.1 = (s32[1,8]{1,0:T(1,128)S(4)}, s32[8,128]{1,0:T(8,128)S(1)}, f32[8,1024]{1,0:T(8,128)S(1)}, f32[8,1024]{1,0:T(8,128)S(1)}, bf16[7,256,256]{2,1,0:T(8,...) custom-call(s32[2,128]{1,0:T(2,128)} %refs_0_.3, s32[2,128]{1,0:T(2,128)} %refs_1_.3), custom_call_target="tpu_custom_call" | custom-call | flops 4194304 | bytes 2097152 | tf_op jit(solution)/shard_map/prepare/pallas_call | solution.py:279
  15.5 0.0 collective-permute-done.4
  15.5 0.8 %collective-permute-done.6.other_ref = f32[44,128]{1,0:T(8,128)S(1)} collective-permute-done((f32[44,128]{1,0:T(8,128)S(1)}, f32[44,128]{1,0:T(8,128)S(1)}, u32[]{:S(2)}, u32[]{:S(2)}) %collective-permute-start.6) | collective-permute-done | bytes 22560 | tf_op jit(solution)/shard_map/ppermute | solution.py:388
  16.3 1.0 %invert.1 = f32[1,8,1024]{2,1,0:T(8,128)} custom-call(f32[44,128]{1,0:T(8,128)S(1)} %fusion.1.mine_ref, f32[44,128]{1,0:T(8,128)S(1)} %collective-permute-done.6.other_ref, s32[1,8]{1,0:T(1,128)S(4)} %get-tuple-element.37.offset_ref, s32[8,128]{1,0:T(8,128)S(1)} %get-tuple-element.38.rank_ref, f32[8,1024]{1,0:T(8,128)S(1)} %get-tuple-element.39.inner_ref, ...), custom_call_target="tpu_custom_call" | custom-call | tf_op jit(solution)/shard_map/invert/pallas_call | solution.py:348
  (6 shorter events, 0.1 us)
Async XLA Ops:
  2.6 1.5 %collective-permute-start.1 = (f32[184,128]{1,0:T(8,128)S(1)}, f32[184,128]{1,0:T(8,128)S(1)}, u32[]{:S(2)}, u32[]{:S(2)}) collective-permute-start(f32[184,128]{1,0:T(8,128)S(1)} %get-tuple-element.27), channel_id=1, source_target_pairs={{0,2},{2,0},{4,6},{6,4},{8,10},{10,8},{12,14},{14,12},{16,18},{18,... | collective-permute-start | bytes 282632 | tf_op jit(solution)/shard_map/ppermute | solution.py:378
  3.1 3.7 %collective-permute-start = (f32[184,128]{1,0:T(8,128)S(1)}, f32[184,128]{1,0:T(8,128)S(1)}, u32[]{:S(2)}, u32[]{:S(2)}) collective-permute-start(f32[184,128]{1,0:T(8,128)S(1)} %get-tuple-element.25), channel_id=1, source_target_pairs={{0,2},{2,0},{4,6},{6,4},{8,10},{10,8},{12,14},{14,12},{16,18},{18,... | collective-permute-start | bytes 282632 | tf_op jit(solution)/shard_map/ppermute | solution.py:378
  4.0 4.4 %collective-permute-start.3 = (f32[88,128]{1,0:T(8,128)S(1)}, f32[88,128]{1,0:T(8,128)S(1)}, u32[]{:S(2)}, u32[]{:S(2)}) collective-permute-start(f32[88,128]{1,0:T(8,128)S(1)} %slice_add_fusion), channel_id=1, source_target_pairs={{0,6},{2,8},{4,14},{6,0},{8,2},{10,12},{12,10},{14,4},{16,22},{18,... | collective-permute-start | bytes 135176 | tf_op jit(solution)/shard_map/ppermute | solution.py:378
  6.7 4.0 %collective-permute-start.2 = (f32[88,128]{1,0:T(8,128)S(1)}, f32[88,128]{1,0:T(8,128)S(1)}, u32[]{:S(2)}, u32[]{:S(2)}) collective-permute-start(f32[88,128]{1,0:T(8,128)S(1)} %slice_add_fusion.1), channel_id=1, source_target_pairs={{0,6},{2,8},{4,14},{6,0},{8,2},{10,12},{12,10},{14,4},{16,22},{18,... | collective-permute-start | bytes 135176 | tf_op jit(solution)/shard_map/ppermute | solution.py:378
  8.4 3.7 %collective-permute-start.5 = (f32[44,128]{1,0:T(8,128)S(1)}, f32[44,128]{1,0:T(8,128)S(1)}, u32[]{:S(2)}, u32[]{:S(2)}) collective-permute-start(f32[44,128]{1,0:T(8,128)S(1)} %slice_add_fusion.4), channel_id=1, source_target_pairs={{0,10},{2,4},{4,2},{6,12},{8,14},{10,0},{12,6},{14,8},{16,26},{18,... | collective-permute-start | bytes 67592 | tf_op jit(solution)/shard_map/ppermute | solution.py:378
  10.6 4.9 %collective-permute-start.4 = (f32[44,128]{1,0:T(8,128)S(1)}, f32[44,128]{1,0:T(8,128)S(1)}, u32[]{:S(2)}, u32[]{:S(2)}) collective-permute-start(f32[44,128]{1,0:T(8,128)S(1)} %slice_add_fusion.8), channel_id=1, source_target_pairs={{0,10},{2,4},{4,2},{6,12},{8,14},{10,0},{12,6},{14,8},{16,26},{18,... | collective-permute-start | bytes 67592 | tf_op jit(solution)/shard_map/ppermute | solution.py:378
  12.1 4.2 %collective-permute-start.6 = (f32[44,128]{1,0:T(8,128)S(1)}, f32[44,128]{1,0:T(8,128)S(1)}, u32[]{:S(2)}, u32[]{:S(2)}) collective-permute-start(f32[44,128]{1,0:T(8,128)S(1)} %fusion), channel_id=1, source_target_pairs={{0,18},{2,16},{4,22},{6,20},{8,26},{10,24},{12,30},{14,28},{16,2},... | collective-permute-start | bytes 67592 | tf_op jit(solution)/shard_map/ppermute | solution.py:388

commit v7 on v5

--- a/solution.py
+++ b/solution.py
@@ -54,7 +54,7 @@
 
 
 def project_kernel(
-    devices, owner_hbm, lengths_hbm, proj_hbm, tiles_hbm, keep_ref, send_ref,
+    devices, owner_hbm, lengths_hbm, proj_hbm, tiles_hbm, keep_ref, rest_ref, first_ref,
     owner_v, lengths_v, offset_v, offset_s, proj_buf, tile_buf, left_buf, sums_buf,
     small_sem, offset_sem, proj_sem, tile_sem,
 ):
@@ -83,8 +83,8 @@
         copy.start()
         tile_copies.append(copy)
 
-    keep_ref[...] = jnp.zeros_like(keep_ref)
-    send_ref[...] = jnp.zeros_like(send_ref)
+    for ref in (keep_ref, rest_ref, first_ref):
+        ref[...] = jnp.zeros_like(ref)
     for copy in small:
         copy.wait()
     down = lax.broadcasted_iota(jnp.int32, (rows, rows), 0)
@@ -138,17 +138,20 @@
     half = devices // 2
 
     def put(slot_index, offset, value):
-        def to(out_ref, base):
-            out_ref[pl.ds(base + offset, owned), :] = value
+        def to(out_ref, index):
+            out_ref[pl.ds(index * packed + offset, owned), :] = value
 
         if isinstance(slot_index, int):
-            if slot_index < half:
-                to(keep_ref, slot_index * packed)
+            if slot_index == devices - 1:
+                to(first_ref, 0)
+            elif slot_index < half:
+                to(keep_ref, slot_index)
             else:
-                to(send_ref, (slot_index - half) * packed)
+                to(rest_ref, slot_index - half)
         else:
-            pl.when(slot_index < half)(lambda: to(keep_ref, slot_index * packed))
-            pl.when(slot_index >= half)(lambda: to(send_ref, (slot_index - half) * packed))
+            pl.when(slot_index == devices - 1)(lambda: to(first_ref, 0))
+            pl.when(slot_index < half)(lambda: to(keep_ref, slot_index))
+            pl.when((slot_index >= half) & (slot_index < devices - 1))(lambda: to(rest_ref, slot_index - half))
 
     def pack(first, last):
         def one(slot_index):
@@ -179,8 +182,11 @@
     blocks, depth, samples = tiles.shape
     owned = rows // devices
     chunks = column_chunks(samples)
-    half_rows = devices // 2 * rows_per_owner(owned) + owned
-    shape = pltpu.VMEM((half_rows, LANE), jnp.float32)
+    half = devices // 2
+    shapes = [
+        pltpu.VMEM((-(-(slots * rows_per_owner(owned) + owned) // 8) * 8, LANE), jnp.float32)
+        for slots in (half, half - 1, 1)
+    ]
     inputs = [pltpu.with_memory_space_constraint(x, pltpu.HBM) for x in (owner, lengths, proj, tiles)]
 
     def kernel(*refs):
@@ -190,9 +196,9 @@
     hbm = pl.BlockSpec(memory_space=pltpu.HBM)
     return pl.pallas_call(
         kernel,
-        out_shape=(shape, shape),
+        out_shape=tuple(shapes),
         in_specs=[hbm] * 4,
-        out_specs=(vmem, vmem),
+        out_specs=(vmem,) * 3,
         scratch_shapes=[
             pltpu.VMEM(owner.shape, jnp.int32),
             pltpu.VMEM(lengths.shape, jnp.int32),
@@ -217,10 +223,15 @@
     )(*inputs)
 
 
+def chord_rows(packed_ref, offset, rank):
+    ordered = packed_ref[pl.ds(offset, rank.shape[0]), :]
+    return jnp.take_along_axis(ordered, rank, axis=0)
+
+
 def prepare_kernel(
-    devices, owner_hbm, lengths_hbm, offset_ref, rank_ref, inner_ref, outer_ref, coarse_ref, fine_ref,
-    owner_s, lengths_s, sem,
+    devices, owner_hbm, lengths_hbm, *refs
 ):
+    *term_refs, offset_ref, rank_ref, kept_ref, inner_ref, outer_ref, coarse_ref, fine_ref, owner_s, lengths_s, sum_buf, sem = refs
     owned, samples = inner_ref.shape
     blocks = samples // LANE
     distances = coarse_ref.shape[0]
@@ -253,11 +264,17 @@
         ahead = (lengths[index] > length) | ((lengths[index] == length) & (index < sub))
         rank = rank + jnp.where(ahead, 1, 0)
     rank_ref[...] = rank
+    packed = rows_per_owner(owned)
+    kept = term_refs[0][0:packed, :]
+    for ref in term_refs[1:]:
+        kept = kept + ref[0:packed, :]
+    sum_buf[0:packed, :] = kept
     for block in range(blocks):
         offset = jnp.int32(0)
         for index in range(owned):
             offset = offset + jnp.minimum((lengths[index] + (LANE - 1)) >> 7, block)
         offset_ref[0, block] = offset
+        kept_ref[:, block * LANE : (block + 1) * LANE] = chord_rows(sum_buf, offset, rank)
 
     long = length.astype(jnp.float32)
     for block in range(blocks):
@@ -269,7 +286,7 @@
         outer_ref[:, columns] = jnp.where(inside, 1.0 / (math.pi * weight), 0.0)
 
 
-def prepare(owner, lengths, devices, owned, samples):
+def prepare(owner, lengths, terms, devices, owned, samples):
     distances = 2 * (samples // COLS) - 1
     inputs = [pltpu.with_memory_space_constraint(x, pltpu.HBM) for x in (owner, lengths)]
     vmem = pl.BlockSpec(memory_space=pltpu.VMEM)
@@ -284,24 +301,26 @@
             pltpu.VMEM((owned, LANE), jnp.int32),
             pltpu.VMEM((owned, samples), jnp.float32),
             pltpu.VMEM((owned, samples), jnp.float32),
+            pltpu.VMEM((owned, samples), jnp.float32),
             pltpu.VMEM((distances, COLS, COLS), jnp.bfloat16),
             pltpu.VMEM((distances, COLS, COLS), jnp.bfloat16),
         ),
-        in_specs=[pl.BlockSpec(memory_space=pltpu.HBM)] * 2,
-        out_specs=(pl.BlockSpec(memory_space=pltpu.SMEM),) + (vmem,) * 5,
+        in_specs=[pl.BlockSpec(memory_space=pltpu.HBM)] * 2 + [vmem] * len(terms),
+        out_specs=(pl.BlockSpec(memory_space=pltpu.SMEM),) + (vmem,) * 6,
         scratch_shapes=[
             pltpu.SMEM(owner.shape, jnp.int32),
             pltpu.SMEM(lengths.shape, jnp.int32),
+            pltpu.VMEM((rows_per_owner(owned) + owned, LANE), jnp.float32),
             pltpu.SemaphoreType.DMA((2,)),
         ],
         compiler_params=pltpu.CompilerParams(vmem_limit_bytes=32 << 20),
         cost_estimate=pl.CostEstimate(flops=1 << 22, bytes_accessed=1 << 21, transcendentals=1 << 19),
         name="prepare",
-    )(*inputs)
+    )(*inputs, *terms)
 
 
 def invert_kernel(
-    mine_ref, other_ref, offset_ref, rank_ref, inner_ref, outer_ref, coarse_ref, fine_ref, out_ref, sum_buf
+    other_ref, offset_ref, rank_ref, kept_ref, inner_ref, outer_ref, coarse_ref, fine_ref, out_ref, sum_buf
 ):
     owned, samples = inner_ref.shape
     bins = samples // COLS
@@ -311,19 +330,18 @@
         coarse = value.astype(jnp.bfloat16)
         return coarse, (value - coarse.astype(jnp.float32)).astype(jnp.bfloat16)
 
-    packed = mine_ref.shape[0]
-    sum_buf[0:packed, :] = mine_ref[...] + other_ref[...]
+    sum_buf[0 : other_ref.shape[0], :] = other_ref[...]
     rank = rank_ref[...]
-
-    def chord_rows(block):
-        ordered = sum_buf[pl.ds(offset_ref[0, block], owned), :]
-        return jnp.take_along_axis(ordered, rank, axis=0)
-
     left = []
     for part in range(bins):
         sums = jnp.concatenate(
-            [chord_rows(block) for block in range(part * per_bin, (part + 1) * per_bin)], axis=1
+            [
+                chord_rows(sum_buf, offset_ref[0, block], rank)
+                for block in range(part * per_bin, (part + 1) * per_bin)
+            ],
+            axis=1,
         )
+        sums = sums + kept_ref[:, part * COLS : (part + 1) * COLS]
         weight = inner_ref[:, part * COLS : (part + 1) * COLS]
         scaled = jnp.where(weight > 0.0, weight * sums, 0.0)
         left.append(jnp.concatenate(halves(scaled), axis=0))
@@ -344,17 +362,41 @@
         out_ref[0, :, columns] = image[part] * outer_ref[:, columns]
 
 
-def invert(mine, other, prepared, owned, samples):
+def invert(other, prepared, owned, samples):
     vmem = pl.BlockSpec(memory_space=pltpu.VMEM)
     return pl.pallas_call(
         invert_kernel,
         out_shape=jax.ShapeDtypeStruct((1, owned, samples), jnp.float32),
-        in_specs=[vmem, vmem, pl.BlockSpec(memory_space=pltpu.SMEM)] + [vmem] * 5,
+        in_specs=[vmem, pl.BlockSpec(memory_space=pltpu.SMEM)] + [vmem] * 6,
         out_specs=vmem,
-        scratch_shapes=[pltpu.VMEM((mine.shape[0] + owned, LANE), jnp.float32)],
+        scratch_shapes=[pltpu.VMEM((other.shape[0] + owned, LANE), jnp.float32)],
         compiler_params=pltpu.CompilerParams(vmem_limit_bytes=32 << 20),
         name="invert",
-    )(mine, other, *prepared)
+    )(other, *prepared)
+
+
+def add_kernel(start, *refs):
+    *term_refs, out_ref = refs
+    rows = pl.ds(start, out_ref.shape[0])
+    value = term_refs[0][rows, :]
+    for ref in term_refs[1:]:
+        value = value + ref[rows, :]
+    out_ref[...] = value
+
+
+def add_rows(terms, start, count):
+    vmem = pl.BlockSpec(memory_space=pltpu.VMEM)
+    return pl.pallas_call(
+        lambda *refs: add_kernel(start, *refs),
+        out_shape=pltpu.VMEM((count, LANE), jnp.float32),
+        in_specs=[vmem] * len(terms),
+        out_specs=vmem,
+        compiler_params=pltpu.CompilerParams(vmem_limit_bytes=16 << 20),
+        cost_estimate=pl.CostEstimate(
+            flops=count * LANE * (len(terms) - 1), bytes_accessed=4 * count * LANE * (len(terms) + 1), transcendentals=0
+        ),
+        name="add_rows",
+    )(*terms)
 
 
 def per_device(proj, tiles, owner, lengths):
@@ -363,17 +405,27 @@
     samples = tiles.shape[2]
     owned = rows // devices
     packed = rows_per_owner(owned)
-    keep, send = project(proj, tiles, owner, lengths, devices)
-    prepared = prepare(owner, lengths, devices, owned, samples)
+    keep, rest, first = project(proj, tiles, owner, lengths, devices)
+    *steps, last_step = exchange_pairs(devices)
+
+    def total(terms, place, count=1):
+        value, *others = [array[place * packed : (place + count) * packed] for array in terms]
+        for other in others:
+            value = value + other
+        return value
+
     held = devices // 2
-    steps = exchange_pairs(devices)
-    for pairs in steps[:-1]:
-        other = lax.ppermute(send, "view", pairs)
+    terms = [keep]
+    for pairs in steps:
+        got_first, got_rest = lax.ppermute(first, "view", pairs), lax.ppermute(rest, "view", pairs)
+        first = total(terms, held - 1) + got_first[:packed]
+        terms = terms + [got_rest]
         held //= 2
-        middle = held * packed
-        keep, send = keep[:middle] + other[:middle], keep[middle : 2 * middle] + other[middle : 2 * middle]
-    other = lax.ppermute(send, "view", steps[-1])
-    return invert(keep, other, prepared, owned, samples)
+        if held > 1:
+            rest = add_rows(terms, held * packed, (held - 1) * packed)
+    other = lax.ppermute(first, "view", last_step)
+    prepared = prepare(owner, lengths, terms, devices, owned, samples)
+    return invert(other, prepared, owned, samples)
 
 
 def solution(mesh):

time: 18.2 us -> 17.3 us (0.951)
  waiting for transfers between devices: 5.69 us -> 2.77 us
  starting transfers between devices: 7.9 us -> 9.94 us
    ppermute x4 -> x7, waiting for transfers between devices: 5.69 us -> 2.77 us  [the longest x3 1.69 us: per_device(): lax.ppermute(first, 'view', pairs)]
    ppermute x4 -> x7, starting transfers between devices: 7.9 us -> 9.94 us  [the longest x3 5.31 us: per_device(): lax.ppermute(first, 'view', pairs)]
    pallas_call x1 -> x3, Pallas kernels: 2.56 us -> 2.57 us  [the longest x1 2.55 us: project(): pl.pallas_call(kernel, out_shape=tuple(shapes), in_specs=[hbm] * 4, out_s...]
  transfers between devices with their start and end apart: 4 -> 7, of which waited for: 4 -> 4; matrix products, arithmetic and copies ran while one was open for 0% -> 0% of each run, Pallas kernels for 5% -> 5%
where the time goes in v7:
time: 17.3 us; the launch traced here: 17.2 us
  starting transfers between devices  9.94 us (57%)
  Pallas kernels  4.41 us (25%)
  waiting for transfers between devices  2.77 us (16%)
    ppermute x3, starting transfers between devices, per_device(): lax.ppermute(first, 'view', pairs)  5.31 us
    pallas_call x1, Pallas kernels, project(): pl.pallas_call(kernel, out_shape=tuple(shapes), in_specs=[hbm] * 4, out_s...  2.55 us
    ppermute x1, starting transfers between devices, per_device(): other = lax.ppermute(first, 'view', last_step)  2.43 us
    ppermute x3, starting transfers between devices, per_device(): lax.ppermute(rest, 'view', pairs)  2.2 us
    ppermute x3, waiting for transfers between devices, per_device(): lax.ppermute(first, 'view', pairs)  1.69 us
    pallas_call x1, Pallas kernels, invert(): pl.pallas_call(invert_kernel, out_shape=jax.ShapeDtypeStruct((1, owned, s...  1.01 us
    ppermute x1, waiting for transfers between devices, per_device(): other = lax.ppermute(first, 'view', last_step)  0.95 us
    pallas_call x1, Pallas kernels, prepare(): pl.pallas_call(kernel, out_shape=(pltpu.SMEM((1, samples // LANE), jnp.in...  0.82 us
  transfers between devices with their start and end apart: 7, of which 4 were waited for; matrix products, arithmetic and copies ran while one was open for 0% of the time, Pallas kernels for 5%

profile of v7, /device:TPU:0, one launch (start us, length us, event | category | flops | bytes accessed | tf_op | source)
XLA Modules:
  0.0 17.2 jit_solution(13775227857181223196)
XLA Ops:
  0.0 2.6 %project.1 = (f32[360,128]{1,0:T(8,128)S(1)}, f32[320,128]{1,0:T(8,128)S(1)}, f32[56,128]{1,0:T(8,128)S(1)}) custom-call(s32[2,128]{1,0:T(2,128)} %refs_0_.3, s32[2,128]{1,0:T(2,128)} %refs_1_.3, bf16[12,128,128]{2,1,0:T(8,128)(2,1)} %refs_2_.1, bf16[6,256,1024]{2,1,0:T(8,128)(2,1)} %refs_3_.1), custom_call_target="tpu_custom_call" | custom-call | flops 402653184 | bytes 3538944 | tf_op jit(solution)/shard_map/project/pallas_call | solution.py:197
  2.6 0.5 %collective-permute-start.2 = (f32[56,128]{1,0:T(8,128)S(1)}, f32[56,128]{1,0:T(8,128)S(1)}, u32[]{:S(2)}, u32[]{:S(2)}) collective-permute-start(f32[56,128]{1,0:T(8,128)S(1)} %get-tuple-element.17), channel_id=1, source_target_pairs={{0,2},{2,0},{4,6},{6,4},{8,10},{10,8},{12,14},{14,12},{16,18},{18,... | collective-permute-start | bytes 86024 | tf_op jit(solution)/shard_map/ppermute | solution.py:420
  3.1 0.1 collective-permute-start
  3.2 0.8 %collective-permute-done.2 = f32[56,128]{1,0:T(8,128)S(1)} collective-permute-done((f32[56,128]{1,0:T(8,128)S(1)}, f32[56,128]{1,0:T(8,128)S(1)}, u32[]{:S(2)}, u32[]{:S(2)}) %collective-permute-start.2) | collective-permute-done | bytes 28704 | tf_op jit(solution)/shard_map/ppermute | solution.py:420
  3.9 2.6 %collective-permute-start.3 = (f32[44,128]{1,0:T(8,128)S(1)}, f32[44,128]{1,0:T(8,128)S(1)}, u32[]{:S(2)}, u32[]{:S(2)}) collective-permute-start(f32[44,128]{1,0:T(8,128)S(1)} %slice_add_fusion), channel_id=1, source_target_pairs={{0,6},{2,8},{4,14},{6,0},{8,2},{10,12},{12,10},{14,4},{16,22},{18,... | collective-permute-start | bytes 67592 | tf_op jit(solution)/shard_map/ppermute | solution.py:420
  6.6 0.0 collective-permute-done.refs_1_.refs_3_
  6.6 0.6 %collective-permute-start.1 = (f32[132,128]{1,0:T(8,128)S(1)}, f32[132,128]{1,0:T(8,128)S(1)}, u32[]{:S(2)}, u32[]{:S(2)}) collective-permute-start(f32[132,128]{1,0:T(8,128)S(1)} %add_rows.2), channel_id=1, source_target_pairs={{0,6},{2,8},{4,14},{6,0},{8,2},{10,12},{12,10},{14,4},{16,22},{18,... | collective-permute-start | bytes 202760 | tf_op jit(solution)/shard_map/ppermute | solution.py:420
  7.2 0.9 %collective-permute-done.3 = f32[44,128]{1,0:T(8,128)S(1)} collective-permute-done((f32[44,128]{1,0:T(8,128)S(1)}, f32[44,128]{1,0:T(8,128)S(1)}, u32[]{:S(2)}, u32[]{:S(2)}) %collective-permute-start.3) | collective-permute-done | bytes 22560 | tf_op jit(solution)/shard_map/ppermute | solution.py:420
  8.1 2.2 %collective-permute-start.4 = (f32[44,128]{1,0:T(8,128)S(1)}, f32[44,128]{1,0:T(8,128)S(1)}, u32[]{:S(2)}, u32[]{:S(2)}) collective-permute-start(f32[44,128]{1,0:T(8,128)S(1)} %fusion), channel_id=1, source_target_pairs={{0,10},{2,4},{4,2},{6,12},{8,14},{10,0},{12,6},{14,8},{16,26},{18,... | collective-permute-start | bytes 67592 | tf_op jit(solution)/shard_map/ppermute | solution.py:420
  10.3 0.1 collective-permute-done.1.refs_2_.refs_4_
  10.4 1.5 %collective-permute-start.6 = (f32[44,128]{1,0:T(8,128)S(1)}, f32[44,128]{1,0:T(8,128)S(1)}, u32[]{:S(2)}, u32[]{:S(2)}) collective-permute-start(f32[44,128]{1,0:T(8,128)S(1)} %add_rows.3), channel_id=1, source_target_pairs={{0,10},{2,4},{4,2},{6,12},{8,14},{10,0},{12,6},{14,8},{16,26},{18,... | collective-permute-start | bytes 67592 | tf_op jit(solution)/shard_map/ppermute | solution.py:420
  11.9 0.0 collective-permute-done.4
  11.9 2.4 %collective-permute-start.5 = (f32[44,128]{1,0:T(8,128)S(1)}, f32[44,128]{1,0:T(8,128)S(1)}, u32[]{:S(2)}, u32[]{:S(2)}) collective-permute-start(f32[44,128]{1,0:T(8,128)S(1)} %fusion.1), channel_id=1, source_target_pairs={{0,18},{2,16},{4,22},{6,20},{8,26},{10,24},{12,30},{14,28},{16,2},... | collective-permute-start | bytes 67592 | tf_op jit(solution)/shard_map/ppermute | solution.py:426
  14.4 0.0 collective-permute-done.6.refs_5_
  14.4 0.8 %prepare.1 = (s32[1,8]{1,0:T(1,128)S(4)}, s32[8,128]{1,0:T(8,128)S(1)}, f32[8,1024]{1,0:T(8,128)S(1)}, f32[8,1024]{1,0:T(8,128)S(1)}, f32[8,1024]{1,0:T(8,128)S(...) custom-call(s32[2,128]{1,0:T(2,128)} %refs_0_.3, s32[2,128]{1,0:T(2,128)} %refs_1_.3, ...), custom_call_target="tpu_custom_call" | custom-call | flops 4194304 | bytes 2097152 | tf_op jit(solution)/shard_map/prepare/pallas_call | solution.py:297
  15.2 0.9 %collective-permute-done.5.other_ref = f32[44,128]{1,0:T(8,128)S(1)} collective-permute-done((f32[44,128]{1,0:T(8,128)S(1)}, f32[44,128]{1,0:T(8,128)S(1)}, u32[]{:S(2)}, u32[]{:S(2)}) %collective-permute-start.5) | collective-permute-done | bytes 22560 | tf_op jit(solution)/shard_map/ppermute | solution.py:426
  16.2 1.0 %invert.1 = f32[1,8,1024]{2,1,0:T(8,128)} custom-call(f32[44,128]{1,0:T(8,128)S(1)} %collective-permute-done.5.other_ref, s32[1,8]{1,0:T(1,128)S(4)} %get-tuple-element.18.offset_ref, s32[8,128]{1,0:T(8,128)S(1)} %get-tuple-element.19.rank_ref, f32[8,1024]{1,0:T(8,128)S(1)} %get-tuple-element.20.kept_ref, f32[8,1024]{1,0:T(8,128)S(1)} %get-tuple-element.21.inner_ref, ...), custom_call_target="tpu_custom_call" | custom-call | tf_op jit(solution)/shard_map/invert/pallas_call | solution.py:367
  (5 shorter events, 0.0 us)
Async XLA Ops:
  2.6 1.4 %collective-permute-start.2 = (f32[56,128]{1,0:T(8,128)S(1)}, f32[56,128]{1,0:T(8,128)S(1)}, u32[]{:S(2)}, u32[]{:S(2)}) collective-permute-start(f32[56,128]{1,0:T(8,128)S(1)} %get-tuple-element.17), channel_id=1, source_target_pairs={{0,2},{2,0},{4,6},{6,4},{8,10},{10,8},{12,14},{14,12},{16,18},{18,... | collective-permute-start | bytes 86024 | tf_op jit(solution)/shard_map/ppermute | solution.py:420
  3.1 3.5 %collective-permute-start = (f32[320,128]{1,0:T(8,128)S(1)}, f32[320,128]{1,0:T(8,128)S(1)}, u32[]{:S(2)}, u32[]{:S(2)}) collective-permute-start(f32[320,128]{1,0:T(8,128)S(1)} %get-tuple-element.16), channel_id=1, source_target_pairs={{0,2},{2,0},{4,6},{6,4},{8,10},{10,8},{12,14},{14,12},{16,18},{18,... | collective-permute-start | bytes 491528 | tf_op jit(solution)/shard_map/ppermute | solution.py:420
  3.9 4.2 %collective-permute-start.3 = (f32[44,128]{1,0:T(8,128)S(1)}, f32[44,128]{1,0:T(8,128)S(1)}, u32[]{:S(2)}, u32[]{:S(2)}) collective-permute-start(f32[44,128]{1,0:T(8,128)S(1)} %slice_add_fusion), channel_id=1, source_target_pairs={{0,6},{2,8},{4,14},{6,0},{8,2},{10,12},{12,10},{14,4},{16,22},{18,... | collective-permute-start | bytes 67592 | tf_op jit(solution)/shard_map/ppermute | solution.py:420
  6.6 3.8 %collective-permute-start.1 = (f32[132,128]{1,0:T(8,128)S(1)}, f32[132,128]{1,0:T(8,128)S(1)}, u32[]{:S(2)}, u32[]{:S(2)}) collective-permute-start(f32[132,128]{1,0:T(8,128)S(1)} %add_rows.2), channel_id=1, source_target_pairs={{0,6},{2,8},{4,14},{6,0},{8,2},{10,12},{12,10},{14,4},{16,22},{18,... | collective-permute-start | bytes 202760 | tf_op jit(solution)/shard_map/ppermute | solution.py:420
  8.1 3.8 %collective-permute-start.4 = (f32[44,128]{1,0:T(8,128)S(1)}, f32[44,128]{1,0:T(8,128)S(1)}, u32[]{:S(2)}, u32[]{:S(2)}) collective-permute-start(f32[44,128]{1,0:T(8,128)S(1)} %fusion), channel_id=1, source_target_pairs={{0,10},{2,4},{4,2},{6,12},{8,14},{10,0},{12,6},{14,8},{16,26},{18,... | collective-permute-start | bytes 67592 | tf_op jit(solution)/shard_map/ppermute | solution.py:420
  10.4 4.0 %collective-permute-start.6 = (f32[44,128]{1,0:T(8,128)S(1)}, f32[44,128]{1,0:T(8,128)S(1)}, u32[]{:S(2)}, u32[]{:S(2)}) collective-permute-start(f32[44,128]{1,0:T(8,128)S(1)} %add_rows.3), channel_id=1, source_target_pairs={{0,10},{2,4},{4,2},{6,12},{8,14},{10,0},{12,6},{14,8},{16,26},{18,... | collective-permute-start | bytes 67592 | tf_op jit(solution)/shard_map/ppermute | solution.py:420
  11.9 4.2 %collective-permute-start.5 = (f32[44,128]{1,0:T(8,128)S(1)}, f32[44,128]{1,0:T(8,128)S(1)}, u32[]{:S(2)}, u32[]{:S(2)}) collective-permute-start(f32[44,128]{1,0:T(8,128)S(1)} %fusion.1), channel_id=1, source_target_pairs={{0,18},{2,16},{4,22},{6,20},{8,26},{10,24},{12,30},{14,28},{16,2},... | collective-permute-start | bytes 67592 | tf_op jit(solution)/shard_map/ppermute | solution.py:426

commit v8 on v7

--- a/solution.py
+++ b/solution.py
@@ -375,19 +375,20 @@
     )(other, *prepared)
 
 
-def add_kernel(start, *refs):
+def add_kernel(starts, *refs):
     *term_refs, out_ref = refs
-    rows = pl.ds(start, out_ref.shape[0])
-    value = term_refs[0][rows, :]
-    for ref in term_refs[1:]:
-        value = value + ref[rows, :]
-    out_ref[...] = value
-
-
-def add_rows(terms, start, count):
+    count = out_ref.shape[0]
+    values = [ref[pl.ds(start, count), :] for ref, start in zip(term_refs, starts)]
+    total = values[0]
+    for value in values[1:]:
+        total = total + value
+    out_ref[...] = total
+
+
+def add_rows(terms, starts, count):
     vmem = pl.BlockSpec(memory_space=pltpu.VMEM)
     return pl.pallas_call(
-        lambda *refs: add_kernel(start, *refs),
+        lambda *refs: add_kernel(starts, *refs),
         out_shape=pltpu.VMEM((count, LANE), jnp.float32),
         in_specs=[vmem] * len(terms),
         out_specs=vmem,
@@ -406,25 +407,37 @@
     owned = rows // devices
     packed = rows_per_owner(owned)
     keep, rest, first = project(proj, tiles, owner, lengths, devices)
-    *steps, last_step = exchange_pairs(devices)
-
-    def total(terms, place, count=1):
-        value, *others = [array[place * packed : (place + count) * packed] for array in terms]
+
+    def total(terms, place):
+        value, *others = [array[(place - base) * packed : (place - base + 1) * packed] for array, base in terms]
         for other in others:
             value = value + other
         return value
 
+    def apart(terms, place, count):
+        return add_rows([array for array, _ in terms], [(place - base) * packed for _, base in terms], count * packed)
+
+    def give(value):
+        return lax.ppermute(value, "view", pairs)
+
     held = devices // 2
-    terms = [keep]
+    pairs, *steps, last_pairs = exchange_pairs(devices)
+    got_first, got_rest = give(first), give(rest)
+    first = total([(keep, 0)], held - 1) + got_first[:packed]
+    terms = [(keep, 0), (got_rest, 0)]
+    sent_next = terms
     for pairs in steps:
-        got_first, got_rest = lax.ppermute(first, "view", pairs), lax.ppermute(rest, "view", pairs)
-        first = total(terms, held - 1) + got_first[:packed]
-        terms = terms + [got_rest]
         held //= 2
-        if held > 1:
-            rest = add_rows(terms, held * packed, (held - 1) * packed)
-    other = lax.ppermute(first, "view", last_step)
-    prepared = prepare(owner, lengths, terms, devices, owned, samples)
+        got_first, got_second = give(first), None
+        if held > 2:
+            got_second = give(apart(sent_next, held + held // 2, held // 2 - 1))
+        got_third = give(apart(sent_next, held, held // 2))
+        first = total(terms, held - 1) + got_first
+        sent_next = terms + [(got_second, held // 2)]
+        terms = terms + [(got_third, 0)]
+    pairs = last_pairs
+    other = give(first)
+    prepared = prepare(owner, lengths, [array for array, _ in terms], devices, owned, samples)
     return invert(other, prepared, owned, samples)
 
 

time: 17.3 us -> 17.2 us (level)
  waiting for transfers between devices: 2.77 us -> 1.6 us
  starting transfers between devices: 9.94 us -> 11 us
    ppermute x7 -> x8, waiting for transfers between devices: 2.77 us -> 1.6 us  [give(): return lax.ppermute(value, 'view', pairs)]
    ppermute x7 -> x8, starting transfers between devices: 9.94 us -> 11 us  [give(): return lax.ppermute(value, 'view', pairs)]
  transfers between devices with their start and end apart: 7 -> 8, of which waited for: 4 -> 2; matrix products, arithmetic and copies ran while one was open for 0% -> 0% of each run, Pallas kernels for 5% -> 5%
where the time goes in v8:
time: 17.2 us; the launch traced here: 17 us
  starting transfers between devices  11 us (64%)
  Pallas kernels  4.42 us (26%)
  waiting for transfers between devices  1.6 us (9%)
    ppermute x8, starting transfers between devices, give(): return lax.ppermute(value, 'view', pairs)  11 us
    pallas_call x1, Pallas kernels, project(): pl.pallas_call(kernel, out_shape=tuple(shapes), in_specs=[hbm] * 4, out_s...  2.55 us
    ppermute x8, waiting for transfers between devices, give(): return lax.ppermute(value, 'view', pairs)  1.6 us
    pallas_call x1, Pallas kernels, invert(): pl.pallas_call(invert_kernel, out_shape=jax.ShapeDtypeStruct((1, owned, s...  1.02 us
    pallas_call x1, Pallas kernels, prepare(): pl.pallas_call(kernel, out_shape=(pltpu.SMEM((1, samples // LANE), jnp.in...  0.82 us
  transfers between devices with their start and end apart: 8, of which 2 were waited for; matrix products, arithmetic and copies ran while one was open for 0% of the time, Pallas kernels for 5%

profile of v8, /device:TPU:0, one launch (start us, length us, event | category | flops | bytes accessed | tf_op | source)
XLA Modules:
  0.0 17.0 jit_solution(16077831910031850317)
XLA Ops:
  0.0 2.6 %project.1 = (f32[360,128]{1,0:T(8,128)S(1)}, f32[320,128]{1,0:T(8,128)S(1)}, f32[56,128]{1,0:T(8,128)S(1)}) custom-call(s32[2,128]{1,0:T(2,128)} %refs_0_.3, s32[2,128]{1,0:T(2,128)} %refs_1_.3, bf16[12,128,128]{2,1,0:T(8,128)(2,1)} %refs_2_.1, bf16[6,256,1024]{2,1,0:T(8,128)(2,1)} %refs_3_.1), custom_call_target="tpu_custom_call" | custom-call | flops 402653184 | bytes 3538944 | tf_op jit(solution)/shard_map/project/pallas_call | solution.py:197
  2.6 0.5 %collective-permute-start.2 = (f32[56,128]{1,0:T(8,128)S(1)}, f32[56,128]{1,0:T(8,128)S(1)}, u32[]{:S(2)}, u32[]{:S(2)}) collective-permute-start(f32[56,128]{1,0:T(8,128)S(1)} %get-tuple-element.17), channel_id=1, source_target_pairs={{0,2},{2,0},{4,6},{6,4},{8,10},{10,8},{12,14},{14,12},{16,18},{18,... | collective-permute-start | bytes 86024 | tf_op jit(solution)/shard_map/ppermute | solution.py:421
  3.1 0.1 collective-permute-start
  3.2 0.8 %collective-permute-done.2 = f32[56,128]{1,0:T(8,128)S(1)} collective-permute-done((f32[56,128]{1,0:T(8,128)S(1)}, f32[56,128]{1,0:T(8,128)S(1)}, u32[]{:S(2)}, u32[]{:S(2)}) %collective-permute-start.2) | collective-permute-done | bytes 28704 | tf_op jit(solution)/shard_map/ppermute | solution.py:421
  3.9 2.6 %collective-permute-start.3 = (f32[44,128]{1,0:T(8,128)S(1)}, f32[44,128]{1,0:T(8,128)S(1)}, u32[]{:S(2)}, u32[]{:S(2)}) collective-permute-start(f32[44,128]{1,0:T(8,128)S(1)} %slice_add_fusion), channel_id=1, source_target_pairs={{0,6},{2,8},{4,14},{6,0},{8,2},{10,12},{12,10},{14,4},{16,22},{18,... | collective-permute-start | bytes 67592 | tf_op jit(solution)/shard_map/ppermute | solution.py:421
  6.6 0.0 collective-permute-done.refs_1_.refs_3_
  6.6 0.5 %collective-permute-start.6 = (f32[44,128]{1,0:T(8,128)S(1)}, f32[44,128]{1,0:T(8,128)S(1)}, u32[]{:S(2)}, u32[]{:S(2)}) collective-permute-start(f32[44,128]{1,0:T(8,128)S(1)} %add_rows.4), channel_id=1, source_target_pairs={{0,6},{2,8},{4,14},{6,0},{8,2},{10,12},{12,10},{14,4},{16,22},{18,... | collective-permute-start | bytes 67592 | tf_op jit(solution)/shard_map/ppermute | solution.py:421
  7.1 1.3 %collective-permute-start.1 = (f32[88,128]{1,0:T(8,128)S(1)}, f32[88,128]{1,0:T(8,128)S(1)}, u32[]{:S(2)}, u32[]{:S(2)}) collective-permute-start(f32[88,128]{1,0:T(8,128)S(1)} %add_rows.3), channel_id=1, source_target_pairs={{0,6},{2,8},{4,14},{6,0},{8,2},{10,12},{12,10},{14,4},{16,22},{18,... | collective-permute-start | bytes 135176 | tf_op jit(solution)/shard_map/ppermute | solution.py:421
  8.4 0.0 collective-permute-done.3
  8.4 1.8 %collective-permute-start.4 = (f32[44,128]{1,0:T(8,128)S(1)}, f32[44,128]{1,0:T(8,128)S(1)}, u32[]{:S(2)}, u32[]{:S(2)}) collective-permute-start(f32[44,128]{1,0:T(8,128)S(1)} %fusion), channel_id=1, source_target_pairs={{0,10},{2,4},{4,2},{6,12},{8,14},{10,0},{12,6},{14,8},{16,26},{18,... | collective-permute-start | bytes 67592 | tf_op jit(solution)/shard_map/ppermute | solution.py:421
  10.3 0.0 collective-permute-done.6.refs_2_
  10.3 1.5 %collective-permute-start.7 = (f32[44,128]{1,0:T(8,128)S(1)}, f32[44,128]{1,0:T(8,128)S(1)}, u32[]{:S(2)}, u32[]{:S(2)}) collective-permute-start(f32[44,128]{1,0:T(8,128)S(1)} %add_rows.5), channel_id=1, source_target_pairs={{0,10},{2,4},{4,2},{6,12},{8,14},{10,0},{12,6},{14,8},{16,26},{18,... | collective-permute-start | bytes 67592 | tf_op jit(solution)/shard_map/ppermute | solution.py:421
  11.7 0.0 collective-permute-done.4
  11.8 0.0 collective-permute-done.1.refs_4_
  11.8 2.6 %collective-permute-start.5 = (f32[44,128]{1,0:T(8,128)S(1)}, f32[44,128]{1,0:T(8,128)S(1)}, u32[]{:S(2)}, u32[]{:S(2)}) collective-permute-start(f32[44,128]{1,0:T(8,128)S(1)} %fusion.1), channel_id=1, source_target_pairs={{0,18},{2,16},{4,22},{6,20},{8,26},{10,24},{12,30},{14,28},{16,2},... | collective-permute-start | bytes 67592 | tf_op jit(solution)/shard_map/ppermute | solution.py:421
  14.4 0.0 collective-permute-done.7.refs_5_
  14.4 0.8 %prepare.1 = (s32[1,8]{1,0:T(1,128)S(4)}, s32[8,128]{1,0:T(8,128)S(1)}, f32[8,1024]{1,0:T(8,128)S(1)}, f32[8,1024]{1,0:T(8,128)S(1)}, f32[8,1024]{1,0:T(8,128)S(...) custom-call(s32[2,128]{1,0:T(2,128)} %refs_0_.3, s32[2,128]{1,0:T(2,128)} %refs_1_.3, ...), custom_call_target="tpu_custom_call" | custom-call | flops 4194304 | bytes 2097152 | tf_op jit(solution)/shard_map/prepare/pallas_call | solution.py:297
  15.3 0.8 %collective-permute-done.5.other_ref = f32[44,128]{1,0:T(8,128)S(1)} collective-permute-done((f32[44,128]{1,0:T(8,128)S(1)}, f32[44,128]{1,0:T(8,128)S(1)}, u32[]{:S(2)}, u32[]{:S(2)}) %collective-permute-start.5) | collective-permute-done | bytes 22560 | tf_op jit(solution)/shard_map/ppermute | solution.py:421
  16.0 1.0 %invert.1 = f32[1,8,1024]{2,1,0:T(8,128)} custom-call(f32[44,128]{1,0:T(8,128)S(1)} %collective-permute-done.5.other_ref, s32[1,8]{1,0:T(1,128)S(4)} %get-tuple-element.18.offset_ref, s32[8,128]{1,0:T(8,128)S(1)} %get-tuple-element.19.rank_ref, f32[8,1024]{1,0:T(8,128)S(1)} %get-tuple-element.20.kept_ref, f32[8,1024]{1,0:T(8,128)S(1)} %get-tuple-element.21.inner_ref, ...), custom_call_target="tpu_custom_call" | custom-call | tf_op jit(solution)/shard_map/invert/pallas_call | solution.py:367
  (6 shorter events, 0.0 us)
Async XLA Ops:
  2.6 1.4 %collective-permute-start.2 = (f32[56,128]{1,0:T(8,128)S(1)}, f32[56,128]{1,0:T(8,128)S(1)}, u32[]{:S(2)}, u32[]{:S(2)}) collective-permute-start(f32[56,128]{1,0:T(8,128)S(1)} %get-tuple-element.17), channel_id=1, source_target_pairs={{0,2},{2,0},{4,6},{6,4},{8,10},{10,8},{12,14},{14,12},{16,18},{18,... | collective-permute-start | bytes 86024 | tf_op jit(solution)/shard_map/ppermute | solution.py:421
  3.1 3.5 %collective-permute-start = (f32[320,128]{1,0:T(8,128)S(1)}, f32[320,128]{1,0:T(8,128)S(1)}, u32[]{:S(2)}, u32[]{:S(2)}) collective-permute-start(f32[320,128]{1,0:T(8,128)S(1)} %get-tuple-element.16), channel_id=1, source_target_pairs={{0,2},{2,0},{4,6},{6,4},{8,10},{10,8},{12,14},{14,12},{16,18},{18,... | collective-permute-start | bytes 491528 | tf_op jit(solution)/shard_map/ppermute | solution.py:421
  3.9 4.5 %collective-permute-start.3 = (f32[44,128]{1,0:T(8,128)S(1)}, f32[44,128]{1,0:T(8,128)S(1)}, u32[]{:S(2)}, u32[]{:S(2)}) collective-permute-start(f32[44,128]{1,0:T(8,128)S(1)} %slice_add_fusion), channel_id=1, source_target_pairs={{0,6},{2,8},{4,14},{6,0},{8,2},{10,12},{12,10},{14,4},{16,22},{18,... | collective-permute-start | bytes 67592 | tf_op jit(solution)/shard_map/ppermute | solution.py:421
  6.6 3.7 %collective-permute-start.6 = (f32[44,128]{1,0:T(8,128)S(1)}, f32[44,128]{1,0:T(8,128)S(1)}, u32[]{:S(2)}, u32[]{:S(2)}) collective-permute-start(f32[44,128]{1,0:T(8,128)S(1)} %add_rows.4), channel_id=1, source_target_pairs={{0,6},{2,8},{4,14},{6,0},{8,2},{10,12},{12,10},{14,4},{16,22},{18,... | collective-permute-start | bytes 67592 | tf_op jit(solution)/shard_map/ppermute | solution.py:421
  7.1 4.7 %collective-permute-start.1 = (f32[88,128]{1,0:T(8,128)S(1)}, f32[88,128]{1,0:T(8,128)S(1)}, u32[]{:S(2)}, u32[]{:S(2)}) collective-permute-start(f32[88,128]{1,0:T(8,128)S(1)} %add_rows.3), channel_id=1, source_target_pairs={{0,6},{2,8},{4,14},{6,0},{8,2},{10,12},{12,10},{14,4},{16,22},{18,... | collective-permute-start | bytes 135176 | tf_op jit(solution)/shard_map/ppermute | solution.py:421
  8.4 3.4 %collective-permute-start.4 = (f32[44,128]{1,0:T(8,128)S(1)}, f32[44,128]{1,0:T(8,128)S(1)}, u32[]{:S(2)}, u32[]{:S(2)}) collective-permute-start(f32[44,128]{1,0:T(8,128)S(1)} %fusion), channel_id=1, source_target_pairs={{0,10},{2,4},{4,2},{6,12},{8,14},{10,0},{12,6},{14,8},{16,26},{18,... | collective-permute-start | bytes 67592 | tf_op jit(solution)/shard_map/ppermute | solution.py:421
  10.3 4.2 %collective-permute-start.7 = (f32[44,128]{1,0:T(8,128)S(1)}, f32[44,128]{1,0:T(8,128)S(1)}, u32[]{:S(2)}, u32[]{:S(2)}) collective-permute-start(f32[44,128]{1,0:T(8,128)S(1)} %add_rows.5), channel_id=1, source_target_pairs={{0,10},{2,4},{4,2},{6,12},{8,14},{10,0},{12,6},{14,8},{16,26},{18,... | collective-permute-start | bytes 67592 | tf_op jit(solution)/shard_map/ppermute | solution.py:421
  11.8 4.2 %collective-permute-start.5 = (f32[44,128]{1,0:T(8,128)S(1)}, f32[44,128]{1,0:T(8,128)S(1)}, u32[]{:S(2)}, u32[]{:S(2)}) collective-permute-start(f32[44,128]{1,0:T(8,128)S(1)} %fusion.1), channel_id=1, source_target_pairs={{0,18},{2,16},{4,22},{6,20},{8,26},{10,24},{12,30},{14,28},{16,2},... | collective-permute-start | bytes 67592 | tf_op jit(solution)/shard_map/ppermute | solution.py:421

commit v9 on v8

--- a/solution.py
+++ b/solution.py
@@ -49,8 +49,9 @@
     return -(-rows // 4) * 4
 
 
-def column_chunks(samples):
-    return [(0, samples // 2), (samples // 2, samples // 2)]
+def tile_pieces(blocks, samples):
+    half, head = samples // 2, blocks * 2 // 3
+    return [(0, half, 0, blocks), (half, half, 0, head), (half, half, head, blocks - head)]
 
 
 def project_kernel(
@@ -60,7 +61,8 @@
 ):
     views, rows, footprint = proj_buf.shape
     samples = tile_buf.shape[2]
-    chunks = column_chunks(samples)
+    pieces = tile_pieces(tile_buf.shape[0], samples)
+    depth = tile_buf.shape[1]
     owned = rows // devices
     group = lax.axis_index("chord")
     me = lax.axis_index("view")
@@ -75,11 +77,9 @@
     proj_copy = pltpu.make_async_copy(proj_hbm, proj_buf, proj_sem)
     proj_copy.start()
     tile_copies = []
-    for index, (start, width) in enumerate(chunks):
-        columns = pl.ds(start, width)
-        copy = pltpu.make_async_copy(
-            tiles_hbm.at[:, :, columns], tile_buf.at[:, :, columns], tile_sem.at[index]
-        )
+    for index, (start, width, first, count) in enumerate(pieces):
+        place = pl.ds(first, count), slice(None), pl.ds(start, width)
+        copy = pltpu.make_async_copy(tiles_hbm.at[place], tile_buf.at[place], tile_sem.at[index])
         copy.start()
         tile_copies.append(copy)
 
@@ -161,19 +161,19 @@
 
         each_slot(one)
 
-    ready = 1
-    for index, (start, width) in enumerate(chunks):
+    half_blocks = samples // 2 // LANE
+    for index, (start, width, first, count) in enumerate(pieces):
         tile_copies[index].wait()
-        right = tile_buf[:, :, start : start + width].reshape(views * footprint, width)
-        sums_buf[:, start : start + width] = jnp.dot(
-            left_buf[...], right, preferred_element_type=jnp.float32
-        )
+        right = tile_buf[first : first + count, :, start : start + width].reshape(count * depth, width)
+        left = left_buf[:, first * depth : (first + count) * depth]
+        sums = jnp.dot(left, right, preferred_element_type=jnp.float32)
+        if first:
+            sums = sums + sums_buf[:, start : start + width]
+        sums_buf[:, start : start + width] = sums
         if index == 1:
             offset_copy.wait()
-        if index:
-            pack(ready, start // LANE)
-            ready = max(ready, start // LANE)
-    pack(ready, samples // LANE)
+            pack(1, half_blocks)
+    pack(half_blocks, samples // LANE)
     pack(0, 1)
 
 
@@ -181,7 +181,6 @@
     views, rows, footprint = proj.shape
     blocks, depth, samples = tiles.shape
     owned = rows // devices
-    chunks = column_chunks(samples)
     half = devices // 2
     shapes = [
         pltpu.VMEM((-(-(slots * rows_per_owner(owned) + owned) // 8) * 8, LANE), jnp.float32)
@@ -211,7 +210,7 @@
             pltpu.SemaphoreType.DMA((2,)),
             pltpu.SemaphoreType.DMA,
             pltpu.SemaphoreType.DMA,
-            pltpu.SemaphoreType.DMA((len(chunks),)),
+            pltpu.SemaphoreType.DMA((len(tile_pieces(blocks, samples)),)),
         ],
         compiler_params=pltpu.CompilerParams(vmem_limit_bytes=40 << 20),
         cost_estimate=pl.CostEstimate(
@@ -326,10 +325,6 @@
     bins = samples // COLS
     per_bin = COLS // LANE
 
-    def halves(value):
-        coarse = value.astype(jnp.bfloat16)
-        return coarse, (value - coarse.astype(jnp.float32)).astype(jnp.bfloat16)
-
     sum_buf[0 : other_ref.shape[0], :] = other_ref[...]
     rank = rank_ref[...]
     left = []
@@ -344,7 +339,8 @@
         sums = sums + kept_ref[:, part * COLS : (part + 1) * COLS]
         weight = inner_ref[:, part * COLS : (part + 1) * COLS]
         scaled = jnp.where(weight > 0.0, weight * sums, 0.0)
-        left.append(jnp.concatenate(halves(scaled), axis=0))
+        coarse = scaled.astype(jnp.bfloat16).astype(jnp.float32)
+        left.append(jnp.concatenate([coarse, scaled - coarse], axis=0).astype(jnp.bfloat16))
     image = [None] * bins
     for shift in range(1 - bins, bins):
         first, last = max(0, -shift), min(bins, bins - shift)

time: 17.2 us -> 17.1 us (level)
  no operation moved by 1% of the time
where the time goes in v9:
time: 17.1 us; the launch traced here: 17 us
  starting transfers between devices  11 us (64%)
  Pallas kernels  4.37 us (26%)
  waiting for transfers between devices  1.59 us (9%)
    ppermute x8, starting transfers between devices, give(): return lax.ppermute(value, 'view', pairs)  11 us
    pallas_call x1, Pallas kernels, project(): pl.pallas_call(kernel, out_shape=tuple(shapes), in_specs=[hbm] * 4, out_s...  2.5 us
    ppermute x8, waiting for transfers between devices, give(): return lax.ppermute(value, 'view', pairs)  1.59 us
    pallas_call x1, Pallas kernels, invert(): pl.pallas_call(invert_kernel, out_shape=jax.ShapeDtypeStruct((1, owned, s...  1.02 us
    pallas_call x1, Pallas kernels, prepare(): pl.pallas_call(kernel, out_shape=(pltpu.SMEM((1, samples // LANE), jnp.in...  0.82 us
  transfers between devices with their start and end apart: 8, of which 2 were waited for; matrix products, arithmetic and copies ran while one was open for 0% of the time, Pallas kernels for 5%

profile of v9, /device:TPU:0, one launch (start us, length us, event | category | flops | bytes accessed | tf_op | source)
XLA Modules:
  0.0 17.0 jit_solution(18214921291724952649)
XLA Ops:
  0.0 2.5 %project.1 = (f32[360,128]{1,0:T(8,128)S(1)}, f32[320,128]{1,0:T(8,128)S(1)}, f32[56,128]{1,0:T(8,128)S(1)}) custom-call(s32[2,128]{1,0:T(2,128)} %refs_0_.3, s32[2,128]{1,0:T(2,128)} %refs_1_.3, bf16[12,128,128]{2,1,0:T(8,128)(2,1)} %refs_2_.1, bf16[6,256,1024]{2,1,0:T(8,128)(2,1)} %refs_3_.1), custom_call_target="tpu_custom_call" | custom-call | flops 402653184 | bytes 3538944 | tf_op jit(solution)/shard_map/project/pallas_call | solution.py:196
  2.5 0.5 %collective-permute-start.2 = (f32[56,128]{1,0:T(8,128)S(1)}, f32[56,128]{1,0:T(8,128)S(1)}, u32[]{:S(2)}, u32[]{:S(2)}) collective-permute-start(f32[56,128]{1,0:T(8,128)S(1)} %get-tuple-element.17), channel_id=1, source_target_pairs={{0,2},{2,0},{4,6},{6,4},{8,10},{10,8},{12,14},{14,12},{16,18},{18,... | collective-permute-start | bytes 86024 | tf_op jit(solution)/shard_map/ppermute | solution.py:417
  3.0 0.1 collective-permute-start
  3.1 0.8 %collective-permute-done.2 = f32[56,128]{1,0:T(8,128)S(1)} collective-permute-done((f32[56,128]{1,0:T(8,128)S(1)}, f32[56,128]{1,0:T(8,128)S(1)}, u32[]{:S(2)}, u32[]{:S(2)}) %collective-permute-start.2) | collective-permute-done | bytes 28704 | tf_op jit(solution)/shard_map/ppermute | solution.py:417
  3.9 2.6 %collective-permute-start.3 = (f32[44,128]{1,0:T(8,128)S(1)}, f32[44,128]{1,0:T(8,128)S(1)}, u32[]{:S(2)}, u32[]{:S(2)}) collective-permute-start(f32[44,128]{1,0:T(8,128)S(1)} %slice_add_fusion), channel_id=1, source_target_pairs={{0,6},{2,8},{4,14},{6,0},{8,2},{10,12},{12,10},{14,4},{16,22},{18,... | collective-permute-start | bytes 67592 | tf_op jit(solution)/shard_map/ppermute | solution.py:417
  6.5 0.0 collective-permute-done.refs_1_.refs_3_
  6.5 0.5 %collective-permute-start.6 = (f32[44,128]{1,0:T(8,128)S(1)}, f32[44,128]{1,0:T(8,128)S(1)}, u32[]{:S(2)}, u32[]{:S(2)}) collective-permute-start(f32[44,128]{1,0:T(8,128)S(1)} %add_rows.4), channel_id=1, source_target_pairs={{0,6},{2,8},{4,14},{6,0},{8,2},{10,12},{12,10},{14,4},{16,22},{18,... | collective-permute-start | bytes 67592 | tf_op jit(solution)/shard_map/ppermute | solution.py:417
  7.1 1.3 %collective-permute-start.1 = (f32[88,128]{1,0:T(8,128)S(1)}, f32[88,128]{1,0:T(8,128)S(1)}, u32[]{:S(2)}, u32[]{:S(2)}) collective-permute-start(f32[88,128]{1,0:T(8,128)S(1)} %add_rows.3), channel_id=1, source_target_pairs={{0,6},{2,8},{4,14},{6,0},{8,2},{10,12},{12,10},{14,4},{16,22},{18,... | collective-permute-start | bytes 135176 | tf_op jit(solution)/shard_map/ppermute | solution.py:417
  8.4 0.0 collective-permute-done.3
  8.4 1.8 %collective-permute-start.4 = (f32[44,128]{1,0:T(8,128)S(1)}, f32[44,128]{1,0:T(8,128)S(1)}, u32[]{:S(2)}, u32[]{:S(2)}) collective-permute-start(f32[44,128]{1,0:T(8,128)S(1)} %fusion), channel_id=1, source_target_pairs={{0,10},{2,4},{4,2},{6,12},{8,14},{10,0},{12,6},{14,8},{16,26},{18,... | collective-permute-start | bytes 67592 | tf_op jit(solution)/shard_map/ppermute | solution.py:417
  10.2 0.0 collective-permute-done.6.refs_2_
  10.2 1.5 %collective-permute-start.7 = (f32[44,128]{1,0:T(8,128)S(1)}, f32[44,128]{1,0:T(8,128)S(1)}, u32[]{:S(2)}, u32[]{:S(2)}) collective-permute-start(f32[44,128]{1,0:T(8,128)S(1)} %add_rows.5), channel_id=1, source_target_pairs={{0,10},{2,4},{4,2},{6,12},{8,14},{10,0},{12,6},{14,8},{16,26},{18,... | collective-permute-start | bytes 67592 | tf_op jit(solution)/shard_map/ppermute | solution.py:417
  11.7 0.0 collective-permute-done.4
  11.7 0.0 collective-permute-done.1.refs_4_
  11.7 2.6 %collective-permute-start.5 = (f32[44,128]{1,0:T(8,128)S(1)}, f32[44,128]{1,0:T(8,128)S(1)}, u32[]{:S(2)}, u32[]{:S(2)}) collective-permute-start(f32[44,128]{1,0:T(8,128)S(1)} %fusion.1), channel_id=1, source_target_pairs={{0,18},{2,16},{4,22},{6,20},{8,26},{10,24},{12,30},{14,28},{16,2},... | collective-permute-start | bytes 67592 | tf_op jit(solution)/shard_map/ppermute | solution.py:417
  14.4 0.0 collective-permute-done.7.refs_5_
  14.4 0.8 %prepare.1 = (s32[1,8]{1,0:T(1,128)S(4)}, s32[8,128]{1,0:T(8,128)S(1)}, f32[8,1024]{1,0:T(8,128)S(1)}, f32[8,1024]{1,0:T(8,128)S(1)}, f32[8,1024]{1,0:T(8,128)S(...) custom-call(s32[2,128]{1,0:T(2,128)} %refs_0_.3, s32[2,128]{1,0:T(2,128)} %refs_1_.3, ...), custom_call_target="tpu_custom_call" | custom-call | flops 4194304 | bytes 2097152 | tf_op jit(solution)/shard_map/prepare/pallas_call | solution.py:296
  15.2 0.8 %collective-permute-done.5.other_ref = f32[44,128]{1,0:T(8,128)S(1)} collective-permute-done((f32[44,128]{1,0:T(8,128)S(1)}, f32[44,128]{1,0:T(8,128)S(1)}, u32[]{:S(2)}, u32[]{:S(2)}) %collective-permute-start.5) | collective-permute-done | bytes 22560 | tf_op jit(solution)/shard_map/ppermute | solution.py:417
  16.0 1.0 %invert.1 = f32[1,8,1024]{2,1,0:T(8,128)} custom-call(f32[44,128]{1,0:T(8,128)S(1)} %collective-permute-done.5.other_ref, s32[1,8]{1,0:T(1,128)S(4)} %get-tuple-element.18.offset_ref, s32[8,128]{1,0:T(8,128)S(1)} %get-tuple-element.19.rank_ref, f32[8,1024]{1,0:T(8,128)S(1)} %get-tuple-element.20.kept_ref, f32[8,1024]{1,0:T(8,128)S(1)} %get-tuple-element.21.inner_ref, ...), custom_call_target="tpu_custom_call" | custom-call | tf_op jit(solution)/shard_map/invert/pallas_call | solution.py:363
  (6 shorter events, 0.0 us)
Async XLA Ops:
  2.5 1.4 %collective-permute-start.2 = (f32[56,128]{1,0:T(8,128)S(1)}, f32[56,128]{1,0:T(8,128)S(1)}, u32[]{:S(2)}, u32[]{:S(2)}) collective-permute-start(f32[56,128]{1,0:T(8,128)S(1)} %get-tuple-element.17), channel_id=1, source_target_pairs={{0,2},{2,0},{4,6},{6,4},{8,10},{10,8},{12,14},{14,12},{16,18},{18,... | collective-permute-start | bytes 86024 | tf_op jit(solution)/shard_map/ppermute | solution.py:417
  3.0 3.5 %collective-permute-start = (f32[320,128]{1,0:T(8,128)S(1)}, f32[320,128]{1,0:T(8,128)S(1)}, u32[]{:S(2)}, u32[]{:S(2)}) collective-permute-start(f32[320,128]{1,0:T(8,128)S(1)} %get-tuple-element.16), channel_id=1, source_target_pairs={{0,2},{2,0},{4,6},{6,4},{8,10},{10,8},{12,14},{14,12},{16,18},{18,... | collective-permute-start | bytes 491528 | tf_op jit(solution)/shard_map/ppermute | solution.py:417
  3.9 4.5 %collective-permute-start.3 = (f32[44,128]{1,0:T(8,128)S(1)}, f32[44,128]{1,0:T(8,128)S(1)}, u32[]{:S(2)}, u32[]{:S(2)}) collective-permute-start(f32[44,128]{1,0:T(8,128)S(1)} %slice_add_fusion), channel_id=1, source_target_pairs={{0,6},{2,8},{4,14},{6,0},{8,2},{10,12},{12,10},{14,4},{16,22},{18,... | collective-permute-start | bytes 67592 | tf_op jit(solution)/shard_map/ppermute | solution.py:417
  6.5 3.7 %collective-permute-start.6 = (f32[44,128]{1,0:T(8,128)S(1)}, f32[44,128]{1,0:T(8,128)S(1)}, u32[]{:S(2)}, u32[]{:S(2)}) collective-permute-start(f32[44,128]{1,0:T(8,128)S(1)} %add_rows.4), channel_id=1, source_target_pairs={{0,6},{2,8},{4,14},{6,0},{8,2},{10,12},{12,10},{14,4},{16,22},{18,... | collective-permute-start | bytes 67592 | tf_op jit(solution)/shard_map/ppermute | solution.py:417
  7.1 4.7 %collective-permute-start.1 = (f32[88,128]{1,0:T(8,128)S(1)}, f32[88,128]{1,0:T(8,128)S(1)}, u32[]{:S(2)}, u32[]{:S(2)}) collective-permute-start(f32[88,128]{1,0:T(8,128)S(1)} %add_rows.3), channel_id=1, source_target_pairs={{0,6},{2,8},{4,14},{6,0},{8,2},{10,12},{12,10},{14,4},{16,22},{18,... | collective-permute-start | bytes 135176 | tf_op jit(solution)/shard_map/ppermute | solution.py:417
  8.4 3.4 %collective-permute-start.4 = (f32[44,128]{1,0:T(8,128)S(1)}, f32[44,128]{1,0:T(8,128)S(1)}, u32[]{:S(2)}, u32[]{:S(2)}) collective-permute-start(f32[44,128]{1,0:T(8,128)S(1)} %fusion), channel_id=1, source_target_pairs={{0,10},{2,4},{4,2},{6,12},{8,14},{10,0},{12,6},{14,8},{16,26},{18,... | collective-permute-start | bytes 67592 | tf_op jit(solution)/shard_map/ppermute | solution.py:417
  10.2 4.2 %collective-permute-start.7 = (f32[44,128]{1,0:T(8,128)S(1)}, f32[44,128]{1,0:T(8,128)S(1)}, u32[]{:S(2)}, u32[]{:S(2)}) collective-permute-start(f32[44,128]{1,0:T(8,128)S(1)} %add_rows.5), channel_id=1, source_target_pairs={{0,10},{2,4},{4,2},{6,12},{8,14},{10,0},{12,6},{14,8},{16,26},{18,... | collective-permute-start | bytes 67592 | tf_op jit(solution)/shard_map/ppermute | solution.py:417
  11.7 4.2 %collective-permute-start.5 = (f32[44,128]{1,0:T(8,128)S(1)}, f32[44,128]{1,0:T(8,128)S(1)}, u32[]{:S(2)}, u32[]{:S(2)}) collective-permute-start(f32[44,128]{1,0:T(8,128)S(1)} %fusion.1), channel_id=1, source_target_pairs={{0,18},{2,16},{4,22},{6,20},{8,26},{10,24},{12,30},{14,28},{16,2},... | collective-permute-start | bytes 67592 | tf_op jit(solution)/shard_map/ppermute | solution.py:417

commit v10 on v9

--- a/solution.py
+++ b/solution.py
@@ -55,7 +55,7 @@
 
 
 def project_kernel(
-    devices, owner_hbm, lengths_hbm, proj_hbm, tiles_hbm, keep_ref, rest_ref, first_ref,
+    devices, owner_hbm, lengths_hbm, proj_hbm, tiles_hbm, keep_ref, third_ref, second_ref, first_ref,
     owner_v, lengths_v, offset_v, offset_s, proj_buf, tile_buf, left_buf, sums_buf,
     small_sem, offset_sem, proj_sem, tile_sem,
 ):
@@ -83,7 +83,7 @@
         copy.start()
         tile_copies.append(copy)
 
-    for ref in (keep_ref, rest_ref, first_ref):
+    for ref in (keep_ref, third_ref, second_ref, first_ref):
         ref[...] = jnp.zeros_like(ref)
     for copy in small:
         copy.wait()
@@ -141,17 +141,13 @@
         def to(out_ref, index):
             out_ref[pl.ds(index * packed + offset, owned), :] = value
 
-        if isinstance(slot_index, int):
-            if slot_index == devices - 1:
-                to(first_ref, 0)
-            elif slot_index < half:
-                to(keep_ref, slot_index)
-            else:
-                to(rest_ref, slot_index - half)
-        else:
-            pl.when(slot_index == devices - 1)(lambda: to(first_ref, 0))
-            pl.when(slot_index < half)(lambda: to(keep_ref, slot_index))
-            pl.when((slot_index >= half) & (slot_index < devices - 1))(lambda: to(rest_ref, slot_index - half))
+        bounds = [0, half, half + half // 2, devices - 1, devices]
+        for low, high, ref in zip(bounds, bounds[1:], (keep_ref, third_ref, second_ref, first_ref)):
+            if not isinstance(slot_index, int):
+                here = (slot_index >= low) & (slot_index < high)
+                pl.when(here)(lambda ref=ref, low=low: to(ref, slot_index - low))
+            elif low <= slot_index < high:
+                to(ref, slot_index - low)
 
     def pack(first, last):
         def one(slot_index):
@@ -184,7 +180,7 @@
     half = devices // 2
     shapes = [
         pltpu.VMEM((-(-(slots * rows_per_owner(owned) + owned) // 8) * 8, LANE), jnp.float32)
-        for slots in (half, half - 1, 1)
+        for slots in (half, half // 2, half // 2 - 1, 1)
     ]
     inputs = [pltpu.with_memory_space_constraint(x, pltpu.HBM) for x in (owner, lengths, proj, tiles)]
 
@@ -197,7 +193,7 @@
         kernel,
         out_shape=tuple(shapes),
         in_specs=[hbm] * 4,
-        out_specs=(vmem,) * 3,
+        out_specs=(vmem,) * 4,
         scratch_shapes=[
             pltpu.VMEM(owner.shape, jnp.int32),
             pltpu.VMEM(lengths.shape, jnp.int32),
@@ -402,7 +398,7 @@
     samples = tiles.shape[2]
     owned = rows // devices
     packed = rows_per_owner(owned)
-    keep, rest, first = project(proj, tiles, owner, lengths, devices)
+    keep, third, second, first = project(proj, tiles, owner, lengths, devices)
 
     def total(terms, place):
         value, *others = [array[(place - base) * packed : (place - base + 1) * packed] for array, base in terms]
@@ -417,18 +413,15 @@
         return lax.ppermute(value, "view", pairs)
 
     held = devices // 2
-    pairs, *steps, last_pairs = exchange_pairs(devices)
-    got_first, got_rest = give(first), give(rest)
-    first = total([(keep, 0)], held - 1) + got_first[:packed]
-    terms = [(keep, 0), (got_rest, 0)]
-    sent_next = terms
+    *steps, last_pairs = exchange_pairs(devices)
+    terms = [(keep, 0)]
     for pairs in steps:
-        held //= 2
-        got_first, got_second = give(first), None
-        if held > 2:
-            got_second = give(apart(sent_next, held + held // 2, held // 2 - 1))
-        got_third = give(apart(sent_next, held, held // 2))
-        first = total(terms, held - 1) + got_first
+        if len(terms) > 1:
+            held //= 2
+            second = apart(sent_next, held + held // 2, held // 2 - 1) if held > 2 else None
+            third = apart(sent_next, held, held // 2)
+        got_first, got_second, got_third = give(first), None if second is None else give(second), give(third)
+        first = total(terms, held - 1) + got_first[:packed]
         sent_next = terms + [(got_second, held // 2)]
         terms = terms + [(got_third, 0)]
     pairs = last_pairs

time: 17.1 us -> 17.1 us (level)
  waiting for transfers between devices: 1.59 us -> 1.08 us
  starting transfers between devices: 11 us -> 11.4 us
    ppermute x8 -> x9, waiting for transfers between devices: 1.59 us -> 1.08 us  [give(): return lax.ppermute(value, 'view', pairs)]
    ppermute x8 -> x9, starting transfers between devices: 11 us -> 11.4 us  [give(): return lax.ppermute(value, 'view', pairs)]
  transfers between devices with their start and end apart: 8 -> 9, of which waited for: 2 -> 2; matrix products, arithmetic and copies ran while one was open for 0% -> 0% of each run, Pallas kernels for 5% -> 5%
where the time goes in v10:
time: 17.1 us; the launch traced here: 16.9 us
  starting transfers between devices  11.4 us (67%)
  Pallas kernels  4.36 us (25%)
  waiting for transfers between devices  1.08 us (6%)
    ppermute x9, starting transfers between devices, give(): return lax.ppermute(value, 'view', pairs)  11.4 us
    pallas_call x1, Pallas kernels, project(): pl.pallas_call(kernel, out_shape=tuple(shapes), in_specs=[hbm] * 4, out_s...  2.5 us
    ppermute x9, waiting for transfers between devices, give(): return lax.ppermute(value, 'view', pairs)  1.08 us
    pallas_call x1, Pallas kernels, invert(): pl.pallas_call(invert_kernel, out_shape=jax.ShapeDtypeStruct((1, owned, s...  1.02 us
    pallas_call x1, Pallas kernels, prepare(): pl.pallas_call(kernel, out_shape=(pltpu.SMEM((1, samples // LANE), jnp.in...  0.82 us
  transfers between devices with their start and end apart: 9, of which 2 were waited for; matrix products, arithmetic and copies ran while one was open for 0% of the time, Pallas kernels for 5%

profile of v10, /device:TPU:0, one launch (start us, length us, event | category | flops | bytes accessed | tf_op | source)
XLA Modules:
  0.0 16.9 jit_solution(1515931161383148728)
XLA Ops:
  0.0 2.5 %project.1 = (f32[360,128]{1,0:T(8,128)S(1)}, f32[184,128]{1,0:T(8,128)S(1)}, f32[144,128]{1,0:T(8,128)S(1)}, f32[56,128]{1,0:T(8,128)S(1)}) custom-call(s32[2,128]{1,0:T(2,128)} %refs_0_.3, s32[2,128]{1,0:T(2,128)} %refs_1_.3, bf16[12,128,128]{2,1,0:T(8,128)(2,1)} %refs_2_.1, bf16[6,256,1024]{2,1,0:T(8,128)(2,1)} %refs_3_.1), custom_call_target="tpu_custom_call" | custom-call | flops 402653184 | bytes 3538944 | tf_op jit(solution)/shard_map/project/pallas_call | solution.py:192
  2.5 0.5 %collective-permute-start.3 = (f32[56,128]{1,0:T(8,128)S(1)}, f32[56,128]{1,0:T(8,128)S(1)}, u32[]{:S(2)}, u32[]{:S(2)}) collective-permute-start(f32[56,128]{1,0:T(8,128)S(1)} %get-tuple-element.19), channel_id=1, source_target_pairs={{0,2},{2,0},{4,6},{6,4},{8,10},{10,8},{12,14},{14,12},{16,18},{18,... | collective-permute-start | bytes 86024 | tf_op jit(solution)/shard_map/ppermute | solution.py:413
  3.0 0.1 collective-permute-start.1
  3.1 0.4 %collective-permute-start = (f32[184,128]{1,0:T(8,128)S(1)}, f32[184,128]{1,0:T(8,128)S(1)}, u32[]{:S(2)}, u32[]{:S(2)}) collective-permute-start(f32[184,128]{1,0:T(8,128)S(1)} %get-tuple-element.17), channel_id=1, source_target_pairs={{0,2},{2,0},{4,6},{6,4},{8,10},{10,8},{12,14},{14,12},{16,18},{18,... | collective-permute-start | bytes 282632 | tf_op jit(solution)/shard_map/ppermute | solution.py:413
  3.5 0.3 %collective-permute-done.3 = f32[56,128]{1,0:T(8,128)S(1)} collective-permute-done((f32[56,128]{1,0:T(8,128)S(1)}, f32[56,128]{1,0:T(8,128)S(1)}, u32[]{:S(2)}, u32[]{:S(2)}) %collective-permute-start.3) | collective-permute-done | bytes 28704 | tf_op jit(solution)/shard_map/ppermute | solution.py:413
  3.9 2.6 %collective-permute-start.4 = (f32[44,128]{1,0:T(8,128)S(1)}, f32[44,128]{1,0:T(8,128)S(1)}, u32[]{:S(2)}, u32[]{:S(2)}) collective-permute-start(f32[44,128]{1,0:T(8,128)S(1)} %slice_add_fusion), channel_id=1, source_target_pairs={{0,6},{2,8},{4,14},{6,0},{8,2},{10,12},{12,10},{14,4},{16,22},{18,... | collective-permute-start | bytes 67592 | tf_op jit(solution)/shard_map/ppermute | solution.py:413
  6.5 0.0 collective-permute-done.1.refs_1_
  6.5 0.4 %collective-permute-start.7 = (f32[44,128]{1,0:T(8,128)S(1)}, f32[44,128]{1,0:T(8,128)S(1)}, u32[]{:S(2)}, u32[]{:S(2)}) collective-permute-start(f32[44,128]{1,0:T(8,128)S(1)} %add_rows.4), channel_id=1, source_target_pairs={{0,6},{2,8},{4,14},{6,0},{8,2},{10,12},{12,10},{14,4},{16,22},{18,... | collective-permute-start | bytes 67592 | tf_op jit(solution)/shard_map/ppermute | solution.py:413
  6.9 1.4 %collective-permute-start.2 = (f32[88,128]{1,0:T(8,128)S(1)}, f32[88,128]{1,0:T(8,128)S(1)}, u32[]{:S(2)}, u32[]{:S(2)}) collective-permute-start(f32[88,128]{1,0:T(8,128)S(1)} %add_rows.3), channel_id=1, source_target_pairs={{0,6},{2,8},{4,14},{6,0},{8,2},{10,12},{12,10},{14,4},{16,22},{18,... | collective-permute-start | bytes 135176 | tf_op jit(solution)/shard_map/ppermute | solution.py:413
  8.3 0.0 collective-permute-done.4
  8.3 0.0 collective-permute-done.refs_1_.refs_3_
  8.4 1.8 %collective-permute-start.5 = (f32[44,128]{1,0:T(8,128)S(1)}, f32[44,128]{1,0:T(8,128)S(1)}, u32[]{:S(2)}, u32[]{:S(2)}) collective-permute-start(f32[44,128]{1,0:T(8,128)S(1)} %fusion), channel_id=1, source_target_pairs={{0,10},{2,4},{4,2},{6,12},{8,14},{10,0},{12,6},{14,8},{16,26},{18,... | collective-permute-start | bytes 67592 | tf_op jit(solution)/shard_map/ppermute | solution.py:413
  10.1 0.0 collective-permute-done.7.refs_2_
  10.1 1.5 %collective-permute-start.8 = (f32[44,128]{1,0:T(8,128)S(1)}, f32[44,128]{1,0:T(8,128)S(1)}, u32[]{:S(2)}, u32[]{:S(2)}) collective-permute-start(f32[44,128]{1,0:T(8,128)S(1)} %add_rows.5), channel_id=1, source_target_pairs={{0,10},{2,4},{4,2},{6,12},{8,14},{10,0},{12,6},{14,8},{16,26},{18,... | collective-permute-start | bytes 67592 | tf_op jit(solution)/shard_map/ppermute | solution.py:413
  11.7 0.0 collective-permute-done.5
  11.7 0.0 collective-permute-done.2.refs_4_
  11.7 2.7 %collective-permute-start.6 = (f32[44,128]{1,0:T(8,128)S(1)}, f32[44,128]{1,0:T(8,128)S(1)}, u32[]{:S(2)}, u32[]{:S(2)}) collective-permute-start(f32[44,128]{1,0:T(8,128)S(1)} %fusion.1), channel_id=1, source_target_pairs={{0,18},{2,16},{4,22},{6,20},{8,26},{10,24},{12,30},{14,28},{16,2},... | collective-permute-start | bytes 67592 | tf_op jit(solution)/shard_map/ppermute | solution.py:413
  14.4 0.0 collective-permute-done.8.refs_5_
  14.4 0.8 %prepare.1 = (s32[1,8]{1,0:T(1,128)S(4)}, s32[8,128]{1,0:T(8,128)S(1)}, f32[8,1024]{1,0:T(8,128)S(1)}, f32[8,1024]{1,0:T(8,128)S(1)}, f32[8,1024]{1,0:T(8,128)S(...) custom-call(s32[2,128]{1,0:T(2,128)} %refs_0_.3, s32[2,128]{1,0:T(2,128)} %refs_1_.3, ...), custom_call_target="tpu_custom_call" | custom-call | flops 4194304 | bytes 2097152 | tf_op jit(solution)/shard_map/prepare/pallas_call | solution.py:292
  15.2 0.7 %collective-permute-done.6.other_ref = f32[44,128]{1,0:T(8,128)S(1)} collective-permute-done((f32[44,128]{1,0:T(8,128)S(1)}, f32[44,128]{1,0:T(8,128)S(1)}, u32[]{:S(2)}, u32[]{:S(2)}) %collective-permute-start.6) | collective-permute-done | bytes 22560 | tf_op jit(solution)/shard_map/ppermute | solution.py:413
  15.9 1.0 %invert.1 = f32[1,8,1024]{2,1,0:T(8,128)} custom-call(f32[44,128]{1,0:T(8,128)S(1)} %collective-permute-done.6.other_ref, s32[1,8]{1,0:T(1,128)S(4)} %get-tuple-element.20.offset_ref, s32[8,128]{1,0:T(8,128)S(1)} %get-tuple-element.21.rank_ref, f32[8,1024]{1,0:T(8,128)S(1)} %get-tuple-element.22.kept_ref, f32[8,1024]{1,0:T(8,128)S(1)} %get-tuple-element.23.inner_ref, ...), custom_call_target="tpu_custom_call" | custom-call | tf_op jit(solution)/shard_map/invert/pallas_call | solution.py:359
  (6 shorter events, 0.0 us)
Async XLA Ops:
  2.5 1.4 %collective-permute-start.3 = (f32[56,128]{1,0:T(8,128)S(1)}, f32[56,128]{1,0:T(8,128)S(1)}, u32[]{:S(2)}, u32[]{:S(2)}) collective-permute-start(f32[56,128]{1,0:T(8,128)S(1)} %get-tuple-element.19), channel_id=1, source_target_pairs={{0,2},{2,0},{4,6},{6,4},{8,10},{10,8},{12,14},{14,12},{16,18},{18,... | collective-permute-start | bytes 86024 | tf_op jit(solution)/shard_map/ppermute | solution.py:413
  3.0 3.5 %collective-permute-start.1 = (f32[144,128]{1,0:T(8,128)S(1)}, f32[144,128]{1,0:T(8,128)S(1)}, u32[]{:S(2)}, u32[]{:S(2)}) collective-permute-start(f32[144,128]{1,0:T(8,128)S(1)} %get-tuple-element.18), channel_id=1, source_target_pairs={{0,2},{2,0},{4,6},{6,4},{8,10},{10,8},{12,14},{14,12},{16,18},{18,... | collective-permute-start | bytes 221192 | tf_op jit(solution)/shard_map/ppermute | solution.py:413
  3.1 5.2 %collective-permute-start = (f32[184,128]{1,0:T(8,128)S(1)}, f32[184,128]{1,0:T(8,128)S(1)}, u32[]{:S(2)}, u32[]{:S(2)}) collective-permute-start(f32[184,128]{1,0:T(8,128)S(1)} %get-tuple-element.17), channel_id=1, source_target_pairs={{0,2},{2,0},{4,6},{6,4},{8,10},{10,8},{12,14},{14,12},{16,18},{18,... | collective-permute-start | bytes 282632 | tf_op jit(solution)/shard_map/ppermute | solution.py:413
  3.9 4.5 %collective-permute-start.4 = (f32[44,128]{1,0:T(8,128)S(1)}, f32[44,128]{1,0:T(8,128)S(1)}, u32[]{:S(2)}, u32[]{:S(2)}) collective-permute-start(f32[44,128]{1,0:T(8,128)S(1)} %slice_add_fusion), channel_id=1, source_target_pairs={{0,6},{2,8},{4,14},{6,0},{8,2},{10,12},{12,10},{14,4},{16,22},{18,... | collective-permute-start | bytes 67592 | tf_op jit(solution)/shard_map/ppermute | solution.py:413
  6.5 3.6 %collective-permute-start.7 = (f32[44,128]{1,0:T(8,128)S(1)}, f32[44,128]{1,0:T(8,128)S(1)}, u32[]{:S(2)}, u32[]{:S(2)}) collective-permute-start(f32[44,128]{1,0:T(8,128)S(1)} %add_rows.4), channel_id=1, source_target_pairs={{0,6},{2,8},{4,14},{6,0},{8,2},{10,12},{12,10},{14,4},{16,22},{18,... | collective-permute-start | bytes 67592 | tf_op jit(solution)/shard_map/ppermute | solution.py:413
  6.9 4.7 %collective-permute-start.2 = (f32[88,128]{1,0:T(8,128)S(1)}, f32[88,128]{1,0:T(8,128)S(1)}, u32[]{:S(2)}, u32[]{:S(2)}) collective-permute-start(f32[88,128]{1,0:T(8,128)S(1)} %add_rows.3), channel_id=1, source_target_pairs={{0,6},{2,8},{4,14},{6,0},{8,2},{10,12},{12,10},{14,4},{16,22},{18,... | collective-permute-start | bytes 135176 | tf_op jit(solution)/shard_map/ppermute | solution.py:413
  8.4 3.3 %collective-permute-start.5 = (f32[44,128]{1,0:T(8,128)S(1)}, f32[44,128]{1,0:T(8,128)S(1)}, u32[]{:S(2)}, u32[]{:S(2)}) collective-permute-start(f32[44,128]{1,0:T(8,128)S(1)} %fusion), channel_id=1, source_target_pairs={{0,10},{2,4},{4,2},{6,12},{8,14},{10,0},{12,6},{14,8},{16,26},{18,... | collective-permute-start | bytes 67592 | tf_op jit(solution)/shard_map/ppermute | solution.py:413
  10.1 4.2 %collective-permute-start.8 = (f32[44,128]{1,0:T(8,128)S(1)}, f32[44,128]{1,0:T(8,128)S(1)}, u32[]{:S(2)}, u32[]{:S(2)}) collective-permute-start(f32[44,128]{1,0:T(8,128)S(1)} %add_rows.5), channel_id=1, source_target_pairs={{0,10},{2,4},{4,2},{6,12},{8,14},{10,0},{12,6},{14,8},{16,26},{18,... | collective-permute-start | bytes 67592 | tf_op jit(solution)/shard_map/ppermute | solution.py:413
  11.7 4.2 %collective-permute-start.6 = (f32[44,128]{1,0:T(8,128)S(1)}, f32[44,128]{1,0:T(8,128)S(1)}, u32[]{:S(2)}, u32[]{:S(2)}) collective-permute-start(f32[44,128]{1,0:T(8,128)S(1)} %fusion.1), channel_id=1, source_target_pairs={{0,18},{2,16},{4,22},{6,20},{8,26},{10,24},{12,30},{14,28},{16,2},... | collective-permute-start | bytes 67592 | tf_op jit(solution)/shard_map/ppermute | solution.py:413

commit v11 on v10

--- a/solution.py
+++ b/solution.py
@@ -130,9 +130,8 @@
             pl.loop(0, devices)(body)
 
     proj_copy.wait()
-    for view in range(views):
-        moved = jnp.dot(pick, proj_buf[view], preferred_element_type=jnp.float32)
-        left_buf[:, view * footprint : (view + 1) * footprint] = moved.astype(jnp.bfloat16)
+    wide = jnp.concatenate([proj_buf[view] for view in range(views)], axis=1)
+    left_buf[...] = jnp.dot(pick, wide, preferred_element_type=jnp.float32).astype(jnp.bfloat16)
 
     packed = rows_per_owner(owned)
     half = devices // 2

time: 17.1 us -> 17.1 us (level)
  no operation moved by 1% of the time
where the time goes in v11:
time: 17.1 us; the launch traced here: 16.9 us
  starting transfers between devices  11.4 us (67%)
  Pallas kernels  4.35 us (25%)
  waiting for transfers between devices  1.08 us (6%)
    ppermute x9, starting transfers between devices, give(): return lax.ppermute(value, 'view', pairs)  11.4 us
    pallas_call x1, Pallas kernels, project(): pl.pallas_call(kernel, out_shape=tuple(shapes), in_specs=[hbm] * 4, out_s...  2.49 us
    ppermute x9, waiting for transfers between devices, give(): return lax.ppermute(value, 'view', pairs)  1.08 us
    pallas_call x1, Pallas kernels, invert(): pl.pallas_call(invert_kernel, out_shape=jax.ShapeDtypeStruct((1, owned, s...  1.02 us
    pallas_call x1, Pallas kernels, prepare(): pl.pallas_call(kernel, out_shape=(pltpu.SMEM((1, samples // LANE), jnp.in...  0.82 us
  transfers between devices with their start and end apart: 9, of which 2 were waited for; matrix products, arithmetic and copies ran while one was open for 0% of the time, Pallas kernels for 5%

profile of v11, /device:TPU:0, one launch (start us, length us, event | category | flops | bytes accessed | tf_op | source)
XLA Modules:
  0.0 16.9 jit_solution(11851798745593857914)
XLA Ops:
  0.0 2.5 %project.1 = (f32[360,128]{1,0:T(8,128)S(1)}, f32[184,128]{1,0:T(8,128)S(1)}, f32[144,128]{1,0:T(8,128)S(1)}, f32[56,128]{1,0:T(8,128)S(1)}) custom-call(s32[2,128]{1,0:T(2,128)} %refs_0_.3, s32[2,128]{1,0:T(2,128)} %refs_1_.3, bf16[12,128,128]{2,1,0:T(8,128)(2,1)} %refs_2_.1, bf16[6,256,1024]{2,1,0:T(8,128)(2,1)} %refs_3_.1), custom_call_target="tpu_custom_call" | custom-call | flops 402653184 | bytes 3538944 | tf_op jit(solution)/shard_map/project/pallas_call | solution.py:191
  2.5 0.5 %collective-permute-start.3 = (f32[56,128]{1,0:T(8,128)S(1)}, f32[56,128]{1,0:T(8,128)S(1)}, u32[]{:S(2)}, u32[]{:S(2)}) collective-permute-start(f32[56,128]{1,0:T(8,128)S(1)} %get-tuple-element.19), channel_id=1, source_target_pairs={{0,2},{2,0},{4,6},{6,4},{8,10},{10,8},{12,14},{14,12},{16,18},{18,... | collective-permute-start | bytes 86024 | tf_op jit(solution)/shard_map/ppermute | solution.py:412
  3.0 0.1 collective-permute-start.1
  3.1 0.4 %collective-permute-start = (f32[184,128]{1,0:T(8,128)S(1)}, f32[184,128]{1,0:T(8,128)S(1)}, u32[]{:S(2)}, u32[]{:S(2)}) collective-permute-start(f32[184,128]{1,0:T(8,128)S(1)} %get-tuple-element.17), channel_id=1, source_target_pairs={{0,2},{2,0},{4,6},{6,4},{8,10},{10,8},{12,14},{14,12},{16,18},{18,... | collective-permute-start | bytes 282632 | tf_op jit(solution)/shard_map/ppermute | solution.py:412
  3.5 0.3 %collective-permute-done.3 = f32[56,128]{1,0:T(8,128)S(1)} collective-permute-done((f32[56,128]{1,0:T(8,128)S(1)}, f32[56,128]{1,0:T(8,128)S(1)}, u32[]{:S(2)}, u32[]{:S(2)}) %collective-permute-start.3) | collective-permute-done | bytes 28704 | tf_op jit(solution)/shard_map/ppermute | solution.py:412
  3.9 2.6 %collective-permute-start.4 = (f32[44,128]{1,0:T(8,128)S(1)}, f32[44,128]{1,0:T(8,128)S(1)}, u32[]{:S(2)}, u32[]{:S(2)}) collective-permute-start(f32[44,128]{1,0:T(8,128)S(1)} %slice_add_fusion), channel_id=1, source_target_pairs={{0,6},{2,8},{4,14},{6,0},{8,2},{10,12},{12,10},{14,4},{16,22},{18,... | collective-permute-start | bytes 67592 | tf_op jit(solution)/shard_map/ppermute | solution.py:412
  6.5 0.0 collective-permute-done.1.refs_1_
  6.5 0.4 %collective-permute-start.7 = (f32[44,128]{1,0:T(8,128)S(1)}, f32[44,128]{1,0:T(8,128)S(1)}, u32[]{:S(2)}, u32[]{:S(2)}) collective-permute-start(f32[44,128]{1,0:T(8,128)S(1)} %add_rows.4), channel_id=1, source_target_pairs={{0,6},{2,8},{4,14},{6,0},{8,2},{10,12},{12,10},{14,4},{16,22},{18,... | collective-permute-start | bytes 67592 | tf_op jit(solution)/shard_map/ppermute | solution.py:412
  6.9 1.4 %collective-permute-start.2 = (f32[88,128]{1,0:T(8,128)S(1)}, f32[88,128]{1,0:T(8,128)S(1)}, u32[]{:S(2)}, u32[]{:S(2)}) collective-permute-start(f32[88,128]{1,0:T(8,128)S(1)} %add_rows.3), channel_id=1, source_target_pairs={{0,6},{2,8},{4,14},{6,0},{8,2},{10,12},{12,10},{14,4},{16,22},{18,... | collective-permute-start | bytes 135176 | tf_op jit(solution)/shard_map/ppermute | solution.py:412
  8.3 0.0 collective-permute-done.4
  8.3 0.0 collective-permute-done.refs_1_.refs_3_
  8.4 1.8 %collective-permute-start.5 = (f32[44,128]{1,0:T(8,128)S(1)}, f32[44,128]{1,0:T(8,128)S(1)}, u32[]{:S(2)}, u32[]{:S(2)}) collective-permute-start(f32[44,128]{1,0:T(8,128)S(1)} %fusion), channel_id=1, source_target_pairs={{0,10},{2,4},{4,2},{6,12},{8,14},{10,0},{12,6},{14,8},{16,26},{18,... | collective-permute-start | bytes 67592 | tf_op jit(solution)/shard_map/ppermute | solution.py:412
  10.1 0.0 collective-permute-done.7.refs_2_
  10.1 1.5 %collective-permute-start.8 = (f32[44,128]{1,0:T(8,128)S(1)}, f32[44,128]{1,0:T(8,128)S(1)}, u32[]{:S(2)}, u32[]{:S(2)}) collective-permute-start(f32[44,128]{1,0:T(8,128)S(1)} %add_rows.5), channel_id=1, source_target_pairs={{0,10},{2,4},{4,2},{6,12},{8,14},{10,0},{12,6},{14,8},{16,26},{18,... | collective-permute-start | bytes 67592 | tf_op jit(solution)/shard_map/ppermute | solution.py:412
  11.7 0.0 collective-permute-done.5
  11.7 0.0 collective-permute-done.2.refs_4_
  11.7 2.7 %collective-permute-start.6 = (f32[44,128]{1,0:T(8,128)S(1)}, f32[44,128]{1,0:T(8,128)S(1)}, u32[]{:S(2)}, u32[]{:S(2)}) collective-permute-start(f32[44,128]{1,0:T(8,128)S(1)} %fusion.1), channel_id=1, source_target_pairs={{0,18},{2,16},{4,22},{6,20},{8,26},{10,24},{12,30},{14,28},{16,2},... | collective-permute-start | bytes 67592 | tf_op jit(solution)/shard_map/ppermute | solution.py:412
  14.4 0.0 collective-permute-done.8.refs_5_
  14.4 0.8 %prepare.1 = (s32[1,8]{1,0:T(1,128)S(4)}, s32[8,128]{1,0:T(8,128)S(1)}, f32[8,1024]{1,0:T(8,128)S(1)}, f32[8,1024]{1,0:T(8,128)S(1)}, f32[8,1024]{1,0:T(8,128)S(...) custom-call(s32[2,128]{1,0:T(2,128)} %refs_0_.3, s32[2,128]{1,0:T(2,128)} %refs_1_.3, ...), custom_call_target="tpu_custom_call" | custom-call | flops 4194304 | bytes 2097152 | tf_op jit(solution)/shard_map/prepare/pallas_call | solution.py:291
  15.2 0.7 %collective-permute-done.6.other_ref = f32[44,128]{1,0:T(8,128)S(1)} collective-permute-done((f32[44,128]{1,0:T(8,128)S(1)}, f32[44,128]{1,0:T(8,128)S(1)}, u32[]{:S(2)}, u32[]{:S(2)}) %collective-permute-start.6) | collective-permute-done | bytes 22560 | tf_op jit(solution)/shard_map/ppermute | solution.py:412
  15.9 1.0 %invert.1 = f32[1,8,1024]{2,1,0:T(8,128)} custom-call(f32[44,128]{1,0:T(8,128)S(1)} %collective-permute-done.6.other_ref, s32[1,8]{1,0:T(1,128)S(4)} %get-tuple-element.20.offset_ref, s32[8,128]{1,0:T(8,128)S(1)} %get-tuple-element.21.rank_ref, f32[8,1024]{1,0:T(8,128)S(1)} %get-tuple-element.22.kept_ref, f32[8,1024]{1,0:T(8,128)S(1)} %get-tuple-element.23.inner_ref, ...), custom_call_target="tpu_custom_call" | custom-call | tf_op jit(solution)/shard_map/invert/pallas_call | solution.py:358
  (6 shorter events, 0.0 us)
Async XLA Ops:
  2.5 1.4 %collective-permute-start.3 = (f32[56,128]{1,0:T(8,128)S(1)}, f32[56,128]{1,0:T(8,128)S(1)}, u32[]{:S(2)}, u32[]{:S(2)}) collective-permute-start(f32[56,128]{1,0:T(8,128)S(1)} %get-tuple-element.19), channel_id=1, source_target_pairs={{0,2},{2,0},{4,6},{6,4},{8,10},{10,8},{12,14},{14,12},{16,18},{18,... | collective-permute-start | bytes 86024 | tf_op jit(solution)/shard_map/ppermute | solution.py:412
  3.0 3.5 %collective-permute-start.1 = (f32[144,128]{1,0:T(8,128)S(1)}, f32[144,128]{1,0:T(8,128)S(1)}, u32[]{:S(2)}, u32[]{:S(2)}) collective-permute-start(f32[144,128]{1,0:T(8,128)S(1)} %get-tuple-element.18), channel_id=1, source_target_pairs={{0,2},{2,0},{4,6},{6,4},{8,10},{10,8},{12,14},{14,12},{16,18},{18,... | collective-permute-start | bytes 221192 | tf_op jit(solution)/shard_map/ppermute | solution.py:412
  3.1 5.2 %collective-permute-start = (f32[184,128]{1,0:T(8,128)S(1)}, f32[184,128]{1,0:T(8,128)S(1)}, u32[]{:S(2)}, u32[]{:S(2)}) collective-permute-start(f32[184,128]{1,0:T(8,128)S(1)} %get-tuple-element.17), channel_id=1, source_target_pairs={{0,2},{2,0},{4,6},{6,4},{8,10},{10,8},{12,14},{14,12},{16,18},{18,... | collective-permute-start | bytes 282632 | tf_op jit(solution)/shard_map/ppermute | solution.py:412
  3.9 4.5 %collective-permute-start.4 = (f32[44,128]{1,0:T(8,128)S(1)}, f32[44,128]{1,0:T(8,128)S(1)}, u32[]{:S(2)}, u32[]{:S(2)}) collective-permute-start(f32[44,128]{1,0:T(8,128)S(1)} %slice_add_fusion), channel_id=1, source_target_pairs={{0,6},{2,8},{4,14},{6,0},{8,2},{10,12},{12,10},{14,4},{16,22},{18,... | collective-permute-start | bytes 67592 | tf_op jit(solution)/shard_map/ppermute | solution.py:412
  6.5 3.6 %collective-permute-start.7 = (f32[44,128]{1,0:T(8,128)S(1)}, f32[44,128]{1,0:T(8,128)S(1)}, u32[]{:S(2)}, u32[]{:S(2)}) collective-permute-start(f32[44,128]{1,0:T(8,128)S(1)} %add_rows.4), channel_id=1, source_target_pairs={{0,6},{2,8},{4,14},{6,0},{8,2},{10,12},{12,10},{14,4},{16,22},{18,... | collective-permute-start | bytes 67592 | tf_op jit(solution)/shard_map/ppermute | solution.py:412
  6.9 4.7 %collective-permute-start.2 = (f32[88,128]{1,0:T(8,128)S(1)}, f32[88,128]{1,0:T(8,128)S(1)}, u32[]{:S(2)}, u32[]{:S(2)}) collective-permute-start(f32[88,128]{1,0:T(8,128)S(1)} %add_rows.3), channel_id=1, source_target_pairs={{0,6},{2,8},{4,14},{6,0},{8,2},{10,12},{12,10},{14,4},{16,22},{18,... | collective-permute-start | bytes 135176 | tf_op jit(solution)/shard_map/ppermute | solution.py:412
  8.4 3.3 %collective-permute-start.5 = (f32[44,128]{1,0:T(8,128)S(1)}, f32[44,128]{1,0:T(8,128)S(1)}, u32[]{:S(2)}, u32[]{:S(2)}) collective-permute-start(f32[44,128]{1,0:T(8,128)S(1)} %fusion), channel_id=1, source_target_pairs={{0,10},{2,4},{4,2},{6,12},{8,14},{10,0},{12,6},{14,8},{16,26},{18,... | collective-permute-start | bytes 67592 | tf_op jit(solution)/shard_map/ppermute | solution.py:412
  10.1 4.2 %collective-permute-start.8 = (f32[44,128]{1,0:T(8,128)S(1)}, f32[44,128]{1,0:T(8,128)S(1)}, u32[]{:S(2)}, u32[]{:S(2)}) collective-permute-start(f32[44,128]{1,0:T(8,128)S(1)} %add_rows.5), channel_id=1, source_target_pairs={{0,10},{2,4},{4,2},{6,12},{8,14},{10,0},{12,6},{14,8},{16,26},{18,... | collective-permute-start | bytes 67592 | tf_op jit(solution)/shard_map/ppermute | solution.py:412
  11.7 4.2 %collective-permute-start.6 = (f32[44,128]{1,0:T(8,128)S(1)}, f32[44,128]{1,0:T(8,128)S(1)}, u32[]{:S(2)}, u32[]{:S(2)}) collective-permute-start(f32[44,128]{1,0:T(8,128)S(1)} %fusion.1), channel_id=1, source_target_pairs={{0,18},{2,16},{4,22},{6,20},{8,26},{10,24},{12,30},{14,28},{16,2},... | collective-permute-start | bytes 67592 | tf_op jit(solution)/shard_map/ppermute | solution.py:412

commit v12 on v11

--- a/solution.py
+++ b/solution.py
@@ -83,8 +83,6 @@
         copy.start()
         tile_copies.append(copy)
 
-    for ref in (keep_ref, third_ref, second_ref, first_ref):
-        ref[...] = jnp.zeros_like(ref)
     for copy in small:
         copy.wait()
     down = lax.broadcasted_iota(jnp.int32, (rows, rows), 0)

time: 17.1 us -> 17.6 us (1.029)
  Pallas kernels: 4.35 us -> 4.84 us
    pallas_call x1, Pallas kernels: 2.49 us -> 2.99 us  [project(): pl.pallas_call(kernel, out_shape=tuple(shapes), in_specs=[hbm] * 4, out_s...]
where the time goes in v12:
time: 17.6 us; the launch traced here: 17.4 us
  starting transfers between devices  11.4 us (65%)
  Pallas kernels  4.84 us (27%)
  waiting for transfers between devices  1.08 us (6%)
    ppermute x9, starting transfers between devices, give(): return lax.ppermute(value, 'view', pairs)  11.4 us
    pallas_call x1, Pallas kernels, project(): pl.pallas_call(kernel, out_shape=tuple(shapes), in_specs=[hbm] * 4, out_s...  2.99 us
    ppermute x9, waiting for transfers between devices, give(): return lax.ppermute(value, 'view', pairs)  1.08 us
    pallas_call x1, Pallas kernels, invert(): pl.pallas_call(invert_kernel, out_shape=jax.ShapeDtypeStruct((1, owned, s...  1.02 us
    pallas_call x1, Pallas kernels, prepare(): pl.pallas_call(kernel, out_shape=(pltpu.SMEM((1, samples // LANE), jnp.in...  0.82 us
  transfers between devices with their start and end apart: 9, of which 2 were waited for; matrix products, arithmetic and copies ran while one was open for 0% of the time, Pallas kernels for 5%

profile of v12, /device:TPU:0, one launch (start us, length us, event | category | flops | bytes accessed | tf_op | source)
XLA Modules:
  0.0 17.4 jit_solution(5146593186115404615)
XLA Ops:
  0.0 3.0 %project.1 = (f32[360,128]{1,0:T(8,128)S(1)}, f32[184,128]{1,0:T(8,128)S(1)}, f32[144,128]{1,0:T(8,128)S(1)}, f32[56,128]{1,0:T(8,128)S(1)}) custom-call(s32[2,128]{1,0:T(2,128)} %refs_0_.3, s32[2,128]{1,0:T(2,128)} %refs_1_.3, bf16[12,128,128]{2,1,0:T(8,128)(2,1)} %refs_2_.1, bf16[6,256,1024]{2,1,0:T(8,128)(2,1)} %refs_3_.1), custom_call_target="tpu_custom_call" | custom-call | flops 402653184 | bytes 3538944 | tf_op jit(solution)/shard_map/project/pallas_call | solution.py:189
  3.0 0.5 %collective-permute-start.3 = (f32[56,128]{1,0:T(8,128)S(1)}, f32[56,128]{1,0:T(8,128)S(1)}, u32[]{:S(2)}, u32[]{:S(2)}) collective-permute-start(f32[56,128]{1,0:T(8,128)S(1)} %get-tuple-element.19), channel_id=1, source_target_pairs={{0,2},{2,0},{4,6},{6,4},{8,10},{10,8},{12,14},{14,12},{16,18},{18,... | collective-permute-start | bytes 86024 | tf_op jit(solution)/shard_map/ppermute | solution.py:410
  3.5 0.1 collective-permute-start.1
  3.6 0.4 %collective-permute-start = (f32[184,128]{1,0:T(8,128)S(1)}, f32[184,128]{1,0:T(8,128)S(1)}, u32[]{:S(2)}, u32[]{:S(2)}) collective-permute-start(f32[184,128]{1,0:T(8,128)S(1)} %get-tuple-element.17), channel_id=1, source_target_pairs={{0,2},{2,0},{4,6},{6,4},{8,10},{10,8},{12,14},{14,12},{16,18},{18,... | collective-permute-start | bytes 282632 | tf_op jit(solution)/shard_map/ppermute | solution.py:410
  4.0 0.3 %collective-permute-done.3 = f32[56,128]{1,0:T(8,128)S(1)} collective-permute-done((f32[56,128]{1,0:T(8,128)S(1)}, f32[56,128]{1,0:T(8,128)S(1)}, u32[]{:S(2)}, u32[]{:S(2)}) %collective-permute-start.3) | collective-permute-done | bytes 28704 | tf_op jit(solution)/shard_map/ppermute | solution.py:410
  4.4 2.6 %collective-permute-start.4 = (f32[44,128]{1,0:T(8,128)S(1)}, f32[44,128]{1,0:T(8,128)S(1)}, u32[]{:S(2)}, u32[]{:S(2)}) collective-permute-start(f32[44,128]{1,0:T(8,128)S(1)} %slice_add_fusion), channel_id=1, source_target_pairs={{0,6},{2,8},{4,14},{6,0},{8,2},{10,12},{12,10},{14,4},{16,22},{18,... | collective-permute-start | bytes 67592 | tf_op jit(solution)/shard_map/ppermute | solution.py:410
  7.0 0.0 collective-permute-done.1.refs_1_
  7.0 0.4 %collective-permute-start.7 = (f32[44,128]{1,0:T(8,128)S(1)}, f32[44,128]{1,0:T(8,128)S(1)}, u32[]{:S(2)}, u32[]{:S(2)}) collective-permute-start(f32[44,128]{1,0:T(8,128)S(1)} %add_rows.4), channel_id=1, source_target_pairs={{0,6},{2,8},{4,14},{6,0},{8,2},{10,12},{12,10},{14,4},{16,22},{18,... | collective-permute-start | bytes 67592 | tf_op jit(solution)/shard_map/ppermute | solution.py:410
  7.4 1.4 %collective-permute-start.2 = (f32[88,128]{1,0:T(8,128)S(1)}, f32[88,128]{1,0:T(8,128)S(1)}, u32[]{:S(2)}, u32[]{:S(2)}) collective-permute-start(f32[88,128]{1,0:T(8,128)S(1)} %add_rows.3), channel_id=1, source_target_pairs={{0,6},{2,8},{4,14},{6,0},{8,2},{10,12},{12,10},{14,4},{16,22},{18,... | collective-permute-start | bytes 135176 | tf_op jit(solution)/shard_map/ppermute | solution.py:410
  8.8 0.0 collective-permute-done.4
  8.8 0.0 collective-permute-done.refs_1_.refs_3_
  8.8 1.8 %collective-permute-start.5 = (f32[44,128]{1,0:T(8,128)S(1)}, f32[44,128]{1,0:T(8,128)S(1)}, u32[]{:S(2)}, u32[]{:S(2)}) collective-permute-start(f32[44,128]{1,0:T(8,128)S(1)} %fusion), channel_id=1, source_target_pairs={{0,10},{2,4},{4,2},{6,12},{8,14},{10,0},{12,6},{14,8},{16,26},{18,... | collective-permute-start | bytes 67592 | tf_op jit(solution)/shard_map/ppermute | solution.py:410
  10.6 0.0 collective-permute-done.7.refs_2_
  10.6 1.5 %collective-permute-start.8 = (f32[44,128]{1,0:T(8,128)S(1)}, f32[44,128]{1,0:T(8,128)S(1)}, u32[]{:S(2)}, u32[]{:S(2)}) collective-permute-start(f32[44,128]{1,0:T(8,128)S(1)} %add_rows.5), channel_id=1, source_target_pairs={{0,10},{2,4},{4,2},{6,12},{8,14},{10,0},{12,6},{14,8},{16,26},{18,... | collective-permute-start | bytes 67592 | tf_op jit(solution)/shard_map/ppermute | solution.py:410
  12.2 0.0 collective-permute-done.5
  12.2 0.0 collective-permute-done.2.refs_4_
  12.2 2.7 %collective-permute-start.6 = (f32[44,128]{1,0:T(8,128)S(1)}, f32[44,128]{1,0:T(8,128)S(1)}, u32[]{:S(2)}, u32[]{:S(2)}) collective-permute-start(f32[44,128]{1,0:T(8,128)S(1)} %fusion.1), channel_id=1, source_target_pairs={{0,18},{2,16},{4,22},{6,20},{8,26},{10,24},{12,30},{14,28},{16,2},... | collective-permute-start | bytes 67592 | tf_op jit(solution)/shard_map/ppermute | solution.py:410
  14.9 0.0 collective-permute-done.8.refs_5_
  14.9 0.8 %prepare.1 = (s32[1,8]{1,0:T(1,128)S(4)}, s32[8,128]{1,0:T(8,128)S(1)}, f32[8,1024]{1,0:T(8,128)S(1)}, f32[8,1024]{1,0:T(8,128)S(1)}, f32[8,1024]{1,0:T(8,128)S(...) custom-call(s32[2,128]{1,0:T(2,128)} %refs_0_.3, s32[2,128]{1,0:T(2,128)} %refs_1_.3, ...), custom_call_target="tpu_custom_call" | custom-call | flops 4194304 | bytes 2097152 | tf_op jit(solution)/shard_map/prepare/pallas_call | solution.py:289
  15.7 0.7 %collective-permute-done.6.other_ref = f32[44,128]{1,0:T(8,128)S(1)} collective-permute-done((f32[44,128]{1,0:T(8,128)S(1)}, f32[44,128]{1,0:T(8,128)S(1)}, u32[]{:S(2)}, u32[]{:S(2)}) %collective-permute-start.6) | collective-permute-done | bytes 22560 | tf_op jit(solution)/shard_map/ppermute | solution.py:410
  16.4 1.0 %invert.1 = f32[1,8,1024]{2,1,0:T(8,128)} custom-call(f32[44,128]{1,0:T(8,128)S(1)} %collective-permute-done.6.other_ref, s32[1,8]{1,0:T(1,128)S(4)} %get-tuple-element.20.offset_ref, s32[8,128]{1,0:T(8,128)S(1)} %get-tuple-element.21.rank_ref, f32[8,1024]{1,0:T(8,128)S(1)} %get-tuple-element.22.kept_ref, f32[8,1024]{1,0:T(8,128)S(1)} %get-tuple-element.23.inner_ref, ...), custom_call_target="tpu_custom_call" | custom-call | tf_op jit(solution)/shard_map/invert/pallas_call | solution.py:356
  (6 shorter events, 0.0 us)
Async XLA Ops:
  3.0 1.4 %collective-permute-start.3 = (f32[56,128]{1,0:T(8,128)S(1)}, f32[56,128]{1,0:T(8,128)S(1)}, u32[]{:S(2)}, u32[]{:S(2)}) collective-permute-start(f32[56,128]{1,0:T(8,128)S(1)} %get-tuple-element.19), channel_id=1, source_target_pairs={{0,2},{2,0},{4,6},{6,4},{8,10},{10,8},{12,14},{14,12},{16,18},{18,... | collective-permute-start | bytes 86024 | tf_op jit(solution)/shard_map/ppermute | solution.py:410
  3.5 3.5 %collective-permute-start.1 = (f32[144,128]{1,0:T(8,128)S(1)}, f32[144,128]{1,0:T(8,128)S(1)}, u32[]{:S(2)}, u32[]{:S(2)}) collective-permute-start(f32[144,128]{1,0:T(8,128)S(1)} %get-tuple-element.18), channel_id=1, source_target_pairs={{0,2},{2,0},{4,6},{6,4},{8,10},{10,8},{12,14},{14,12},{16,18},{18,... | collective-permute-start | bytes 221192 | tf_op jit(solution)/shard_map/ppermute | solution.py:410
  3.6 5.2 %collective-permute-start = (f32[184,128]{1,0:T(8,128)S(1)}, f32[184,128]{1,0:T(8,128)S(1)}, u32[]{:S(2)}, u32[]{:S(2)}) collective-permute-start(f32[184,128]{1,0:T(8,128)S(1)} %get-tuple-element.17), channel_id=1, source_target_pairs={{0,2},{2,0},{4,6},{6,4},{8,10},{10,8},{12,14},{14,12},{16,18},{18,... | collective-permute-start | bytes 282632 | tf_op jit(solution)/shard_map/ppermute | solution.py:410
  4.4 4.5 %collective-permute-start.4 = (f32[44,128]{1,0:T(8,128)S(1)}, f32[44,128]{1,0:T(8,128)S(1)}, u32[]{:S(2)}, u32[]{:S(2)}) collective-permute-start(f32[44,128]{1,0:T(8,128)S(1)} %slice_add_fusion), channel_id=1, source_target_pairs={{0,6},{2,8},{4,14},{6,0},{8,2},{10,12},{12,10},{14,4},{16,22},{18,... | collective-permute-start | bytes 67592 | tf_op jit(solution)/shard_map/ppermute | solution.py:410
  7.0 3.6 %collective-permute-start.7 = (f32[44,128]{1,0:T(8,128)S(1)}, f32[44,128]{1,0:T(8,128)S(1)}, u32[]{:S(2)}, u32[]{:S(2)}) collective-permute-start(f32[44,128]{1,0:T(8,128)S(1)} %add_rows.4), channel_id=1, source_target_pairs={{0,6},{2,8},{4,14},{6,0},{8,2},{10,12},{12,10},{14,4},{16,22},{18,... | collective-permute-start | bytes 67592 | tf_op jit(solution)/shard_map/ppermute | solution.py:410
  7.4 4.7 %collective-permute-start.2 = (f32[88,128]{1,0:T(8,128)S(1)}, f32[88,128]{1,0:T(8,128)S(1)}, u32[]{:S(2)}, u32[]{:S(2)}) collective-permute-start(f32[88,128]{1,0:T(8,128)S(1)} %add_rows.3), channel_id=1, source_target_pairs={{0,6},{2,8},{4,14},{6,0},{8,2},{10,12},{12,10},{14,4},{16,22},{18,... | collective-permute-start | bytes 135176 | tf_op jit(solution)/shard_map/ppermute | solution.py:410
  8.8 3.3 %collective-permute-start.5 = (f32[44,128]{1,0:T(8,128)S(1)}, f32[44,128]{1,0:T(8,128)S(1)}, u32[]{:S(2)}, u32[]{:S(2)}) collective-permute-start(f32[44,128]{1,0:T(8,128)S(1)} %fusion), channel_id=1, source_target_pairs={{0,10},{2,4},{4,2},{6,12},{8,14},{10,0},{12,6},{14,8},{16,26},{18,... | collective-permute-start | bytes 67592 | tf_op jit(solution)/shard_map/ppermute | solution.py:410
  10.6 4.2 %collective-permute-start.8 = (f32[44,128]{1,0:T(8,128)S(1)}, f32[44,128]{1,0:T(8,128)S(1)}, u32[]{:S(2)}, u32[]{:S(2)}) collective-permute-start(f32[44,128]{1,0:T(8,128)S(1)} %add_rows.5), channel_id=1, source_target_pairs={{0,10},{2,4},{4,2},{6,12},{8,14},{10,0},{12,6},{14,8},{16,26},{18,... | collective-permute-start | bytes 67592 | tf_op jit(solution)/shard_map/ppermute | solution.py:410
  12.2 4.2 %collective-permute-start.6 = (f32[44,128]{1,0:T(8,128)S(1)}, f32[44,128]{1,0:T(8,128)S(1)}, u32[]{:S(2)}, u32[]{:S(2)}) collective-permute-start(f32[44,128]{1,0:T(8,128)S(1)} %fusion.1), channel_id=1, source_target_pairs={{0,18},{2,16},{4,22},{6,20},{8,26},{10,24},{12,30},{14,28},{16,2},... | collective-permute-start | bytes 67592 | tf_op jit(solution)/shard_map/ppermute | solution.py:410
